TPU v7x, 32 devices: a whole 2x2x4 slice. The times are simulated.
32 devices in a mesh: expert: 8 (over z, y), shard: 4 (over x, core).
Axes of the slice: x: 2, y: 2, z: 4, core: 2. Of those that a mesh axis runs over, the one named last changes fastest.
Arguments:
- tokens: bfloat16 [20480, 768], P(('expert', 'shard')), may hold values from -6 to 6
- gain_attn: bfloat16 [768], P('shard'), may hold values from 0.5 to 1.5
- w_query: bfloat16 [768, 768], P('shard'), may hold values from -0.21875 to 0.21875
- w_key: bfloat16 [768, 768], P('shard'), may hold values from -0.21875 to 0.21875
- w_value: bfloat16 [768, 768], P('shard'), may hold values from -0.21875 to 0.21875
- w_output: bfloat16 [768, 768], P('shard'), may hold values from -1.75 to 1.75
- rel_table: bfloat16 [12, 16], P('shard'), may hold values from -4 to 4
- gain_moe: bfloat16 [768], P('shard'), may hold values from 0.5 to 1.5
- router: bfloat16 [768, 8], P('shard'), may hold values from -0.15625 to 0.15625
- w_in: bfloat16 [8, 768, 3072], P('expert', 'shard'), may hold values from -0.21875 to 0.21875
- w_out: bfloat16 [8, 3072, 768], P('expert', 'shard'), may hold values from -0.15625 to 0.15625
- routes: int32 [20480, 2], P(('expert', 'shard')), may hold values from 0 to 7, all different within a row; in each aligned block of 640 rows (0 to 639, 640 to 1279, ...) at most 228 rows name the same one
- parents: int32 [8, 20], P('expert'), may hold values from -1 to 19, as said below
- cotangent: bfloat16 [20480, 768], P(('expert', 'shard')), may hold values from -6 to 6
Outputs:
- output: bfloat16 [20480, 768], P(('expert', 'shard'))
- grad_tokens: bfloat16 [20480, 768], P(('expert', 'shard'))
- grad_gain_attn: float32 [768], P('shard')
- grad_w_query: float32 [768, 768], P('shard')
- grad_w_key: float32 [768, 768], P('shard')
- grad_w_value: float32 [768, 768], P('shard')
- grad_w_output: float32 [768, 768], P('shard')
- grad_table: float32 [12, 16], P('shard')
- grad_gain_moe: float32 [768], P('shard')
- grad_router: float32 [768, 8], P('shard')
- grad_w_in: float32 [8, 768, 3072], P('expert', 'shard')
- grad_w_out: float32 [8, 3072, 768], P('expert', 'shard')
Inputs may be any that keep to these rules, and one draw needn't show every extreme that they name: `routes`: in each aligned block of 640 rows (the tokens of one device) no expert is named by more than 228 rows; the two ids of a row differ. `parents`: segments 0 to 7 form the trunk: segment 0 is the root (parent -1) and each trunk segment is the parent of the next. 4 other segments, the last segment always among them, have segment 8 - 1 as parent; each of them is the parent of 2 of the remaining segments.
All inputs are finite; a program needn't handle non-finite values.
Results may differ from a plain program's by a relative error of at most 0.018.
Values may be sent and summed in bfloat16 or wider, within the bound.
No kernel may reach another device: no remote copies, remote signals or barrier semaphores. Data moves between devices by JAX's collectives and lax.ppermute only.
A program may use at most 192 MiB of HBM per device.

v0:
```python
import jax
import jax.numpy as jnp
from jax import lax
from jax.sharding import PartitionSpec as P

H = 12
DH = 64
NB = 16
SEG = 128
SEGS = 20


THRESHOLDS = (1, 2, 3, 4, 5, 6, 7, 8, 12, 16, 24, 32, 48, 64, 96)
EPS = 1e-06
MASKED = -1e30


def tree_tables(parent_row):
    segment_ids = jnp.arange(SEGS, dtype=jnp.int32)
    parent_hot = parent_row[:, None] == segment_ids[None, :]
    identity = segment_ids[:, None] == segment_ids[None, :]
    ancestry = identity
    for hop_step in range(SEGS):
        ancestry = identity | jnp.any(parent_hot[:, :, None] & ancestry[None, :, :], axis=1)
    seg_depth = (jnp.sum(ancestry.astype(jnp.int32), axis=1) - 1) * SEG
    return (ancestry, seg_depth)


def pair_tables(ancestry, seg_depth, query_pos, key_pos):
    segment_ids = jnp.arange(SEGS, dtype=jnp.int32)
    query_seg = query_pos // SEG
    key_seg = key_pos // SEG
    query_hot = query_seg[:, None] == segment_ids[None, :]
    key_hot = key_seg[:, None] == segment_ids[None, :]
    query_depth = jnp.sum(jnp.where(query_hot, seg_depth[None, :], 0), axis=1) + query_pos % SEG
    key_depth = jnp.sum(jnp.where(key_hot, seg_depth[None, :], 0), axis=1) + key_pos % SEG
    path_keys = jnp.dot(ancestry.astype(jnp.float32), key_hot.astype(jnp.float32).T)
    linked = jnp.dot(query_hot.astype(jnp.float32), path_keys) > 0.5
    same_segment = query_seg[:, None] == key_seg[None, :]
    allowed = linked & (~same_segment | (key_pos[None, :] <= query_pos[:, None]))
    depth_gap = query_depth[:, None] - key_depth[None, :]
    bucket = jnp.zeros(depth_gap.shape, jnp.int32)
    for threshold in THRESHOLDS:
        bucket = bucket + (depth_gap >= threshold).astype(jnp.int32)
    return (allowed, bucket)


def head_bias(table_row, bucket):
    score_bias = jnp.zeros(bucket.shape, jnp.float32)
    for bucket_id in range(NB):
        score_bias = score_bias + jnp.where(bucket == bucket_id, table_row[bucket_id], 0.0)
    return score_bias


def head_scores(head_query, head_key, table_row, allowed, bucket):
    raw_scores = jnp.einsum(
        "qd,kd->qk", head_query, head_key, preferred_element_type=jnp.float32
    ) * DH ** (-0.5)
    raw_scores = raw_scores + head_bias(table_row, bucket)
    return jnp.where(allowed, raw_scores, MASKED)


def rms_forward(values, gain_row):
    factor = lax.rsqrt(jnp.mean(values * values, axis=-1, keepdims=True) + EPS)
    unit_rows = values * factor
    return (unit_rows * gain_row, unit_rows, factor)


def rms_backward(grad_out, gain_row, unit_rows, factor):
    scaled = grad_out * gain_row
    grad_in = factor * (scaled - unit_rows * jnp.mean(scaled * unit_rows, axis=-1, keepdims=True))
    return (grad_in, jnp.sum(grad_out * unit_rows, axis=0))


def split_heads(matrix):
    return matrix.reshape(matrix.shape[0], H, DH).transpose(1, 0, 2)


def join_heads(stacked):
    return stacked.transpose(1, 0, 2).reshape(stacked.shape[1], H * DH)


def per_device(
    tokens,
    gain_attn,
    w_query,
    w_key,
    w_value,
    w_output,
    rel_table,
    gain_moe,
    router,
    w_in,
    w_out,
    routes,
    parents,
    cotangent,
):
    gains_one, query_w, key_w, value_w, output_w, table_w, gains_two, router_w = (
        lax.all_gather(gain_attn, "shard", axis=0, tiled=True),
        lax.all_gather(w_query, "shard", axis=0, tiled=True),
        lax.all_gather(w_key, "shard", axis=0, tiled=True),
        lax.all_gather(w_value, "shard", axis=0, tiled=True),
        lax.all_gather(w_output, "shard", axis=0, tiled=True),
        lax.all_gather(rel_table, "shard", axis=0, tiled=True),
        lax.all_gather(gain_moe, "shard", axis=0, tiled=True),
        lax.all_gather(router, "shard", axis=0, tiled=True),
    )
    gain_first = gains_one.astype(jnp.float32)
    gain_second = gains_two.astype(jnp.float32)
    table_f32 = table_w.astype(jnp.float32)
    n_shard = lax.axis_size("shard")
    n_expert = lax.axis_size("expert")
    tok_count = tokens.shape[0]
    model_width = tokens.shape[1]
    tree_len = tok_count * n_shard
    n_experts = router_w.shape[1]
    local_experts = w_in.shape[0]
    capacity = max(2, tok_count * 20 // (7 * n_experts))
    token_f32 = tokens.astype(jnp.float32)
    normed_f32, unit_one, factor_one = rms_forward(token_f32, gain_first)
    normed_one = normed_f32.astype(jnp.bfloat16)
    queries = jnp.dot(normed_one, query_w, preferred_element_type=jnp.float32).astype(jnp.bfloat16)
    keys_local = jnp.dot(normed_one, key_w, preferred_element_type=jnp.float32).astype(jnp.bfloat16)
    values_local = jnp.dot(normed_one, value_w, preferred_element_type=jnp.float32).astype(
        jnp.bfloat16
    )
    keys_tree, values_tree = (
        lax.all_gather(keys_local, "shard", axis=0, tiled=True),
        lax.all_gather(values_local, "shard", axis=0, tiled=True),
    )
    ancestry, seg_depth = tree_tables(parents[0])
    first_pos = lax.axis_index("shard") * tok_count
    query_pos = first_pos + jnp.arange(tok_count, dtype=jnp.int32)
    key_pos = jnp.arange(tree_len, dtype=jnp.int32)
    allowed, bucket = pair_tables(ancestry, seg_depth, query_pos, key_pos)

    def head_forward(loop_state, head_items):
        head_query, head_key, head_value, table_row = head_items
        scores = head_scores(head_query, head_key, table_row, allowed, bucket)
        row_max = jnp.max(scores, axis=-1, keepdims=True)
        exp_scores = jnp.exp(scores - row_max)
        exp_total = jnp.sum(exp_scores, axis=-1, keepdims=True)
        attn_prob = (exp_scores / exp_total).astype(jnp.bfloat16)
        head_out = jnp.dot(attn_prob, head_value, preferred_element_type=jnp.float32)
        return (loop_state, (head_out, row_max + jnp.log(exp_total)))

    query_heads = split_heads(queries)
    key_heads = split_heads(keys_tree)
    value_heads = split_heads(values_tree)
    unused, (head_outs, log_totals) = lax.scan(
        head_forward, jnp.zeros((), jnp.float32), (query_heads, key_heads, value_heads, table_f32)
    )
    mixed_heads = join_heads(head_outs).astype(jnp.bfloat16)
    after_attn = token_f32 + jnp.dot(mixed_heads, output_w, preferred_element_type=jnp.float32)
    normed_two_f32, unit_two, factor_two = rms_forward(after_attn, gain_second)
    normed_two = normed_two_f32.astype(jnp.bfloat16)
    logits = jnp.dot(normed_two, router_w, preferred_element_type=jnp.float32)
    expert_range = jnp.arange(n_experts, dtype=jnp.int32)
    routes_hot = routes[:, :, None] == expert_range
    chosen = jnp.sum(jnp.where(routes_hot, logits[:, None, :], 0.0), axis=-1)
    gate_probs = jax.nn.softmax(chosen, axis=-1)
    flat_routes = routes.reshape(-1)
    expert_hot = (flat_routes[:, None] == expert_range[None, :]).astype(jnp.int32)
    earlier = jnp.cumsum(expert_hot, axis=0) - expert_hot
    places = flat_routes * capacity + jnp.sum(earlier * expert_hot, axis=-1)
    assignment = (
        jnp.zeros((n_experts * capacity,), jnp.int32)
        .at[places]
        .set(jnp.arange(2 * tok_count, dtype=jnp.int32))
    )
    occupied = jnp.zeros((n_experts * capacity,), jnp.bool_).at[places].set(True)

    def to_buffer(row_block):
        picked = row_block[assignment]
        filled = jnp.where(occupied[:, None], picked, jnp.zeros_like(picked))
        return filled.reshape(n_expert, local_experts, capacity, model_width)

    def from_buffer(buffer):
        return buffer.reshape(n_experts * capacity, model_width)[places].reshape(
            tok_count, 2, model_width
        )

    first_w, second_w = (
        lax.all_gather(w_in, "shard", axis=1, tiled=True),
        lax.all_gather(w_out, "shard", axis=1, tiled=True),
    )
    received = lax.all_to_all(
        to_buffer(jnp.repeat(normed_two, 2, axis=0)),
        "expert",
        split_axis=0,
        concat_axis=0,
        tiled=True,
    )
    inner_act = jnp.einsum("sxcd,xdf->sxcf", received, first_w, preferred_element_type=jnp.float32)
    activated = jax.nn.gelu(inner_act).astype(jnp.bfloat16)
    produced = jnp.einsum(
        "sxcf,xfd->sxcd", activated, second_w, preferred_element_type=jnp.float32
    ).astype(jnp.bfloat16)
    produced, inner_kept, received_rows = (produced, inner_act, received)
    returned = lax.all_to_all(produced, "expert", split_axis=0, concat_axis=0, tiled=True)
    expert_rows = from_buffer(returned).astype(jnp.float32)
    output_f32 = after_attn + jnp.sum(gate_probs[:, :, None] * expert_rows, axis=1)
    grad_out = cotangent.astype(jnp.float32)
    grad_gates = jnp.sum(grad_out[:, None, :] * expert_rows, axis=-1)
    grad_rows = (
        (gate_probs[:, :, None] * grad_out[:, None, :])
        .astype(jnp.bfloat16)
        .reshape(2 * tok_count, model_width)
    )
    grads_in = lax.all_to_all(
        to_buffer(grad_rows), "expert", split_axis=0, concat_axis=0, tiled=True
    )
    inner_act = inner_kept
    activated, gelu_pull = jax.vjp(jax.nn.gelu, inner_act)
    grad_second = jnp.einsum(
        "sxcf,sxcd->xfd",
        activated.astype(jnp.bfloat16),
        grads_in,
        preferred_element_type=jnp.float32,
    )
    grad_act = jnp.einsum("sxcd,xfd->sxcf", grads_in, second_w, preferred_element_type=jnp.float32)
    grad_inner = gelu_pull(grad_act)[0].astype(jnp.bfloat16)
    grad_first = jnp.einsum(
        "sxcd,sxcf->xdf", received_rows, grad_inner, preferred_element_type=jnp.float32
    )
    grad_received = jnp.einsum(
        "sxcf,xdf->sxcd", grad_inner, first_w, preferred_element_type=jnp.float32
    ).astype(jnp.bfloat16)
    grad_sent = lax.all_to_all(grad_received, "expert", split_axis=0, concat_axis=0, tiled=True)
    grad_from_experts = jnp.sum(from_buffer(grad_sent).astype(jnp.float32), axis=1)
    grad_w_first, grad_w_second = (
        lax.psum_scatter(
            grad_first.astype(jnp.bfloat16), "shard", scatter_dimension=1, tiled=True
        ).astype(jnp.float32),
        lax.psum_scatter(
            grad_second.astype(jnp.bfloat16), "shard", scatter_dimension=1, tiled=True
        ).astype(jnp.float32),
    )
    grad_chosen = gate_probs * (
        grad_gates - jnp.sum(gate_probs * grad_gates, axis=-1, keepdims=True)
    )
    grad_logits = jnp.sum(jnp.where(routes_hot, grad_chosen[:, :, None], 0.0), axis=1).astype(
        jnp.bfloat16
    )
    grad_router = jnp.einsum(
        "td,te->de", normed_two, grad_logits, preferred_element_type=jnp.float32
    )
    grad_normed_two = (
        jnp.einsum("te,de->td", grad_logits, router_w, preferred_element_type=jnp.float32)
        + grad_from_experts
    )
    grad_norm_two, grad_gain_two = rms_backward(grad_normed_two, gain_second, unit_two, factor_two)
    grad_after = grad_out + grad_norm_two
    grad_branch = grad_after.astype(jnp.bfloat16)
    grad_output_w = jnp.einsum(
        "td,te->de", mixed_heads, grad_branch, preferred_element_type=jnp.float32
    )
    grad_mixed = jnp.einsum(
        "te,de->td", grad_branch, output_w, preferred_element_type=jnp.float32
    ).astype(jnp.bfloat16)
    grad_heads = split_heads(grad_mixed)

    def score_grads(
        head_query, head_key, head_value, table_row, log_total, head_grad, mask_rows, bucket_rows
    ):
        scores = head_scores(head_query, head_key, table_row, mask_rows, bucket_rows)
        attn_prob = jnp.exp(scores - log_total)
        grad_prob = jnp.einsum(
            "qd,kd->qk", head_grad, head_value, preferred_element_type=jnp.float32
        )
        return (attn_prob, grad_prob)

    def head_backward(loop_state, head_items):
        head_query, head_key, head_value, table_row, log_total, head_grad = head_items
        attn_prob, grad_prob = score_grads(
            head_query, head_key, head_value, table_row, log_total, head_grad, allowed, bucket
        )
        row_dot = jnp.sum(grad_prob * attn_prob, axis=-1, keepdims=True)
        grad_score = (attn_prob * (grad_prob - row_dot)).astype(jnp.bfloat16)
        grad_query = jnp.einsum(
            "qk,kd->qd", grad_score, head_key, preferred_element_type=jnp.float32
        ) * DH ** (-0.5)
        grad_key = jnp.einsum(
            "qk,qd->kd", grad_score, head_query, preferred_element_type=jnp.float32
        ) * DH ** (-0.5)
        grad_value = jnp.einsum(
            "qk,qd->kd",
            attn_prob.astype(jnp.bfloat16),
            head_grad,
            preferred_element_type=jnp.float32,
        )
        score_f32 = grad_score.astype(jnp.float32)
        grad_row = jnp.stack(
            [jnp.sum(jnp.where(bucket == bucket_id, score_f32, 0.0)) for bucket_id in range(NB)]
        )
        return (loop_state, (grad_query, grad_key, grad_value, grad_row, row_dot))

    unused, (grad_queries, grad_keys, grad_values, grad_table, row_dots) = lax.scan(
        head_backward,
        jnp.zeros((), jnp.float32),
        (query_heads, key_heads, value_heads, table_f32, log_totals, grad_heads),
    )
    grad_key_local, grad_value_local = (
        lax.psum_scatter(
            join_heads(grad_keys).astype(jnp.bfloat16), "shard", scatter_dimension=0, tiled=True
        ).astype(jnp.float32),
        lax.psum_scatter(
            join_heads(grad_values).astype(jnp.bfloat16), "shard", scatter_dimension=0, tiled=True
        ).astype(jnp.float32),
    )
    grad_query_b = join_heads(grad_queries).astype(jnp.bfloat16)
    grad_key_b = grad_key_local.astype(jnp.bfloat16)
    grad_value_b = grad_value_local.astype(jnp.bfloat16)
    grad_query_w = jnp.einsum(
        "td,te->de", normed_one, grad_query_b, preferred_element_type=jnp.float32
    )
    grad_key_w = jnp.einsum("td,te->de", normed_one, grad_key_b, preferred_element_type=jnp.float32)
    grad_value_w = jnp.einsum(
        "td,te->de", normed_one, grad_value_b, preferred_element_type=jnp.float32
    )
    grad_normed_one = jnp.einsum(
        "te,de->td", grad_query_b, query_w, preferred_element_type=jnp.float32
    )
    grad_normed_one = grad_normed_one + jnp.einsum(
        "te,de->td", grad_key_b, key_w, preferred_element_type=jnp.float32
    )
    grad_normed_one = grad_normed_one + jnp.einsum(
        "te,de->td", grad_value_b, value_w, preferred_element_type=jnp.float32
    )
    grad_norm_one, grad_gain_one = rms_backward(grad_normed_one, gain_first, unit_one, factor_one)
    grad_tokens = (grad_after + grad_norm_one).astype(jnp.bfloat16)
    total_g1, total_q, total_k, total_v, total_o, total_t, total_g2, total_r = lax.psum(
        (
            grad_gain_one,
            grad_query_w,
            grad_key_w,
            grad_value_w,
            grad_output_w,
            grad_table,
            grad_gain_two,
            grad_router,
        ),
        "expert",
    )
    final_g1, final_q, final_k, final_v, final_o, final_t, final_g2, final_r = (
        lax.psum_scatter(
            total_g1.astype(jnp.bfloat16), "shard", scatter_dimension=0, tiled=True
        ).astype(jnp.float32),
        lax.psum_scatter(
            total_q.astype(jnp.bfloat16), "shard", scatter_dimension=0, tiled=True
        ).astype(jnp.float32),
        lax.psum_scatter(
            total_k.astype(jnp.bfloat16), "shard", scatter_dimension=0, tiled=True
        ).astype(jnp.float32),
        lax.psum_scatter(
            total_v.astype(jnp.bfloat16), "shard", scatter_dimension=0, tiled=True
        ).astype(jnp.float32),
        lax.psum_scatter(
            total_o.astype(jnp.bfloat16), "shard", scatter_dimension=0, tiled=True
        ).astype(jnp.float32),
        lax.psum_scatter(
            total_t.astype(jnp.bfloat16), "shard", scatter_dimension=0, tiled=True
        ).astype(jnp.float32),
        lax.psum_scatter(
            total_g2.astype(jnp.bfloat16), "shard", scatter_dimension=0, tiled=True
        ).astype(jnp.float32),
        lax.psum_scatter(
            total_r.astype(jnp.bfloat16), "shard", scatter_dimension=0, tiled=True
        ).astype(jnp.float32),
    )
    return (
        output_f32.astype(jnp.bfloat16),
        grad_tokens,
        final_g1,
        final_q,
        final_k,
        final_v,
        final_o,
        final_t,
        final_g2,
        final_r,
        grad_w_first,
        grad_w_second,
    )


def solution(mesh):
    return jax.shard_map(
        per_device,
        mesh=mesh,
        in_specs=(
            P(("expert", "shard"), None),
            P("shard"),
            P("shard", None),
            P("shard", None),
            P("shard", None),
            P("shard", None),
            P("shard", None),
            P("shard"),
            P("shard", None),
            P("expert", "shard", None),
            P("expert", "shard", None),
            P(("expert", "shard"), None),
            P("expert", None),
            P(("expert", "shard"), None),
        ),
        out_specs=(
            P(("expert", "shard"), None),
            P(("expert", "shard"), None),
            P("shard"),
            P("shard", None),
            P("shard", None),
            P("shard", None),
            P("shard", None),
            P("shard", None),
            P("shard"),
            P("shard", None),
            P("expert", "shard", None),
            P("expert", "shard", None),
        ),
        check_vma=False,
    )
```

profile of v0, /device:TPU:0, one launch (start us, length us, event | category | flops | bytes accessed | tf_op | source)
XLA Modules:
  0.0 2491.0 jit_solution(7202189758424639726)
XLA Ops:
  152.6 459.4 %while.30 = (s32[]{:T(128)}, bf16[12,640,64]{1,2,0:T(8,128)(2,1)S(1)}, f32[12,640,1]{1,2,0:T(1,128)}, bf16[12,640,64]{2,1,0:T(8,128)(2,1)}, bf16[12,2560,64]{2,1...) while((s32[]{:T(128)}, ...), condition=%wide.region_27.28_spmd.clone, body=%wide.region_24.27_spmd.clone.sunk | while | flops 584908160 | bytes 22989692 | solution.py:151
  153.3 33.4 %fusion.254 = (f32[640]{0:T(1024)S(1)}, f32[640,2560]{1,0:T(8,128)S(1)}) fusion(pred[640,2560]{1,0:T(32,128)(4,1)} %get-tuple-element.702, f32[]{:T(128)} %bitcast.370, f32[]{:T(128)} %bitcast.371, f32[]{:T(128)} %bitcast.372, f32[]{:T(128)} %bitcast.373, f32[]{:T(128)} %bitcast.374, f32[]{:T(128)} %bitcast.375, f32[]{:T(128)} %bitcast.376, ...), kind=kOutput, calls=%fused_computation.342.clone.1 | convolution fusion | flops 367000960 | bytes 9035776 | tf_op jit(solution)/shard_map/while/body/eval_jaxpr/qd,kd->qk/dot_general | solution.py:56
  191.7 33.3 %fusion.254 = (f32[640]{0:T(1024)S(1)}, f32[640,2560]{1,0:T(8,128)S(1)}) fusion(pred[640,2560]{1,0:T(32,128)(4,1)} %get-tuple-element.702, f32[]{:T(128)} %bitcast.370, f32[]{:T(128)} %bitcast.371, f32[]{:T(128)} %bitcast.372, f32[]{:T(128)} %bitcast.373, f32[]{:T(128)} %bitcast.374, f32[]{:T(128)} %bitcast.375, f32[]{:T(128)} %bitcast.376, ...), kind=kOutput, calls=%fused_computation.342.clone.1 | convolution fusion | flops 367000960 | bytes 9035776 | tf_op jit(solution)/shard_map/while/body/eval_jaxpr/qd,kd->qk/dot_general | solution.py:56
  229.9 33.3 %fusion.254 = (f32[640]{0:T(1024)S(1)}, f32[640,2560]{1,0:T(8,128)S(1)}) fusion(pred[640,2560]{1,0:T(32,128)(4,1)} %get-tuple-element.702, f32[]{:T(128)} %bitcast.370, f32[]{:T(128)} %bitcast.371, f32[]{:T(128)} %bitcast.372, f32[]{:T(128)} %bitcast.373, f32[]{:T(128)} %bitcast.374, f32[]{:T(128)} %bitcast.375, f32[]{:T(128)} %bitcast.376, ...), kind=kOutput, calls=%fused_computation.342.clone.1 | convolution fusion | flops 367000960 | bytes 9035776 | tf_op jit(solution)/shard_map/while/body/eval_jaxpr/qd,kd->qk/dot_general | solution.py:56
  268.1 33.3 %fusion.254 = (f32[640]{0:T(1024)S(1)}, f32[640,2560]{1,0:T(8,128)S(1)}) fusion(pred[640,2560]{1,0:T(32,128)(4,1)} %get-tuple-element.702, f32[]{:T(128)} %bitcast.370, f32[]{:T(128)} %bitcast.371, f32[]{:T(128)} %bitcast.372, f32[]{:T(128)} %bitcast.373, f32[]{:T(128)} %bitcast.374, f32[]{:T(128)} %bitcast.375, f32[]{:T(128)} %bitcast.376, ...), kind=kOutput, calls=%fused_computation.342.clone.1 | convolution fusion | flops 367000960 | bytes 9035776 | tf_op jit(solution)/shard_map/while/body/eval_jaxpr/qd,kd->qk/dot_general | solution.py:56
  306.4 33.3 %fusion.254 = (f32[640]{0:T(1024)S(1)}, f32[640,2560]{1,0:T(8,128)S(1)}) fusion(pred[640,2560]{1,0:T(32,128)(4,1)} %get-tuple-element.702, f32[]{:T(128)} %bitcast.370, f32[]{:T(128)} %bitcast.371, f32[]{:T(128)} %bitcast.372, f32[]{:T(128)} %bitcast.373, f32[]{:T(128)} %bitcast.374, f32[]{:T(128)} %bitcast.375, f32[]{:T(128)} %bitcast.376, ...), kind=kOutput, calls=%fused_computation.342.clone.1 | convolution fusion | flops 367000960 | bytes 9035776 | tf_op jit(solution)/shard_map/while/body/eval_jaxpr/qd,kd->qk/dot_general | solution.py:56
  344.6 33.3 %fusion.254 = (f32[640]{0:T(1024)S(1)}, f32[640,2560]{1,0:T(8,128)S(1)}) fusion(pred[640,2560]{1,0:T(32,128)(4,1)} %get-tuple-element.702, f32[]{:T(128)} %bitcast.370, f32[]{:T(128)} %bitcast.371, f32[]{:T(128)} %bitcast.372, f32[]{:T(128)} %bitcast.373, f32[]{:T(128)} %bitcast.374, f32[]{:T(128)} %bitcast.375, f32[]{:T(128)} %bitcast.376, ...), kind=kOutput, calls=%fused_computation.342.clone.1 | convolution fusion | flops 367000960 | bytes 9035776 | tf_op jit(solution)/shard_map/while/body/eval_jaxpr/qd,kd->qk/dot_general | solution.py:56
  382.9 33.3 %fusion.254 = (f32[640]{0:T(1024)S(1)}, f32[640,2560]{1,0:T(8,128)S(1)}) fusion(pred[640,2560]{1,0:T(32,128)(4,1)} %get-tuple-element.702, f32[]{:T(128)} %bitcast.370, f32[]{:T(128)} %bitcast.371, f32[]{:T(128)} %bitcast.372, f32[]{:T(128)} %bitcast.373, f32[]{:T(128)} %bitcast.374, f32[]{:T(128)} %bitcast.375, f32[]{:T(128)} %bitcast.376, ...), kind=kOutput, calls=%fused_computation.342.clone.1 | convolution fusion | flops 367000960 | bytes 9035776 | tf_op jit(solution)/shard_map/while/body/eval_jaxpr/qd,kd->qk/dot_general | solution.py:56
  421.1 33.3 %fusion.254 = (f32[640]{0:T(1024)S(1)}, f32[640,2560]{1,0:T(8,128)S(1)}) fusion(pred[640,2560]{1,0:T(32,128)(4,1)} %get-tuple-element.702, f32[]{:T(128)} %bitcast.370, f32[]{:T(128)} %bitcast.371, f32[]{:T(128)} %bitcast.372, f32[]{:T(128)} %bitcast.373, f32[]{:T(128)} %bitcast.374, f32[]{:T(128)} %bitcast.375, f32[]{:T(128)} %bitcast.376, ...), kind=kOutput, calls=%fused_computation.342.clone.1 | convolution fusion | flops 367000960 | bytes 9035776 | tf_op jit(solution)/shard_map/while/body/eval_jaxpr/qd,kd->qk/dot_general | solution.py:56
  459.3 33.3 %fusion.254 = (f32[640]{0:T(1024)S(1)}, f32[640,2560]{1,0:T(8,128)S(1)}) fusion(pred[640,2560]{1,0:T(32,128)(4,1)} %get-tuple-element.702, f32[]{:T(128)} %bitcast.370, f32[]{:T(128)} %bitcast.371, f32[]{:T(128)} %bitcast.372, f32[]{:T(128)} %bitcast.373, f32[]{:T(128)} %bitcast.374, f32[]{:T(128)} %bitcast.375, f32[]{:T(128)} %bitcast.376, ...), kind=kOutput, calls=%fused_computation.342.clone.1 | convolution fusion | flops 367000960 | bytes 9035776 | tf_op jit(solution)/shard_map/while/body/eval_jaxpr/qd,kd->qk/dot_general | solution.py:56
  497.6 33.3 %fusion.254 = (f32[640]{0:T(1024)S(1)}, f32[640,2560]{1,0:T(8,128)S(1)}) fusion(pred[640,2560]{1,0:T(32,128)(4,1)} %get-tuple-element.702, f32[]{:T(128)} %bitcast.370, f32[]{:T(128)} %bitcast.371, f32[]{:T(128)} %bitcast.372, f32[]{:T(128)} %bitcast.373, f32[]{:T(128)} %bitcast.374, f32[]{:T(128)} %bitcast.375, f32[]{:T(128)} %bitcast.376, ...), kind=kOutput, calls=%fused_computation.342.clone.1 | convolution fusion | flops 367000960 | bytes 9035776 | tf_op jit(solution)/shard_map/while/body/eval_jaxpr/qd,kd->qk/dot_general | solution.py:56
  535.8 33.3 %fusion.254 = (f32[640]{0:T(1024)S(1)}, f32[640,2560]{1,0:T(8,128)S(1)}) fusion(pred[640,2560]{1,0:T(32,128)(4,1)} %get-tuple-element.702, f32[]{:T(128)} %bitcast.370, f32[]{:T(128)} %bitcast.371, f32[]{:T(128)} %bitcast.372, f32[]{:T(128)} %bitcast.373, f32[]{:T(128)} %bitcast.374, f32[]{:T(128)} %bitcast.375, f32[]{:T(128)} %bitcast.376, ...), kind=kOutput, calls=%fused_computation.342.clone.1 | convolution fusion | flops 367000960 | bytes 9035776 | tf_op jit(solution)/shard_map/while/body/eval_jaxpr/qd,kd->qk/dot_general | solution.py:56
  574.1 33.3 %fusion.254 = (f32[640]{0:T(1024)S(1)}, f32[640,2560]{1,0:T(8,128)S(1)}) fusion(pred[640,2560]{1,0:T(32,128)(4,1)} %get-tuple-element.702, f32[]{:T(128)} %bitcast.370, f32[]{:T(128)} %bitcast.371, f32[]{:T(128)} %bitcast.372, f32[]{:T(128)} %bitcast.373, f32[]{:T(128)} %bitcast.374, f32[]{:T(128)} %bitcast.375, f32[]{:T(128)} %bitcast.376, ...), kind=kOutput, calls=%fused_computation.342.clone.1 | convolution fusion | flops 367000960 | bytes 9035776 | tf_op jit(solution)/shard_map/while/body/eval_jaxpr/qd,kd->qk/dot_general | solution.py:56
  659.4 64.1 %all-to-all-done = bf16[8,1,228,768]{3,2,1,0:T(8,128)(2,1)S(1)} async-done(((bf16[8,1,228,768]{3,2,1,0:T(8,128)(2,1)}), bf16[8,1,228,768]{3,2,1,0:T(8,128)(2,1)S(1)}, u32[]{:S(2)}, u32[]{:S(2)}) %all-to-all-start) | async-done | bytes 2801696 | tf_op jit(solution)/shard_map/all_to_all | solution.py:188
  891.2 37.6 %all-to-all-done.3 = bf16[8,1,228,768]{3,2,1,0:T(8,128)(2,1)} async-done(((bf16[8,1,228,768]{3,2,1,0:T(8,128)(2,1)}), bf16[8,1,228,768]{3,2,1,0:T(8,128)(2,1)}, u32[]{:S(2)}, u32[]{:S(2)}) %all-to-all-start.3) | async-done | bytes 2801696 | tf_op jit(solution)/shard_map/all_to_all | solution.py:230
  959.5 921.7 %while.31 = (s32[]{:T(128)}, bf16[12,640,64]{1,2,0:T(8,128)(2,1)}, bf16[12,2560,64]{1,2,0:T(8,128)(2,1)}, bf16[12,2560,64]{1,2,0:T(8,128)(2,1)}, f32[12,16]{1,0:...) while((s32[]{:T(128)}, bf16[12,640,64]{1,2,0:T(8,128)(2,1)}, ...), condition=%wide.region_61.62_spmd.clone, body=%wide.region_43.61_spmd.clone.sunk | while | flops 1369906560 | bytes 54775016 | solution.py:299
  961.7 33.1 %subtract_exponential_fusion.4 = f32[640,2560]{1,0:T(8,128)S(1)} fusion(pred[640,2560]{1,0:T(32,128)(4,1)} %get-tuple-element.747, s32[2560]{0:T(1024)S(1)} %get-tuple-element.751, s32[640]{0:T(1024)S(1)} %get-tuple-element.752, f32[640]{0:T(1024)S(1)} %dynamic-slice_reduce_fusion.2, f32[]{:T(128)} %bitcast.398, f32[]{:T(128)} %bitcast.399, ...), kind=kOutput, calls=%fused_computation.92.clone.1 | convolution fusion | flops 367001600 | bytes 9035776 | tf_op jit(solution)/shard_map/while/body/eval_jaxpr/qd,kd->qk/dot_general | solution.py:56
  1038.5 33.1 %subtract_exponential_fusion.4 = f32[640,2560]{1,0:T(8,128)S(1)} fusion(pred[640,2560]{1,0:T(32,128)(4,1)} %get-tuple-element.747, s32[2560]{0:T(1024)S(1)} %get-tuple-element.751, s32[640]{0:T(1024)S(1)} %get-tuple-element.752, f32[640]{0:T(1024)S(1)} %dynamic-slice_reduce_fusion.2, f32[]{:T(128)} %bitcast.398, f32[]{:T(128)} %bitcast.399, ...), kind=kOutput, calls=%fused_computation.92.clone.1 | convolution fusion | flops 367001600 | bytes 9035776 | tf_op jit(solution)/shard_map/while/body/eval_jaxpr/qd,kd->qk/dot_general | solution.py:56
  1268.8 33.1 %subtract_exponential_fusion.4 = f32[640,2560]{1,0:T(8,128)S(1)} fusion(pred[640,2560]{1,0:T(32,128)(4,1)} %get-tuple-element.747, s32[2560]{0:T(1024)S(1)} %get-tuple-element.751, s32[640]{0:T(1024)S(1)} %get-tuple-element.752, f32[640]{0:T(1024)S(1)} %dynamic-slice_reduce_fusion.2, f32[]{:T(128)} %bitcast.398, f32[]{:T(128)} %bitcast.399, ...), kind=kOutput, calls=%fused_computation.92.clone.1 | convolution fusion | flops 367001600 | bytes 9035776 | tf_op jit(solution)/shard_map/while/body/eval_jaxpr/qd,kd->qk/dot_general | solution.py:56
  1345.6 33.1 %subtract_exponential_fusion.4 = f32[640,2560]{1,0:T(8,128)S(1)} fusion(pred[640,2560]{1,0:T(32,128)(4,1)} %get-tuple-element.747, s32[2560]{0:T(1024)S(1)} %get-tuple-element.751, s32[640]{0:T(1024)S(1)} %get-tuple-element.752, f32[640]{0:T(1024)S(1)} %dynamic-slice_reduce_fusion.2, f32[]{:T(128)} %bitcast.398, f32[]{:T(128)} %bitcast.399, ...), kind=kOutput, calls=%fused_computation.92.clone.1 | convolution fusion | flops 367001600 | bytes 9035776 | tf_op jit(solution)/shard_map/while/body/eval_jaxpr/qd,kd->qk/dot_general | solution.py:56
  1499.2 33.1 %subtract_exponential_fusion.4 = f32[640,2560]{1,0:T(8,128)S(1)} fusion(pred[640,2560]{1,0:T(32,128)(4,1)} %get-tuple-element.747, s32[2560]{0:T(1024)S(1)} %get-tuple-element.751, s32[640]{0:T(1024)S(1)} %get-tuple-element.752, f32[640]{0:T(1024)S(1)} %dynamic-slice_reduce_fusion.2, f32[]{:T(128)} %bitcast.398, f32[]{:T(128)} %bitcast.399, ...), kind=kOutput, calls=%fused_computation.92.clone.1 | convolution fusion | flops 367001600 | bytes 9035776 | tf_op jit(solution)/shard_map/while/body/eval_jaxpr/qd,kd->qk/dot_general | solution.py:56
  1652.8 33.1 %subtract_exponential_fusion.4 = f32[640,2560]{1,0:T(8,128)S(1)} fusion(pred[640,2560]{1,0:T(32,128)(4,1)} %get-tuple-element.747, s32[2560]{0:T(1024)S(1)} %get-tuple-element.751, s32[640]{0:T(1024)S(1)} %get-tuple-element.752, f32[640]{0:T(1024)S(1)} %dynamic-slice_reduce_fusion.2, f32[]{:T(128)} %bitcast.398, f32[]{:T(128)} %bitcast.399, ...), kind=kOutput, calls=%fused_computation.92.clone.1 | convolution fusion | flops 367001600 | bytes 9035776 | tf_op jit(solution)/shard_map/while/body/eval_jaxpr/qd,kd->qk/dot_general | solution.py:56
  1729.6 33.1 %subtract_exponential_fusion.4 = f32[640,2560]{1,0:T(8,128)S(1)} fusion(pred[640,2560]{1,0:T(32,128)(4,1)} %get-tuple-element.747, s32[2560]{0:T(1024)S(1)} %get-tuple-element.751, s32[640]{0:T(1024)S(1)} %get-tuple-element.752, f32[640]{0:T(1024)S(1)} %dynamic-slice_reduce_fusion.2, f32[]{:T(128)} %bitcast.398, f32[]{:T(128)} %bitcast.399, ...), kind=kOutput, calls=%fused_computation.92.clone.1 | convolution fusion | flops 367001600 | bytes 9035776 | tf_op jit(solution)/shard_map/while/body/eval_jaxpr/qd,kd->qk/dot_general | solution.py:56
  1982.2 368.7 %all-reduce.9 = (bf16[768]{0:T(1024)(128)(2,1)S(1)}, bf16[768,768]{1,0:T(8,128)(2,1)}, bf16[768,768]{1,0:T(8,128)(2,1)}, bf16[768,768]{1,0:T(8,128)(2,1)}, bf16[...) all-reduce(f32[768]{0:T(1024)S(1)} %get-tuple-element.308, ...), channel_id=1, replica_groups=mesh['expert'=8,'shard'=4] {'expert'}, use_global_device_ids=true, to_apply=%region_66.67 | all-reduce | flops 2367168 | bytes 14203008 | tf_op jit(solution)/shard_map/psum | solution.py:333
  (525 shorter events, 1370.4 us)
Async XLA Ops:
  7.2 22.6 all-gather.13.cloned.1.call-start
  7.9 40.9 %all-gather.17.cloned.1.call-start = ((), (), s32[]{:S(2)}) async-start(), calls=%async_computation.16 | async-start | bytes 1474560 | tf_op jit(solution)/shard_map/all_gather | solution.py:103
  8.7 95.0 %all-gather.11.cloned.1.call-start = ((), (), s32[]{:S(2)}) async-start(), calls=%async_computation.13 | async-start | bytes 1474560 | tf_op jit(solution)/shard_map/all_gather | solution.py:101
  9.4 98.9 %all-gather.15.cloned.1.call-start = ((), (), s32[]{:S(2)}) async-start(), calls=%async_computation.15 | async-start | bytes 4915200 | tf_op jit(solution)/shard_map/all_gather | solution.py:129
  21.5 82.2 %copy-start.34 = (f32[768]{0:T(1024)}, f32[768]{0:T(1024)S(1)}, u32[]{:S(2)}) copy-start(f32[768]{0:T(1024)S(1)} %convert_element_type.273) | copy-start | bytes 9220
  23.0 80.7 %copy-start.36 = (f32[640]{0:T(1024)}, f32[640]{0:T(1024)S(1)}, u32[]{:S(2)}) copy-start(f32[640]{0:T(1024)S(1)} %add_rsqrt_fusion.1) | copy-start | bytes 7684
  33.3 104.6 %all-gather.19.cloned.1.call-start = ((), (), s32[]{:S(2)}) async-start(), calls=%async_computation.17 | async-start | bytes 4915200 | tf_op jit(solution)/shard_map/all_gather | solution.py:130
  52.1 560.1 %all-gather.21.cloned.1.call-start = ((), (), s32[]{:S(2)}) async-start(), calls=%async_computation.18 | async-start | bytes 1474560 | tf_op jit(solution)/shard_map/all_gather | solution.py:104
  52.6 675.4 %all-gather.23.cloned.1.call-start = ((), (), s32[]{:S(2)}) async-start(), calls=%async_computation.19 | async-start | bytes 5898240 | tf_op jit(solution)/shard_map/all_gather | solution.py:185
  152.6 460.1 %copy-start.9 = (bf16[640,768]{1,0:T(8,128)(2,1)S(1)}, bf16[640,768]{1,0:T(8,128)(2,1)}, u32[]{:S(2)}) copy-start(bf16[640,768]{1,0:T(8,128)(2,1)} %param.18) | copy-start | bytes 2949124
  653.3 70.2 %all-to-all-start = ((bf16[8,1,228,768]{3,2,1,0:T(8,128)(2,1)}), bf16[8,1,228,768]{3,2,1,0:T(8,128)(2,1)S(1)}, u32[]{:S(2)}, u32[]{:S(2)}) async-start(bf16[8,1,228,768]{3,2,1,0:T(8,128)(2,1)} %get-tuple-element.411), calls=%async_computation | async-start | bytes 5701632 | tf_op jit(solution)/shard_map/all_to_all | solution.py:188
  658.6 84.0 %all-gather.25.cloned.1.call-start = ((), (), s32[]{:S(2)}) async-start(), calls=%async_computation.20 | async-start | bytes 5898240 | tf_op jit(solution)/shard_map/all_gather | solution.py:186
  723.4 68.6 %all-to-all-start.2 = ((bf16[8,1,228,768]{3,2,1,0:T(8,128)(2,1)}), bf16[8,1,228,768]{3,2,1,0:T(8,128)(2,1)}, u32[]{:S(2)}, u32[]{:S(2)}) async-start(bf16[8,1,228,768]{3,2,1,0:T(8,128)(2,1)} %get-tuple-element.410), calls=%async_computation.2 | async-start | bytes 5701632 | tf_op jit(solution)/shard_map/all_to_all | solution.py:211
  792.0 68.4 %all-to-all-start.1 = ((bf16[8,1,228,768]{3,2,1,0:T(8,128)(2,1)}), bf16[8,1,228,768]{3,2,1,0:T(8,128)(2,1)S(1)}, u32[]{:S(2)}, u32[]{:S(2)}) async-start(bf16[8,1,228,768]{3,2,1,0:T(8,128)(2,1)} %convert_bitcast_fusion.1), calls=%async_computation.1 | async-start | bytes 5701632 | tf_op jit(solution)/shard_map/all_to_all | solution.py:201
  860.4 68.3 %all-to-all-start.3 = ((bf16[8,1,228,768]{3,2,1,0:T(8,128)(2,1)}), bf16[8,1,228,768]{3,2,1,0:T(8,128)(2,1)}, u32[]{:S(2)}, u32[]{:S(2)}) async-start(bf16[8,1,228,768]{3,2,1,0:T(8,128)(2,1)} %convert_bitcast_fusion), calls=%async_computation.3 | async-start | bytes 5701632 | tf_op jit(solution)/shard_map/all_to_all | solution.py:230
  864.8 1076.5 %reduce-scatter.28.cloned.1.call-start = ((), (), s32[]{:S(2)}) async-start(), calls=%async_computation.27 | async-start | bytes 4915200
  1887.5 86.6 %reduce-scatter.30.cloned.1.call-start = ((), (), s32[]{:S(2)}) async-start(), calls=%async_computation.28 | async-start | bytes 4915200
  1893.9 461.5 %reduce-scatter.26.cloned.1.call-start = ((), (), s32[]{:S(2)}) async-start(), calls=%async_computation.26 | async-start | bytes 5898240 | tf_op jit(solution)/shard_map/reduce_scatter | solution.py:236
  1914.9 443.4 %reduce-scatter.24.cloned.1.call-start = ((), (), s32[]{:S(2)}) async-start(), calls=%async_computation.25 | async-start | bytes 5898240 | tf_op jit(solution)/shard_map/reduce_scatter | solution.py:233
  1930.2 442.0 %reduce-scatter.32.cloned.1.call-start = ((), (), s32[]{:S(2)}) async-start(), calls=%async_computation.29 | async-start | bytes 245760
  2351.7 45.6 %reduce-scatter.22.cloned.1.call-start = ((), (), s32[]{:S(2)}) async-start(), calls=%async_computation.24 | async-start | bytes 1474560 | tf_op jit(solution)/shard_map/reduce_scatter | solution.py:359
  2352.3 73.3 %reduce-scatter.20.cloned.1.call-start = ((), (), s32[]{:S(2)}) async-start(), calls=%async_computation.23 | async-start | bytes 1474560 | tf_op jit(solution)/shard_map/reduce_scatter | solution.py:356
  2352.9 100.9 %reduce-scatter.18.cloned.1.call-start = ((), (), s32[]{:S(2)}) async-start(), calls=%async_computation.22 | async-start | bytes 1474560 | tf_op jit(solution)/shard_map/reduce_scatter | solution.py:353
  2353.5 128.7 %reduce-scatter.16.cloned.1.call-start = ((), (), s32[]{:S(2)}) async-start(), calls=%async_computation.21 | async-start | bytes 1474560 | tf_op jit(solution)/shard_map/reduce_scatter | solution.py:350
  (48 other events, 614.5 us)
Sparse Core Ops, SparseCore 0:
  9.6 20.1 all-gather.12
  31.3 17.4 all-gather.16
  50.4 17.4 all-gather.10
  69.9 32.9 all-gather.14
  104.9 32.9 all-gather.18
  139.3 17.4 all-gather.20
  158.4 37.4 all-gather.22
  661.0 37.9 all-gather.24
  1887.6 41.0 reduce-scatter.27
  1931.2 42.8 reduce-scatter.29
  1976.7 47.8 reduce-scatter.25
  2027.1 47.8 reduce-scatter.23
  2351.9 17.2 reduce-scatter.31
  2371.5 25.7 reduce-scatter.21
  2399.9 25.6 reduce-scatter.19
  2428.1 25.7 reduce-scatter.17
  2456.4 25.7 reduce-scatter.15
where the time goes:
time: 2510 us; the launch traced here: 2490 us
  matrix products  1100 us (44%)
  blocking collectives  393 us (16%)
  other arithmetic  331 us (13%)
  waiting for transfers between devices  324 us (13%)
  local copies, waits for them, and re-layouts  303 us (12%)
    dot_general x24, matrix products, head_scores(): jnp.einsum('qd,kd->qk', head_query, head_key, preferred_element_type=jnp....  797 us
    psum x1, blocking collectives, per_device(): lax.psum((grad_gain_one, grad_query_w, grad_key_w, grad_value_w, grad_out...  369 us
    reduce_sum x12, other arithmetic, head_backward(): jnp.sum(jnp.where(bucket == bucket_id, score_f32, 0.0))  262 us
    another operation x12, local copies, waits for them, and re-layouts, head_backward(): jnp.stack([jnp.sum(jnp.where(bucket == bucket_id, score_f32, 0.0)) for bu...  119 us
    all_to_all x1, waiting for transfers between devices, per_device(): lax.all_to_all(to_buffer(jnp.repeat(normed_two, 2, axis=0)), 'expert', sp...  64.1 us
  transfers between devices with their start and end apart: 21, of which 12 were waited for; matrix products, arithmetic and copies ran while one was open for 31% of the time, Pallas kernels for 0%

commit v1 on v0

v1 whole, which is shorter than its diff:
```python
import functools

import jax
import jax.numpy as jnp
from jax import lax
from jax.experimental import pallas as pl
from jax.experimental.pallas import tpu as pltpu
from jax.sharding import PartitionSpec as P

DH = 64
NB = 16
SEG = 128
SEGS = 20
TRUNK = 8

THRESHOLDS = (1, 2, 3, 4, 5, 6, 7, 8, 12, 16, 24, 32, 48, 64, 96)
EPS = 1e-06
MASKED = -1e30
HW = 256

F32 = jnp.float32
BF16 = jnp.bfloat16
VMEM = pl.BlockSpec(memory_space=pltpu.VMEM)
SMEM = pl.BlockSpec(memory_space=pltpu.SMEM)


def params(mib=56, **more):
    return pltpu.CompilerParams(vmem_limit_bytes=mib << 20, **more)


def dot(left, right, contract):
    return lax.dot_general(left, right, ((contract[0], contract[1]), ((), ())), preferred_element_type=F32)


NN = ((1,), (0,))
NT = ((1,), (1,))
TN = ((0,), (0,))


def rms_parts(values):
    factor = lax.rsqrt(jnp.mean(values * values, axis=-1, keepdims=True) + EPS)
    return values * factor, factor


def rms_grad(grad_out, gain_row, unit_rows, factor):
    scaled = grad_out * gain_row
    return factor * (scaled - unit_rows * jnp.mean(scaled * unit_rows, axis=-1, keepdims=True))


def bias_tiles(table):
    key = jnp.arange(SEG, dtype=jnp.int32)[:, None]
    query = jnp.arange(SEG, dtype=jnp.int32)[None, :]
    relative = table - table[:, NB - 1:]

    def looked_up(gap):
        bucket = jnp.zeros(gap.shape, jnp.int32)
        for threshold in THRESHOLDS:
            bucket = bucket + (gap >= threshold).astype(jnp.int32)
        total = jnp.zeros((table.shape[0],) + gap.shape, F32)
        for at in range(NB):
            total = total + jnp.where((bucket == at)[None], relative[:, at][:, None, None], 0.0)
        return total, bucket

    parent, parent_bucket = looked_up(query - key + SEG)
    own, own_bucket = looked_up(query - key)
    own = jnp.where((key <= query)[None], own, MASKED)
    own_bucket = jnp.where(key <= query, own_bucket, NB)
    tiles = jnp.stack([jnp.zeros_like(own), parent, own, jnp.full_like(own, MASKED)])
    tiles = tiles.transpose(0, 2, 1, 3).reshape(4, SEG, -1)
    return tiles, parent_bucket, own_bucket


def by_head(rows, heads):
    lane = lax.broadcasted_iota(jnp.int32, rows.shape, 1)
    zero = jnp.zeros_like(rows)
    return jnp.concatenate(
        [jnp.where((lane >= h * DH) & (lane < (h + 1) * DH), rows, zero) for h in range(heads)], axis=0
    )


def seg_at(index):
    return pl.ds(pl.multiple_of(index * SEG, SEG), SEG)


def attn_forward_kernel(heads, parent_ref, q_ref, k_ref, v_ref, vt_ref, bias_ref, out_ref, raw_ref, lse_ref):
    cols = heads * SEG
    trunk_len = TRUNK * SEG

    def finish(b, parts, v_parts):
        top = functools.reduce(jnp.maximum, [jnp.max(part, axis=0, keepdims=True) for part in parts])
        total = jnp.zeros((1, cols), F32)
        acc = jnp.zeros((HW, cols), F32)
        for part, vt in zip(parts, v_parts):
            prob = jnp.exp(part - top)
            total = total + jnp.sum(prob, axis=0, keepdims=True)
            acc = acc + dot(vt, prob.astype(BF16), NN)
        lse_ref[pl.ds(pl.multiple_of(b * 8, 8), 8), :] = jnp.broadcast_to(top + jnp.log(total), (8, cols))
        acc = acc / total
        pieces = [acc[h * DH:(h + 1) * DH, h * SEG:(h + 1) * SEG] for h in range(heads)]
        pieces.append(jnp.zeros((HW - heads * DH, SEG), F32))
        rows = jnp.transpose(jnp.concatenate(pieces, axis=0))
        raw_ref[seg_at(b), :] = rows
        out_ref[seg_at(b), :] = rows[:, :heads * DH].astype(BF16)

    def trunk_step(b, carry):
        q3 = by_head(q_ref[seg_at(b), :] * jnp.asarray(DH ** -0.5, BF16), heads)
        scores = dot(k_ref[0:trunk_len, :], q3, NT)
        parts = [
            scores[i * SEG:(i + 1) * SEG] + bias_ref[jnp.clip(i - b + 2, 0, 3)] for i in range(TRUNK)
        ]
        finish(b, parts, [vt_ref[:, i * SEG:(i + 1) * SEG] for i in range(TRUNK)])
        return carry

    def other_step(b, carry):
        parent = parent_ref[b]
        leaf = (parent >= TRUNK).astype(jnp.int32)
        q3 = by_head(q_ref[seg_at(b), :] * jnp.asarray(DH ** -0.5, BF16), heads)
        scores = dot(k_ref[0:trunk_len, :], q3, NT)
        last = (TRUNK - 1) * SEG
        parts = [
            scores[:last],
            scores[last:] + bias_ref[1 - leaf],
            dot(k_ref[seg_at(parent), :], q3, NT) + bias_ref[3 - 2 * leaf],
            dot(k_ref[seg_at(b), :], q3, NT) + bias_ref[2],
        ]
        finish(b, parts, [vt_ref[:, :last], vt_ref[:, last:trunk_len], vt_ref[:, seg_at(parent)], vt_ref[:, seg_at(b)]])
        return carry

    lax.fori_loop(0, TRUNK, trunk_step, 0)
    lax.fori_loop(TRUNK, SEGS, other_step, 0)


def attn_backward_kernel(
    heads, parent_ref, q_ref, k_ref, v_ref, kt_ref, raw_ref, lse_ref, grad_ref, bias_ref,
    dq_ref, dk_ref, dv_ref, bins_ref, dk_acc, dv_acc,
):
    cols = heads * SEG
    trunk_len = TRUNK * SEG
    dk_acc[...] = jnp.zeros_like(dk_acc)
    dv_acc[...] = jnp.zeros_like(dv_acc)
    bins_ref[...] = jnp.zeros_like(bins_ref)

    def common(b):
        q3 = by_head(q_ref[seg_at(b), :] * jnp.asarray(DH ** -0.5, BF16), heads)
        grad = grad_ref[seg_at(b), :]
        g3 = by_head(grad, heads)
        raw = raw_ref[seg_at(b), :]
        product = by_head(grad.astype(F32) * raw, heads)
        high = product.astype(BF16)
        low = (product - high.astype(F32)).astype(BF16)
        ones = jnp.ones((8, HW), BF16)
        row_dot = (dot(ones, high, NT) + dot(ones, low, NT))[0:1]
        lse = lse_ref[pl.ds(pl.multiple_of(b * 8, 8), 1), :]
        return q3, g3, row_dot, lse

    def block(scores, grad_prob, row_dot, lse):
        prob = jnp.exp(scores - lse)
        grad_score = prob * (grad_prob - row_dot)
        return prob.astype(BF16), grad_score

    def write_dq(b, acc):
        pieces = [acc[h * DH:(h + 1) * DH, h * SEG:(h + 1) * SEG] for h in range(heads)]
        pieces.append(jnp.zeros((HW - heads * DH, SEG), F32))
        rows = jnp.transpose(jnp.concatenate(pieces, axis=0)) * DH ** -0.5
        dq_ref[seg_at(b), :] = rows[:, :heads * DH].astype(BF16)

    def trunk_step(b, carry):
        q3, g3, row_dot, lse = common(b)
        acc = jnp.zeros((HW, cols), F32)
        for i in range(TRUNK):
            at = slice(i * SEG, (i + 1) * SEG)
            kind = jnp.clip(i - b + 2, 0, 3)
            scores = dot(k_ref[at, :], q3, NT) + bias_ref[kind]
            prob, grad_score = block(scores, dot(v_ref[at, :], g3, NT), row_dot, lse)
            bins_ref[kind] += grad_score
            grad_score = grad_score.astype(BF16)
            dv_acc[at, :] += dot(prob, g3, NN)
            dk_acc[at, :] += dot(grad_score, q3, NN)
            acc = acc + dot(kt_ref[:, at], grad_score, NN)
        write_dq(b, acc)
        return carry

    def other_step(b, carry):
        parent = parent_ref[b]
        leaf = (parent >= TRUNK).astype(jnp.int32)
        q3, g3, row_dot, lse = common(b)
        acc = jnp.zeros((HW, cols), F32)
        far = jnp.zeros((SEG, cols), F32)
        last = (TRUNK - 1) * SEG
        for i in range(TRUNK + 2):
            if i < TRUNK:
                at = slice(i * SEG, (i + 1) * SEG)
            else:
                at = seg_at(parent if i == TRUNK else b)
            scores = dot(k_ref[at, :], q3, NT)
            kind = None
            if i >= TRUNK - 1:
                kind = (1 - leaf, 3 - 2 * leaf, 2)[i - TRUNK + 1]
                scores = scores + bias_ref[kind]
            prob, grad_score = block(scores, dot(v_ref[at, :], g3, NT), row_dot, lse)
            if kind is None:
                far = far + grad_score
            else:
                bins_ref[kind] += grad_score
            grad_score = grad_score.astype(BF16)
            dv_acc[at, :] += dot(prob, g3, NN)
            dk_acc[at, :] += dot(grad_score, q3, NN)
            acc = acc + dot(kt_ref[:, at], grad_score, NN)
        bins_ref[0] += far
        write_dq(b, acc)
        return carry

    lax.fori_loop(0, TRUNK, trunk_step, 0)
    lax.fori_loop(TRUNK, SEGS, other_step, 0)
    dk_ref[...] = dk_acc[:, :heads * DH].astype(BF16)
    dv_ref[...] = dv_acc[:, :heads * DH].astype(BF16)


def one_hot_rows(first, count, places_ref):
    tokens = places_ref.shape[1]
    slot = first + lax.broadcasted_iota(jnp.int32, (count, tokens), 0)
    hit = (slot == places_ref[0:1, :]) | (slot == places_ref[1:2, :])
    return jnp.where(hit, 1.0, 0.0).astype(BF16)


def send_rows(rows, places_ref, out_refs):
    first = 0
    for out_ref in out_refs:
        slots = out_ref.shape[0]
        step = 128
        while slots % step:
            step //= 2

        def one(i, carry, out_ref=out_ref, first=first, step=step):
            at = pl.multiple_of(i * step, step)
            hot = one_hot_rows(first + at, step, places_ref)
            out_ref[pl.ds(at, step), :] = dot(hot, rows, NN).astype(BF16)
            return carry

        lax.fori_loop(0, slots // step, one, 0, unroll=2 if (slots // step) % 2 == 0 else 1)
        first += slots


def dispatch_kernel(places_ref, rows_ref, *out_refs):
    send_rows(rows_ref[...], places_ref, out_refs)


def post_kernel(
    x_ref, mixed_ref, w_ref, gain_ref, router_ref, routes_ref, places_ref,
    after_ref, normed_ref, gates_ref, *out_refs,
):
    groups, _, width = mixed_ref.shape
    after = x_ref[...].astype(F32)
    for s in range(groups):
        after = after + dot(mixed_ref[s], w_ref[s * width:(s + 1) * width, :], NN)
    after_ref[...] = after
    unit, _ = rms_parts(after)
    normed = (unit * gain_ref[...]).astype(BF16)
    normed_ref[...] = normed
    send_rows(normed_ref[...], places_ref, out_refs)
    logits = dot(normed, router_ref[...], NN)
    expert = lax.broadcasted_iota(jnp.int32, logits.shape, 1)
    first = jnp.sum(jnp.where(expert == routes_ref[:, 0:1], logits, 0.0), axis=-1, keepdims=True)
    second = jnp.sum(jnp.where(expert == routes_ref[:, 1:2], logits, 0.0), axis=-1, keepdims=True)
    top = jnp.maximum(first, second)
    first, second = jnp.exp(first - top), jnp.exp(second - top)
    gates_ref[...] = jnp.concatenate([first / (first + second), second / (first + second)], axis=1)


def expert_kernel(
    me_ref, x_ref, g_ref, other_ref, router_ref, first_ref, second_ref,
    out_ref, dx_ref, gg_ref, grad_ref, act_ref, inner_ref, out_acc, dx_acc,
):
    step = pl.program_id(0)
    rows = x_ref.shape[0]
    part = 128
    while rows % part:
        part //= 2

    @pl.when(step == 0)
    def _():
        logits = dot(x_ref[...], router_ref[...], NN)
        expert = lax.broadcasted_iota(jnp.int32, logits.shape, 1)
        mine = jnp.sum(jnp.where(expert == me_ref[0], logits, 0.0), axis=-1, keepdims=True)
        its = jnp.sum(jnp.where(expert == other_ref[...], logits, 0.0), axis=-1, keepdims=True)
        top = jnp.maximum(mine, its)
        mine, its = jnp.exp(mine - top), jnp.exp(its - top)
        grad_ref[...] = (mine / (mine + its) * g_ref[...].astype(F32)).astype(BF16)
        out_acc[...] = jnp.zeros_like(out_acc)
        dx_acc[...] = jnp.zeros_like(dx_acc)

    def one(i, carry):
        at = pl.ds(pl.multiple_of(i * part, part), part)
        value = dot(x_ref[at, :], first_ref[...], NN)
        grad_act = dot(grad_ref[at, :], second_ref[...], NT)
        square = value * value
        half = 0.5 * value
        scale = 0.7978845608028654
        th = jnp.tanh(value * (scale + (scale * 0.044715) * square))
        act = (half + half * th).astype(BF16)
        slope = 0.5 + 0.5 * th + (half * (1.0 - th * th)) * (scale + (3 * scale * 0.044715) * square)
        inner = (grad_act * slope).astype(BF16)
        act_ref[at, :] = act
        inner_ref[at, :] = inner
        out_acc[at, :] += dot(act, second_ref[...], NN)
        dx_acc[at, :] += dot(inner, first_ref[...], NT)
        return carry

    lax.fori_loop(0, rows // part, one, 0, unroll=2 if (rows // part) % 2 == 0 else 1)

    @pl.when(step == pl.num_programs(0) - 1)
    def _():
        out = out_acc[...].astype(BF16)
        out_ref[...] = out
        dx_ref[...] = dx_acc[...].astype(BF16)
        gg_ref[...] = jnp.sum(out.astype(F32) * g_ref[...].astype(F32), axis=-1, keepdims=True)


def run_expert(me, rows, grads, other, router, first_w, second_w):
    count, width = rows.shape
    hidden = first_w.shape[1]
    block = 512
    whole = lambda shape: pl.BlockSpec(shape, lambda i: (0, 0))
    return pl.pallas_call(
        expert_kernel,
        grid=(hidden // block,),
        in_specs=[
            SMEM,
            whole((count, width)),
            whole((count, width)),
            whole((count, 1)),
            whole(router.shape),
            pl.BlockSpec((width, block), lambda i: (0, i)),
            pl.BlockSpec((block, width), lambda i: (i, 0)),
        ],
        out_specs=[
            whole((count, width)),
            whole((count, width)),
            whole((count, 1)),
            whole((count, width)),
            pl.BlockSpec((count, block), lambda i: (0, i)),
            pl.BlockSpec((count, block), lambda i: (0, i)),
        ],
        out_shape=[
            jax.ShapeDtypeStruct((count, width), BF16),
            jax.ShapeDtypeStruct((count, width), BF16),
            jax.ShapeDtypeStruct((count, 1), F32),
            jax.ShapeDtypeStruct((count, width), BF16),
            jax.ShapeDtypeStruct((count, hidden), BF16),
            jax.ShapeDtypeStruct((count, hidden), BF16),
        ],
        scratch_shapes=[pltpu.VMEM((count, width), F32), pltpu.VMEM((count, width), F32)],
        compiler_params=params(dimension_semantics=("arbitrary",)),
        cost_estimate=pl.CostEstimate(
            flops=8 * count * width * hidden, bytes_accessed=4 * width * hidden, transcendentals=count * hidden
        ),
    )(me, rows, grads, other, router, first_w, second_w)


def back_kernel(
    *refs, parts,
):
    ret_refs = refs[:parts]
    (
        gg_ref, places_ref, routes_ref, gates_ref, after_ref, gain_ref, router_ref, g_ref, w_ref,
        grad_after_ref, branch_ref, gmixed_ref, glogits_ref, ggain_ref,
    ) = refs[parts:]
    tokens = after_ref.shape[0]
    groups, _, width = gmixed_ref.shape
    part = 128
    ggain_ref[...] = jnp.zeros_like(ggain_ref)

    def one(i, carry):
        at = pl.ds(pl.multiple_of(i * part, part), part)
        place0, place1 = places_ref[at, 0:1], places_ref[at, 1:2]
        first = 0
        total = jnp.zeros((part, after_ref.shape[1]), F32)
        gg0 = jnp.zeros((part, 1), F32)
        gg1 = jnp.zeros((part, 1), F32)
        for ret_ref in ret_refs:
            slots = ret_ref.shape[0]
            slot = first + lax.broadcasted_iota(jnp.int32, (part, slots), 1)
            hit0, hit1 = slot == place0, slot == place1
            gg = gg_ref[0:1, first:first + slots]
            gg0 = gg0 + jnp.sum(jnp.where(hit0, gg, 0.0), axis=-1, keepdims=True)
            gg1 = gg1 + jnp.sum(jnp.where(hit1, gg, 0.0), axis=-1, keepdims=True)
            hot = jnp.where(hit0 | hit1, 1.0, 0.0).astype(BF16)
            total = total + dot(hot, ret_ref[...], NN)
            first += slots
        gate0, gate1 = gates_ref[at, 0:1], gates_ref[at, 1:2]
        mean = gate0 * gg0 + gate1 * gg1
        expert = lax.broadcasted_iota(jnp.int32, (part, router_ref.shape[1]), 1)
        glogits = jnp.where(expert == routes_ref[at, 0:1], gate0 * (gg0 - mean), 0.0) + jnp.where(
            expert == routes_ref[at, 1:2], gate1 * (gg1 - mean), 0.0
        )
        glogits = glogits.astype(BF16)
        glogits_ref[at, :] = glogits
        incoming = dot(glogits, router_ref[...], NT) + total
        unit, factor = rms_parts(after_ref[at, :])
        grad_after = g_ref[at, :].astype(F32) + rms_grad(incoming, gain_ref[...], unit, factor)
        ggain_ref[0:1, :] += jnp.sum(incoming * unit, axis=0, keepdims=True)
        grad_after_ref[at, :] = grad_after
        branch = grad_after.astype(BF16)
        branch_ref[at, :] = branch
        for s in range(groups):
            gmixed_ref[s, at, :] = dot(branch, w_ref[s * width:(s + 1) * width, :], NT).astype(BF16)
        return carry

    lax.fori_loop(0, tokens // part, one, 0)


def combine_kernel(*refs, parts):
    ret_refs = refs[:parts]
    places_ref, gates_ref, after_ref, out_ref = refs[parts:]
    part = 128

    def one(i, carry):
        at = pl.ds(pl.multiple_of(i * part, part), part)
        total = after_ref[at, :]
        for j in range(2):
            first = 0
            picked = jnp.zeros((part, after_ref.shape[1]), F32)
            for ret_ref in ret_refs:
                slots = ret_ref.shape[0]
                slot = first + lax.broadcasted_iota(jnp.int32, (part, slots), 1)
                hot = jnp.where(slot == places_ref[at, j:j + 1], 1.0, 0.0).astype(BF16)
                picked = picked + dot(hot, ret_ref[...], NN)
                first += slots
            total = total + gates_ref[at, j:j + 1] * picked
        out_ref[at, :] = total.astype(BF16)
        return carry

    lax.fori_loop(0, after_ref.shape[0] // part, one, 0)


def per_device(
    tokens, gain_attn, w_query, w_key, w_value, w_output, rel_table, gain_moe, router,
    w_in, w_out, routes, parents, cotangent,
):
    n_shard = lax.axis_size("shard")
    n_expert = lax.axis_size("expert")
    tok, width = tokens.shape
    tree_len = tok * n_shard
    n_experts = router.shape[1]
    heads = rel_table.shape[0]
    hw = heads * DH
    capacity = max(2, tok * 20 // (7 * n_experts))
    padded = -(-capacity // 16) * 16
    half = -(-padded // 32) * 16
    cuts = (half, padded - half)

    def over_experts(array):
        return lax.all_to_all(array, "expert", split_axis=0, concat_axis=0, tiled=True)

    def over_shards(array):
        return lax.all_to_all(array, "shard", split_axis=0, concat_axis=0, tiled=True)

    tree = lax.all_gather(tokens, "shard", axis=0, tiled=True)
    small = jnp.concatenate([gain_attn, gain_moe, router.reshape(-1)])
    small = lax.all_gather(small, "shard", axis=0)
    rows = width // n_shard
    gain_one = small[:, :rows].reshape(1, width).astype(F32)
    gain_two = small[:, rows:2 * rows].reshape(1, width).astype(F32)
    router_w = small[:, 2 * rows:].reshape(width, n_experts)
    w_qkv = jnp.stack([w_query, w_key, w_value], axis=1).reshape(rows, 3, n_shard, hw).transpose(2, 0, 1, 3)
    w_cols = over_shards(w_qkv).reshape(width, 3, hw)

    expert_range = jnp.arange(n_experts, dtype=jnp.int32)
    flat_routes = routes.reshape(-1)
    expert_hot = (flat_routes[:, None] == expert_range[None, :]).astype(jnp.int32)
    earlier = jnp.cumsum(expert_hot, axis=0) - expert_hot
    rank = jnp.sum(earlier * expert_hot, axis=-1)
    places = jnp.where(
        rank < cuts[0],
        flat_routes * cuts[0] + rank,
        n_experts * cuts[0] + flat_routes * cuts[1] + rank - cuts[0],
    ).reshape(tok, 2)
    places_row = places.T
    slots = [n_experts * cut for cut in cuts]

    def dispatch(rows_of):
        return pl.pallas_call(
            dispatch_kernel,
            in_specs=[VMEM, VMEM],
            out_specs=[VMEM] * len(slots),
            out_shape=[jax.ShapeDtypeStruct((count, width), BF16) for count in slots],
            compiler_params=params(),
        )(places_row, rows_of)

    sent_grads = dispatch(cotangent)
    others = jnp.zeros((sum(slots),), F32).at[places.reshape(-1)].set(routes[:, ::-1].reshape(-1).astype(F32))
    got_grads = [over_experts(block) for block in sent_grads]
    got_others = [
        over_experts(block.reshape(n_experts, -1)).reshape(-1, 1).astype(jnp.int32)
        for block in jnp.split(others, [slots[0]])
    ]

    unit, _ = rms_parts(tree.astype(F32))
    normed_one = (unit * gain_one).astype(BF16)
    w_pad = jnp.pad(w_cols, ((0, 0), (0, 0), (0, HW - hw)))
    qkv = jnp.dot(normed_one, w_pad.reshape(width, 3 * HW), preferred_element_type=F32).astype(BF16)
    queries, keys, values = qkv[:, :HW], qkv[:, HW:2 * HW], qkv[:, 2 * HW:]
    keys_t = lax.dot_general(w_pad[:, 1], normed_one, (((0,), (1,)), ((), ())), preferred_element_type=F32).astype(BF16)
    values_t = lax.dot_general(w_pad[:, 2], normed_one, (((0,), (1,)), ((), ())), preferred_element_type=F32).astype(BF16)
    bias, parent_bucket, own_bucket = bias_tiles(rel_table.astype(F32))
    parent_row = parents[0]
    mixed, raw, lse = pl.pallas_call(
        functools.partial(attn_forward_kernel, heads),
        in_specs=[SMEM] + [VMEM] * 5,
        out_specs=[VMEM] * 3,
        out_shape=[
            jax.ShapeDtypeStruct((tree_len, hw), BF16),
            jax.ShapeDtypeStruct((tree_len, HW), F32),
            jax.ShapeDtypeStruct((SEGS * 8, heads * SEG), F32),
        ],
        compiler_params=params(),
    )(parent_row, queries, keys, values, values_t, bias)
    mixed_own = over_shards(mixed.reshape(n_shard, tok, hw))

    w_o = lax.all_gather(w_output, "shard", axis=0, tiled=True)
    after, normed_two, gates, *sent_rows = pl.pallas_call(
        post_kernel,
        in_specs=[VMEM] * 7,
        out_specs=[VMEM] * (3 + len(slots)),
        out_shape=[
            jax.ShapeDtypeStruct((tok, width), F32),
            jax.ShapeDtypeStruct((tok, width), BF16),
            jax.ShapeDtypeStruct((tok, 2), F32),
        ] + [jax.ShapeDtypeStruct((count, width), BF16) for count in slots],
        compiler_params=params(),
    )(tokens, mixed_own, w_o, gain_two, router_w, routes, places_row)
    got_rows = [over_experts(block) for block in sent_rows]

    first_w = lax.all_gather(w_in[0], "shard", axis=0, tiled=True)
    second_w = lax.all_gather(w_out[0], "shard", axis=0, tiled=True)
    me = lax.axis_index("expert").astype(jnp.int32).reshape(1)
    done = [
        run_expert(me, got_rows[c], got_grads[c], got_others[c], router_w, first_w, second_w) for c in range(len(slots))
    ]
    back_dx = [over_experts(item[1]) for item in done]
    back_gg = [over_experts(item[2].reshape(n_experts, -1)).reshape(1, -1) for item in done]
    back_out = [over_experts(item[0]) for item in done]

    def weight_grad(left, right):
        return functools.reduce(
            jnp.add, [lax.dot_general(a, b, (((0,), (0,)), ((), ())), preferred_element_type=F32) for a, b in zip(left, right)]
        ).astype(BF16)

    grad_w_in = weight_grad(got_rows, [item[5] for item in done])
    grad_w_out = weight_grad([item[4] for item in done], [item[3] for item in done])
    grad_w_in = lax.psum_scatter(grad_w_in, "shard", scatter_dimension=0, tiled=True).astype(F32)[None]
    grad_w_out = lax.psum_scatter(grad_w_out, "shard", scatter_dimension=0, tiled=True).astype(F32)[None]

    grad_after, branch, gmixed, glogits, ggain_two = pl.pallas_call(
        functools.partial(back_kernel, parts=len(slots)),
        in_specs=[VMEM] * (len(slots) + 9),
        out_specs=[VMEM] * 5,
        out_shape=[
            jax.ShapeDtypeStruct((tok, width), F32),
            jax.ShapeDtypeStruct((tok, width), BF16),
            jax.ShapeDtypeStruct((n_shard, tok, hw), BF16),
            jax.ShapeDtypeStruct((tok, n_experts), BF16),
            jax.ShapeDtypeStruct((8, width), F32),
        ],
        compiler_params=params(),
    )(*back_dx, jnp.concatenate(back_gg, axis=1), places, routes, gates, after, gain_two, router_w, cotangent, w_o)
    gmixed_tree = over_shards(gmixed).reshape(tree_len, hw)
    gmixed_tree = jnp.pad(gmixed_tree, ((0, 0), (0, HW - hw)))
    grad_router = lax.dot_general(normed_two, glogits, (((0,), (0,)), ((), ())), preferred_element_type=F32)
    grad_w_o = lax.dot_general(
        mixed_own, branch, (((1,), (0,)), ((), ())), preferred_element_type=F32
    ).astype(BF16).reshape(width, width)
    grad_w_o = lax.psum_scatter(grad_w_o, "shard", scatter_dimension=0, tiled=True).astype(F32)
    grad_w_o = lax.psum(grad_w_o, "expert")

    dq, dk, dv, bins = pl.pallas_call(
        functools.partial(attn_backward_kernel, heads),
        in_specs=[SMEM] + [VMEM] * 8,
        out_specs=[VMEM] * 4,
        out_shape=[jax.ShapeDtypeStruct((tree_len, hw), BF16)] * 3
        + [jax.ShapeDtypeStruct((4, SEG, heads * SEG), F32)],
        scratch_shapes=[pltpu.VMEM((tree_len, HW), F32), pltpu.VMEM((tree_len, HW), F32)],
        compiler_params=params(),
    )(parent_row, queries, keys, values, keys_t, raw, lse, gmixed_tree, bias)
    dqkv = jnp.concatenate([dq, dk, dv], axis=1)
    dqkv_own = over_shards(dqkv.reshape(n_shard, tok, 3 * hw))

    w_all = lax.all_gather(w_cols.reshape(width, 3 * hw), "shard", axis=0)
    grad_normed = functools.reduce(
        jnp.add,
        [
            lax.dot_general(dqkv_own[s], w_all[s], (((1,), (1,)), ((), ())), preferred_element_type=F32)
            for s in range(n_shard)
        ],
    )
    unit_own, factor_own = rms_parts(tokens.astype(F32))
    grad_tokens = (grad_after + rms_grad(grad_normed, gain_one, unit_own, factor_own)).astype(BF16)
    ggain_one = jnp.sum(grad_normed * unit_own, axis=0)

    grad_cols = lax.dot_general(normed_one, dqkv, (((0,), (0,)), ((), ())), preferred_element_type=F32)
    grad_cols = over_experts(grad_cols.astype(BF16).reshape(n_expert, width // n_expert, 3 * hw))
    grad_cols = jnp.sum(grad_cols.astype(F32), axis=0).astype(BF16)
    grad_cols = lax.all_gather(grad_cols, "expert", axis=0, tiled=True)
    grad_cols = over_shards(grad_cols.reshape(n_shard, rows, 3 * hw))
    grad_qkv = grad_cols.reshape(n_shard, rows, 3, hw).transpose(2, 1, 0, 3).reshape(3, rows, width).astype(F32)

    parent_sums = bins[1].reshape(SEG, heads, SEG)
    own_sums = bins[2].reshape(SEG, heads, SEG)
    grad_table = jnp.stack(
        [
            jnp.sum(
                jnp.where((parent_bucket == at)[:, None, :], parent_sums, 0.0)
                + jnp.where((own_bucket == at)[:, None, :], own_sums, 0.0),
                axis=(0, 2),
            )
            for at in range(NB)
        ],
        axis=1,
    )
    far = jnp.sum(bins[0].reshape(SEG, heads, SEG), axis=(0, 2))
    grad_table = grad_table.at[:, NB - 1].add(far)
    own_shard = lax.axis_index("shard")
    sums = jnp.concatenate([ggain_one, ggain_two[0], grad_router.reshape(-1)])
    table_at = jnp.zeros((n_shard, heads * NB), F32).at[own_shard].set(grad_table.reshape(-1))
    sums = lax.psum(jnp.concatenate([sums, table_at.reshape(-1)]), ("expert", "shard"))
    own = lambda array: lax.dynamic_slice_in_dim(array, own_shard * (array.shape[0] // n_shard), array.shape[0] // n_shard, 0)
    final_g1 = own(sums[:width])
    final_g2 = own(sums[width:2 * width])
    final_r = own(sums[2 * width:2 * width + width * n_experts].reshape(width, n_experts))
    final_t = own(sums[2 * width + width * n_experts:].reshape(n_shard * heads, NB))

    output = pl.pallas_call(
        functools.partial(combine_kernel, parts=len(slots)),
        in_specs=[VMEM] * (len(slots) + 3),
        out_specs=VMEM,
        out_shape=jax.ShapeDtypeStruct((tok, width), BF16),
        compiler_params=params(),
    )(*back_out, places, gates, after)

    return (
        output, grad_tokens, final_g1, grad_qkv[0], grad_qkv[1], grad_qkv[2], grad_w_o, final_t, final_g2,
        final_r, grad_w_in, grad_w_out,
    )


def solution(mesh):
    both, shard = P(("expert", "shard"), None), P("shard", None)
    three = P("expert", "shard", None)
    return jax.shard_map(
        per_device,
        mesh=mesh,
        in_specs=(
            both, P("shard"), shard, shard, shard, shard, shard, P("shard"), shard, three, three, both,
            P("expert", None), both,
        ),
        out_specs=(both, both, P("shard"), shard, shard, shard, shard, shard, P("shard"), shard, three, three),
        check_vma=False,
    )
```

time: 2510 us -> 931 us (0.37)
  matrix products: 1100 us -> 67.3 us
  other arithmetic: 331 us -> 48.4 us
  Pallas kernels: 0 us -> 235 us
  waiting for transfers between devices: 324 us -> 98.5 us
  blocking collectives: 393 us -> 230 us
  local copies, waits for them, and re-layouts: 303 us -> 152 us
  starting transfers between devices: 19.1 us -> 69.1 us
    dot_general x106 -> x14, matrix products: 1100 us -> 67.3 us  [the longest x4 36.6 us: weight_grad(): lax.dot_general(a, b, (((0,), (0,)), ((), ())), preferred_element_type=F32)]
    psum x1 -> x2, blocking collectives: 369 us -> 84 us  [the longest x1 46.9 us: per_device(): grad_w_o = lax.psum(grad_w_o, 'expert')]
    reduce_sum x35 -> x25, other arithmetic: 294 us -> 11.7 us  [the longest x19 6.24 us: per_device(): jnp.sum(jnp.where((parent_bucket == at)[:, None, :], parent_sums, 0.0) +...]
    pallas_call x0 -> x8, Pallas kernels: none -> 235 us  [the longest x2 91.9 us: run_expert(): pl.pallas_call(expert_kernel, grid=(hidden // block,), in_specs=[SMEM, wh...]
    another operation x14 -> x21, local copies, waits for them, and re-layouts: 120 us -> 4.07 us  [the longest x1 2.06 us: per_device(): w_all = lax.all_gather(w_cols.reshape(width, 3 * hw), 'shard', axis=0)]
    all_to_all x0 -> x4, blocking collectives: none -> 106 us  [the longest x3 84.1 us: over_experts(): lax.all_to_all(array, 'expert', split_axis=0, concat_axis=0, tiled=True)]
    reduce_scatter x6 -> x3, waiting for transfers between devices: 103 us -> 0.01 us  [the longest x1 0.01 us: per_device(): lax.psum_scatter(grad_w_o, 'shard', scatter_dimension=0, tiled=True)]
    broadcast_in_dim x3 -> x66, local copies, waits for them, and re-layouts: 2.98 us -> 92.1 us  [the longest x32 46.4 us: per_device(): jnp.where((own_bucket == at)[:, None, :], own_sums, 0.0)]
  transfers between devices with their start and end apart: 21 -> 22, of which waited for: 12 -> 5; matrix products, arithmetic and copies ran while one was open for 31% -> 28% of each run, Pallas kernels for 0% -> 24%
where the time goes in v1:
time: 931 us; the launch traced here: 917 us
  Pallas kernels  235 us (25%)
  blocking collectives  230 us (25%)
  local copies, waits for them, and re-layouts  152 us (16%)
  waiting for transfers between devices  98.5 us (11%)
  starting transfers between devices  69.1 us (7%)
  matrix products  67.3 us (7%)
  other arithmetic  48.4 us (5%)
  between operations  16.2 us (2%)
    pallas_call x2, Pallas kernels, run_expert(): pl.pallas_call(expert_kernel, grid=(hidden // block,), in_specs=[SMEM, wh...  91.9 us
    all_to_all x3, blocking collectives, over_experts(): lax.all_to_all(array, 'expert', split_axis=0, concat_axis=0, tiled=True)  84.1 us
    all_to_all x10, waiting for transfers between devices, over_experts(): lax.all_to_all(array, 'expert', split_axis=0, concat_axis=0, tiled=True)  75.7 us
    pallas_call x1, Pallas kernels, per_device(): pl.pallas_call(functools.partial(attn_backward_kernel, heads), in_specs=[...  70.4 us
    all_to_all x10, starting transfers between devices, over_experts(): lax.all_to_all(array, 'expert', split_axis=0, concat_axis=0, tiled=True)  52.2 us
    psum x1, blocking collectives, per_device(): grad_w_o = lax.psum(grad_w_o, 'expert')  46.9 us
    broadcast_in_dim x32, local copies, waits for them, and re-layouts, per_device(): jnp.where((own_bucket == at)[:, None, :], own_sums, 0.0)  46.4 us
    broadcast_in_dim x32, local copies, waits for them, and re-layouts, per_device(): jnp.where((parent_bucket == at)[:, None, :], parent_sums, 0.0)  45.7 us
  transfers between devices with their start and end apart: 22, of which 5 were waited for; matrix products, arithmetic and copies ran while one was open for 28% of the time, Pallas kernels for 24%

profile of v1, /device:TPU:0, one launch (start us, length us, event | category | flops | bytes accessed | tf_op | source)
XLA Modules:
  0.0 917.0 jit_solution(13620514828421850707)
XLA Ops:
  20.5 7.3 all-to-all-start.8
  44.6 16.6 %all-to-all-done = bf16[4,192,3,192]{1,3,2,0:T(8,128)(2,1)S(1)} async-done(((bf16[4,192,3,192]{1,3,2,0:T(8,128)(2,1)}), bf16[4,192,3,192]{1,3,2,0:T(8,128)(2,1)S(1)}, u32[]{:S(2)}, u32[]{:S(2)}) %all-to-all-start) | async-done | bytes 884768 | tf_op jit(solution)/shard_map/all_to_all | solution.py:456
  69.8 6.9 shard_map.231
  97.5 33.4 %shard_map.229 = (bf16[2560,192]{1,0:T(8,128)(2,1)}, f32[2560,256]{1,0:T(8,128)}, f32[160,384]{1,0:T(8,128)}) custom-call(s32[20]{0:T(128)} %bitcast.290, bf16[2560,256]{1,0:T(8,128)(2,1)} %get-tuple-element.207.q_ref, bf16[2560,256]{1,0:T(8,128)(2,1)} %get-tuple-element.206.k_ref, bf16[2560,256]{1,0:T(8,128)(2,1)} %get-tuple-element.205.v_ref, ...), custom_call_target="tpu_custom_call" | custom-call | tf_op jit(solution)/shard_map/pallas_call | solution.py:507
  132.5 21.5 %all_to_all.151 = bf16[4,640,192]{1,2,0:T(8,128)(2,1)S(1)} all-to-all(bf16[4,640,192]{1,2,0:T(8,128)(2,1)S(1)} %copy.421), channel_id=1, replica_groups=mesh['expert'=8,'shard'=4] {'shard'}, dimensions={0} | all-to-all | bytes 1966080 | tf_op jit(solution)/shard_map/all_to_all | solution.py:456
  162.6 10.1 %shard_map.230 = (f32[640,768]{1,0:T(8,128)}, bf16[640,768]{1,0:T(8,128)(2,1)}, f32[640,2]{1,0:T(8,128)}, bf16[1024,768]{1,0:T(8,128)(2,1)}, bf16[896,768]{1,0:T(8,128)(2,1)}) custom-call(bf16[640,768]{1,0:T(8,128)(2,1)} %x_ref.1, bf16[4,640,192]{2,1,0:T(8,128)(2,1)} %copy.426.mixed_ref, bf16[768,768]{1,0:T(8,128)(2,1)} %all-gather.12.cloned.1.call-done.w_ref.refs_10_, ...), custom_call_target="tpu_custom_call" | custom-call | tf_op jit(solution)/shard_map/pallas_call | solution.py:521
  172.7 23.8 %all-to-all-done.3 = bf16[8,128,768]{2,1,0:T(8,128)(2,1)} async-done(((bf16[8,128,768]{2,1,0:T(8,128)(2,1)}), bf16[8,128,768]{2,1,0:T(8,128)(2,1)}, u32[]{:S(2)}, u32[]{:S(2)}) %all-to-all-start.3) | async-done | bytes 1572896 | tf_op jit(solution)/shard_map/all_to_all | solution.py:453
  196.4 37.5 %all_to_all.152 = bf16[8,112,768]{2,1,0:T(8,128)(2,1)} all-to-all(bf16[8,112,768]{2,1,0:T(8,128)(2,1)} %bitcast.247), channel_id=1, replica_groups=mesh['expert'=8,'shard'=4] {'expert'}, dimensions={0} | all-to-all | bytes 2752512 | tf_op jit(solution)/shard_map/all_to_all | solution.py:453
  239.7 44.9 %shard_map.233 = (bf16[896,768]{1,0:T(8,128)(2,1)}, bf16[896,768]{1,0:T(8,128)(2,1)}, f32[896,1]{1,0:T(8,128)}, bf16[896,768]{1,0:T(8,128)(2,1)}, bf16[896,3072]{1,0:T(8,128)(2,1)}, /*index=5*/bf16[896,3072]{1,0:T(8,128)(2,1)}) custom-call(s32[1]{0:T(128)} %bitcast.me_ref, bf16[896,768]{1,0:T(8,128)(2,1)} %bitcast.227, bf16[896,768]{1,0:T(8,128)(2,1)} %bitcast.27.g_ref, ...), custom_call_target="tpu_custom_call" | custom-call | flops 16911433728 | bytes 9437184 | tf_op jit(solution)/shard_map/pallas_call | solution.py:324
  292.5 47.0 %shard_map.232 = (bf16[1024,768]{1,0:T(8,128)(2,1)}, bf16[1024,768]{1,0:T(8,128)(2,1)}, f32[1024,1]{1,0:T(8,128)}, bf16[1024,768]{1,0:T(8,128)(2,1)}, bf16[1024,...) custom-call(s32[1]{0:T(128)} %bitcast.me_ref, bf16[1024,768]{1,0:T(8,128)(2,1)} %bitcast.237, ...), custom_call_target="tpu_custom_call" | custom-call | flops 19327352832 | bytes 9437184 | tf_op jit(solution)/shard_map/pallas_call | solution.py:324
  340.8 12.2 %all_to_all.153 = f32[8,1,128]{2,1,0:T(1,128)S(1)} all-to-all(f32[8,1,128]{2,1,0:T(1,128)S(1)} %bitcast.285), channel_id=1, replica_groups=mesh['expert'=8,'shard'=4] {'expert'}, dimensions={0} | all-to-all | bytes 8192 | tf_op jit(solution)/shard_map/all_to_all | solution.py:453
  353.0 34.4 %all_to_all.154 = bf16[8,112,768]{2,1,0:T(8,128)(2,1)} all-to-all(bf16[8,112,768]{2,1,0:T(8,128)(2,1)} %bitcast.246), channel_id=1, replica_groups=mesh['expert'=8,'shard'=4] {'expert'}, dimensions={0} | all-to-all | bytes 2752512 | tf_op jit(solution)/shard_map/all_to_all | solution.py:453
  392.9 33.2 %all-to-all-done.10 = bf16[8,128,768]{2,1,0:T(8,128)(2,1)S(1)} async-done(((bf16[8,128,768]{2,1,0:T(8,128)(2,1)}), bf16[8,128,768]{2,1,0:T(8,128)(2,1)S(1)}, u32[]{:S(2)}, u32[]{:S(2)}) %all-to-all-start.10) | async-done | bytes 1572896 | tf_op jit(solution)/shard_map/all_to_all | solution.py:453
  427.3 13.8 %shard_map.235 = (f32[640,768]{1,0:T(8,128)}, bf16[640,768]{1,0:T(8,128)(2,1)}, bf16[4,640,192]{2,1,0:T(8,128)(2,1)}, bf16[640,8]{1,0:T(8,128)(2,1)}, f32[8,768]{1,0:T(8,128)}) custom-call(bf16[1024,768]{1,0:T(8,128)(2,1)} %bitcast.223, bf16[896,768]{1,0:T(8,128)(2,1)} %bitcast.229, f32[1,1920]{1,0:T(1,128)} %pad_maximum_fusion.3.refs_2_, ...), custom_call_target="tpu_custom_call" | custom-call | tf_op jit(solution)/shard_map/pallas_call | solution.py:554
  447.0 8.1 fusion.71
  455.2 7.2 add_convert_fusion.1
  480.0 18.7 %all-to-all-done.9 = bf16[8,112,768]{2,1,0:T(8,128)(2,1)S(1)} async-done(((bf16[8,112,768]{2,1,0:T(8,128)(2,1)}), bf16[8,112,768]{2,1,0:T(8,128)(2,1)S(1)}, u32[]{:S(2)}, u32[]{:S(2)}) %all-to-all-start.9) | async-done | bytes 1376288 | tf_op jit(solution)/shard_map/all_to_all | solution.py:453
  502.2 10.3 %fusion.72 = f32[3072,768]{1,0:T(8,128)} fusion(bf16[1024,3072]{1,0:T(8,128)(2,1)} %get-tuple-element.94, bf16[1024,768]{1,0:T(8,128)(2,1)} %get-tuple-element.95), kind=kOutput, calls=%fused_computation.227 | convolution fusion | flops 4831838208 | bytes 17301504 | tf_op jit(solution)/shard_map/dot_general | solution.py:546
  519.8 11.1 %add_convert_fusion = bf16[3072,768]{1,0:T(8,128)(2,1)} fusion(f32[3072,768]{1,0:T(8,128)} %fusion.72, bf16[896,3072]{1,0:T(8,128)(2,1)} %get-tuple-element.96, bf16[896,768]{1,0:T(8,128)(2,1)} %get-tuple-element.97), kind=kOutput, calls=%fused_computation.3 | convolution fusion | flops 4232577024 | bytes 21037056 | tf_op jit(solution)/shard_map/dot_general | solution.py:546
  633.7 70.4 %shard_map.236 = (bf16[2560,192]{1,0:T(8,128)(2,1)}, bf16[2560,192]{1,0:T(8,128)(2,1)}, bf16[2560,192]{1,0:T(8,128)(2,1)}, f32[4,128,384]{2,1,0:T(8,128)}) custom-call(s32[20]{0:T(128)} %bitcast.291, bf16[2560,256]{1,0:T(8,128)(2,1)} %get-tuple-element.207.q_ref, bf16[2560,256]{1,0:T(8,128)(2,1)} %get-tuple-element.206.k_ref, ...), custom_call_target="tpu_custom_call" | custom-call | tf_op jit(solution)/shard_map/pallas_call | solution.py:576
  723.6 8.8 shard_map.234
  754.3 35.0 %all_gather.31 = bf16[768,576]{1,0:T(8,128)(2,1)} all-gather(bf16[96,576]{1,0:T(8,128)(2,1)S(1)} %reduce_sum.394), channel_id=1, replica_groups=mesh['expert'=8,'shard'=4] {'expert'}, dimensions={0}, use_global_device_ids=true | all-gather | bytes 995328 | tf_op jit(solution)/shard_map/all_gather | solution.py:603
  789.3 46.9 %all-reduce.3 = f32[192,768]{1,0:T(8,128)} all-reduce(bf16[192,768]{1,0:T(8,128)(2,1)} %reduce-scatter.4.cloned.1.call-done), channel_id=1, replica_groups=mesh['expert'=8,'shard'=4] {'expert'}, use_global_device_ids=true, to_apply=%region_46.47 | all-reduce | flops 147456 | bytes 884736 | tf_op jit(solution)/shard_map/psum | solution.py:574
  851.1 37.1 %psum.14 = f32[7872]{0:T(1024)S(1)} all-reduce(f32[7872]{0:T(1024)S(1)} %pad_maximum_fusion.2), channel_id=1, replica_groups=mesh['expert'=8,'shard'=4] {'expert','shard'}, use_global_device_ids=true, to_apply=%region_43.44 | all-reduce | flops 7872 | bytes 62976 | tf_op jit(solution)/shard_map/psum | solution.py:625
  (473 shorter events, 304.7 us)
Async XLA Ops:
  7.2 77.9 %all-gather.10.cloned.1.call-start = ((), (), s32[]{:S(2)}) async-start(), calls=%async_computation.21 | async-start | bytes 4915200 | tf_op jit(solution)/shard_map/all_gather | solution.py:458
  7.9 154.7 %all-gather.12.cloned.1.call-start = ((), (), s32[]{:S(2)}) async-start(), calls=%async_computation.22 | async-start | bytes 1474560 | tf_op jit(solution)/shard_map/all_gather | solution.py:520
  8.7 231.1 %all-gather.16.cloned.1.call-start = ((), (), s32[]{:S(2)}) async-start(), calls=%async_computation.27 | async-start | bytes 5898240 | tf_op jit(solution)/shard_map/all_gather | solution.py:534
  13.6 55.5 %copy-start.8 = (s32[640,2]{1,0:T(8,128)}, s32[640,2]{1,0:T(8,128)S(1)}, u32[]{:S(2)}) copy-start(s32[640,2]{1,0:T(8,128)S(1)} %get-tuple-element.212.refs_2_.refs_3_) | copy-start | bytes 15364
  20.5 18.3 %all-to-all-start.8 = ((f32[8,1,112]{2,1,0:T(1,128)}), f32[8,1,112]{2,1,0:T(1,128)S(1)}, u32[]{:S(2)}, u32[]{:S(2)}) async-start(f32[8,1,112]{2,1,0:T(1,128)} %all_to_all.114), calls=%async_computation.8 | async-start | bytes 8192 | tf_op jit(solution)/shard_map/all_to_all | solution.py:453
  27.8 212.0 %all-gather.18.cloned.1.call-start = ((), (), s32[]{:S(2)}) async-start(), calls=%async_computation.28 | async-start | bytes 5898240 | tf_op jit(solution)/shard_map/all_gather | solution.py:535
  39.4 21.8 %all-to-all-start = ((bf16[4,192,3,192]{1,3,2,0:T(8,128)(2,1)}), bf16[4,192,3,192]{1,3,2,0:T(8,128)(2,1)S(1)}, u32[]{:S(2)}, u32[]{:S(2)}) async-start(bf16[4,192,3,192]{1,3,2,0:T(8,128)(2,1)} %maximum_bitcast_fusion), calls=%async_computation | async-start | bytes 2359296 | tf_op jit(solution)/shard_map/all_to_all | solution.py:456
  61.2 17.6 %all-to-all-start.4 = ((f32[8,1,128]{2,1,0:T(1,128)}), f32[8,1,128]{2,1,0:T(1,128)S(1)}, u32[]{:S(2)}, u32[]{:S(2)}) async-start(f32[8,1,128]{2,1,0:T(1,128)} %bitcast.17), calls=%async_computation.4 | async-start | bytes 8192 | tf_op jit(solution)/shard_map/all_to_all | solution.py:453
  78.8 53.6 %all-to-all-start.7 = ((bf16[8,112,768]{2,1,0:T(8,128)(2,1)}), bf16[8,112,768]{2,1,0:T(8,128)(2,1)}, u32[]{:S(2)}, u32[]{:S(2)}) async-start(bf16[8,112,768]{2,1,0:T(8,128)(2,1)} %bitcast.26), calls=%async_computation.7 | async-start | bytes 2752512 | tf_op jit(solution)/shard_map/all_to_all | solution.py:453
  154.0 42.4 %all-to-all-start.3 = ((bf16[8,128,768]{2,1,0:T(8,128)(2,1)}), bf16[8,128,768]{2,1,0:T(8,128)(2,1)}, u32[]{:S(2)}, u32[]{:S(2)}) async-start(bf16[8,128,768]{2,1,0:T(8,128)(2,1)} %bitcast.239), calls=%async_computation.3 | async-start | bytes 3145728 | tf_op jit(solution)/shard_map/all_to_all | solution.py:453
  196.4 41.3 %copy-start.66 = (f32[8,1,112]{2,1,0:T(1,128)S(1)}, f32[8,1,112]{2,1,0:T(1,128)}, u32[]{:S(2)}) copy-start(f32[8,1,112]{2,1,0:T(1,128)} %copy-done.65) | copy-start | bytes 10756
  233.9 52.7 %all-to-all-start.2 = ((bf16[8,128,768]{2,1,0:T(8,128)(2,1)}), bf16[8,128,768]{2,1,0:T(8,128)(2,1)S(1)}, u32[]{:S(2)}, u32[]{:S(2)}) async-start(bf16[8,128,768]{2,1,0:T(8,128)(2,1)} %bitcast.240), calls=%async_computation.2 | async-start | bytes 3145728 | tf_op jit(solution)/shard_map/all_to_all | solution.py:453
  286.6 54.2 %all-to-all-start.13 = ((f32[8,1,112]{2,1,0:T(1,128)}), f32[8,1,112]{2,1,0:T(1,128)S(1)}, u32[]{:S(2)}, u32[]{:S(2)}) async-start(f32[8,1,112]{2,1,0:T(1,128)} %bitcast.36), calls=%async_computation.13 | async-start | bytes 8192 | tf_op jit(solution)/shard_map/all_to_all | solution.py:453
  387.4 38.7 %all-to-all-start.10 = ((bf16[8,128,768]{2,1,0:T(8,128)(2,1)}), bf16[8,128,768]{2,1,0:T(8,128)(2,1)S(1)}, u32[]{:S(2)}, u32[]{:S(2)}) async-start(bf16[8,128,768]{2,1,0:T(8,128)(2,1)} %bitcast.241), calls=%async_computation.10 | async-start | bytes 3145728 | tf_op jit(solution)/shard_map/all_to_all | solution.py:453
  391.0 398.3 %reduce-scatter.4.cloned.1.call-start = ((), (), s32[]{:S(2)}) async-start(), calls=%async_computation.24 | async-start | bytes 1474560 | tf_op jit(solution)/shard_map/reduce_scatter | solution.py:573
  444.4 396.1 %all-gather.14.cloned.1.call-start = ((), (), s32[]{:S(2)}) async-start(), calls=%async_computation.23 | async-start | bytes 4423680 | tf_op jit(solution)/shard_map/all_gather | solution.py:588
  446.5 457.4 %reduce-scatter.6.cloned.1.call-start = ((), (), s32[]{:S(2)}) async-start(), calls=%async_computation.25 | async-start | bytes 5898240 | tf_op jit(solution)/shard_map/reduce_scatter | solution.py:551
  462.4 36.3 %all-to-all-start.9 = ((bf16[8,112,768]{2,1,0:T(8,128)(2,1)}), bf16[8,112,768]{2,1,0:T(8,128)(2,1)S(1)}, u32[]{:S(2)}, u32[]{:S(2)}) async-start(bf16[8,112,768]{2,1,0:T(8,128)(2,1)} %bitcast.245), calls=%async_computation.9 | async-start | bytes 2752512 | tf_op jit(solution)/shard_map/all_to_all | solution.py:453
  498.7 17.2 %all-to-all-start.14 = ((bf16[4,640,192]{1,2,0:T(8,128)(2,1)}), bf16[4,640,192]{1,2,0:T(8,128)(2,1)S(1)}, u32[]{:S(2)}, u32[]{:S(2)}) async-start(bf16[4,640,192]{1,2,0:T(8,128)(2,1)} %copy.438), calls=%async_computation.14 | async-start | bytes 1966080 | tf_op jit(solution)/shard_map/all_to_all | solution.py:456
  515.9 197.5 %all-to-all-start.5 = ((bf16[8,128,768]{2,1,0:T(8,128)(2,1)}), bf16[8,128,768]{2,1,0:T(8,128)(2,1)S(1)}, u32[]{:S(2)}, u32[]{:S(2)}) async-start(bf16[8,128,768]{2,1,0:T(8,128)(2,1)} %bitcast.236), calls=%async_computation.5 | async-start | bytes 3145728 | tf_op jit(solution)/shard_map/all_to_all | solution.py:453
  519.6 387.3 %reduce-scatter.8.cloned.1.call-start = ((), (), s32[]{:S(2)}) async-start(), calls=%async_computation.26 | async-start | bytes 5898240 | tf_op jit(solution)/shard_map/reduce_scatter | solution.py:552
  713.4 31.8 %all-to-all-start.16 = ((bf16[8,96,576]{2,1,0:T(8,128)(2,1)}), bf16[8,96,576]{2,1,0:T(8,128)(2,1)S(1)}, u32[]{:S(2)}, u32[]{:S(2)}) async-start(bf16[8,96,576]{2,1,0:T(8,128)(2,1)} %bitcast.116), calls=%async_computation.16 | async-start | bytes 1966080 | tf_op jit(solution)/shard_map/all_to_all | solution.py:453
  745.2 91.0 %all-to-all-start.15 = ((bf16[4,640,576]{1,2,0:T(8,128)(2,1)}), bf16[4,640,576]{1,2,0:T(8,128)(2,1)}, u32[]{:S(2)}, u32[]{:S(2)}) async-start(bf16[4,640,576]{1,2,0:T(8,128)(2,1)} %copy.441), calls=%async_computation.15 | async-start | bytes 5898240 | tf_op jit(solution)/shard_map/all_to_all | solution.py:456
  836.2 52.0 %all-to-all-start.17 = ((bf16[4,192,576]{2,1,0:T(8,128)(2,1)}), bf16[4,192,576]{2,1,0:T(8,128)(2,1)}, u32[]{:S(2)}, u32[]{:S(2)}) async-start(bf16[4,192,576]{2,1,0:T(8,128)(2,1)} %bitcast.117), calls=%async_computation.17 | async-start | bytes 1966080 | tf_op jit(solution)/shard_map/all_to_all | solution.py:456
  (83 other events, 740.1 us)
Sparse Core Ops, SparseCore 0:
  9.6 35.8 all-gather.9
  47.0 19.5 all-gather.11
  68.2 37.9 all-gather.15
  107.6 42.8 all-gather.17
  444.5 23.9 reduce-scatter.3
  470.0 30.7 all-gather.13
  503.5 47.8 reduce-scatter.5
  553.9 47.8 reduce-scatter.7

commit v2 on v1

v2 whole, which is shorter than its diff:
```python
import functools
import math

import jax
import jax.numpy as jnp
from jax import lax
from jax.experimental import pallas as pl
from jax.experimental.pallas import tpu as pltpu
from jax.sharding import PartitionSpec as P

DH = 64
NB = 16
SEG = 128
SEGS = 20
TRUNK = 8
SPARE = 3

THRESHOLDS = (1, 2, 3, 4, 5, 6, 7, 8, 12, 16, 24, 32, 48, 64, 96)
EPS = 1e-06
MASKED = -1e30
HW = 256

F32 = jnp.float32
BF16 = jnp.bfloat16
VMEM = pl.BlockSpec(memory_space=pltpu.VMEM)
SMEM = pl.BlockSpec(memory_space=pltpu.SMEM)
ANY = pl.BlockSpec(memory_space=pl.ANY)

NN = ((1,), (0,))
NT = ((1,), (1,))
TN = ((0,), (0,))


def params(mib=60, **more):
    return pltpu.CompilerParams(vmem_limit_bytes=mib << 20, **more)


SHORT = pl.CostEstimate(flops=0, bytes_accessed=1024, transcendentals=0)
LONG = pl.CostEstimate(flops=1 << 40, bytes_accessed=1 << 32, transcendentals=0)


def dot(left, right, contract):
    return lax.dot_general(left, right, (contract, ((), ())), preferred_element_type=F32)


def arrays(*shapes):
    return [jax.ShapeDtypeStruct(shape, dtype) for shape, dtype in shapes]


def rms_parts(values):
    factor = lax.rsqrt(jnp.mean(values * values, axis=-1, keepdims=True) + EPS)
    return values * factor, factor


def rms_grad(grad_out, gain_row, unit_rows, factor):
    scaled = grad_out * gain_row
    return factor * (scaled - unit_rows * jnp.mean(scaled * unit_rows, axis=-1, keepdims=True))


def columns_kernel(me_ref, q_ref, k_ref, v_ref, more_ref, out_ref):
    groups, depth, width = out_ref.shape
    hw = q_ref.shape[1] // groups
    blank = jnp.zeros((depth, width - 3 * hw - more_ref.shape[1]), BF16)
    for s in range(groups):
        at = slice(s * hw, (s + 1) * hw)
        out_ref[jnp.bitwise_xor(me_ref[0], s)] = jnp.concatenate(
            [q_ref[:, at], k_ref[:, at], v_ref[:, at], more_ref[...], blank], axis=1
        )


def project_kernel(
    heads, me_ref, table_ref, w0, w1, w2, w3, t0, t1, t2, t3, before_ref,
    n0, n1, n2, n3, q_ref, k_ref, v_ref, kt_ref, vt_ref, w_ref, bias_ref, gain_ref, gain_two_ref, router_ref, w_pad,
):
    hw = heads * DH
    blank = jnp.zeros((w0.shape[0], HW - hw), BF16)
    for rel, piece_ref in enumerate((w0, w1, w2, w3)):
        depth = piece_ref.shape[0]
        at = pl.ds(pl.multiple_of(jnp.bitwise_xor(me_ref[0], rel) * depth, 16), depth)
        piece = piece_ref[...]
        blank_end = jnp.zeros((depth, w_ref.shape[1] - 3 * hw), BF16)
        w_ref[at, :] = jnp.concatenate([piece[:, :3 * hw], blank_end], axis=1)
        router_ref[at, :] = piece[:, 3 * hw + 2:3 * hw + 2 + router_ref.shape[1]]
        padded = [part for c in range(3) for part in (piece[:, c * hw:(c + 1) * hw], blank)]
        padded.append(piece[:, 3 * hw:3 * hw + 2])
        padded.append(jnp.zeros((depth, w_pad.shape[1] - 3 * HW - 2), BF16))
        w_pad[at, :] = jnp.concatenate(padded, axis=1)
    gains = jnp.transpose(w_pad[:, 3 * HW:].astype(F32))
    gain_ref[...] = gains[0:1]
    gain_two_ref[...] = gains[1:2]
    for rel, (t_ref, n_ref) in enumerate(zip((t0, t1, t2, t3), (n0, n1, n2, n3))):
        count = t_ref.shape[0]
        unit, _ = rms_parts(t_ref[...].astype(F32))
        n_ref[...] = (unit * gain_ref[...]).astype(BF16)
        at = pl.ds(pl.multiple_of(jnp.bitwise_xor(me_ref[0], rel) * count, SEG), count)
        qkv = dot(n_ref[...], w_pad[:, :3 * HW], NN)
        q_ref[at, :] = qkv[:, :HW].astype(BF16) * jnp.asarray(DH ** -0.5, BF16)
        k_ref[at, :] = qkv[:, HW:2 * HW].astype(BF16)
        v_ref[at, :] = qkv[:, 2 * HW:].astype(BF16)
        kt_ref[:, at] = jnp.transpose(qkv[:, HW:2 * HW]).astype(BF16)
        vt_ref[:, at] = jnp.transpose(qkv[:, 2 * HW:]).astype(BF16)
    key = lax.broadcasted_iota(jnp.int32, (SEG, SEG), 0)
    query = lax.broadcasted_iota(jnp.int32, (SEG, SEG), 1)
    bias_ref[0] = jnp.zeros((SEG, heads * SEG), F32)
    bias_ref[3] = jnp.full((SEG, heads * SEG), MASKED, F32)
    for h in range(heads):
        last = table_ref[h, NB - 1]
        at = slice(h * SEG, (h + 1) * SEG)
        for kind, gap in ((1, query - key + SEG), (2, query - key)):
            tile = jnp.zeros((SEG, SEG), F32) + (table_ref[h, 0] - last)
            for i, threshold in enumerate(THRESHOLDS):
                tile = jnp.where(gap >= threshold, table_ref[h, i + 1] - last, tile)
            bias_ref[kind, :, at] = jnp.where(gap >= 0, tile, MASKED)


def by_head(rows, heads):
    lane = lax.broadcasted_iota(jnp.int32, rows.shape, 1)
    zero = jnp.zeros_like(rows)
    return jnp.concatenate(
        [jnp.where((lane >= h * DH) & (lane < (h + 1) * DH), rows, zero) for h in range(heads)], axis=0
    )


def seg_at(index):
    if isinstance(index, int):
        return slice(index * SEG, (index + 1) * SEG)
    return pl.ds(pl.multiple_of(index * SEG, SEG), SEG)


def head_rows(acc, heads):
    pieces = [acc[h * DH:(h + 1) * DH, h * SEG:(h + 1) * SEG] for h in range(heads)]
    pieces.append(jnp.zeros((HW - heads * DH, SEG), F32))
    return jnp.transpose(jnp.concatenate(pieces, axis=0))


def pair_bias(bias_ref, first, second):
    return jnp.concatenate([bias_ref[first], bias_ref[second]], axis=1)


def attn_forward_kernel(
    heads, me_ref, parent_ref, q_ref, k_ref, v_ref, vt_ref, bias_ref, o0, o1, o2, o3, raw_ref, lse_ref, out_all
):
    cols = heads * SEG
    trunk_len = TRUNK * SEG
    last = trunk_len - SEG

    def queries(b):
        return by_head(q_ref[seg_at(b), :], heads)

    def finish(b, acc, total, top):
        lse_ref[pl.ds(b * 8, 8), :] = jnp.broadcast_to(top + jnp.log(total), (8, cols))
        rows = head_rows(acc / total, heads)
        raw_ref[seg_at(b), :] = rows
        out_all[seg_at(b), :] = rows.astype(BF16)

    for j in range(TRUNK // 2):
        q6 = jnp.concatenate([queries(2 * j), queries(2 * j + 1)], axis=0)
        scores = dot(k_ref[0:(j + 1) * 2 * SEG, :], q6, NT)
        parts = []
        if j > 0:
            far = (2 * j - 1) * SEG
            parts = [scores[:far], scores[far:far + SEG] + pair_bias(bias_ref, 1, 0)]
        parts.append(scores[2 * j * SEG:(2 * j + 1) * SEG] + pair_bias(bias_ref, 2, 1))
        parts.append(scores[(2 * j + 1) * SEG:] + pair_bias(bias_ref, 3, 2))
        top = functools.reduce(jnp.maximum, [jnp.max(part, axis=0, keepdims=True) for part in parts])
        parts = [jnp.exp(part - top) for part in parts]
        total = functools.reduce(jnp.add, [jnp.sum(part, axis=0, keepdims=True) for part in parts])
        acc = dot(vt_ref[:, 0:(j + 1) * 2 * SEG], jnp.concatenate([p.astype(BF16) for p in parts], axis=0), NN)
        for s in range(2):
            at = slice(s * cols, (s + 1) * cols)
            finish(2 * j + s, acc[:, at], total[:, at], top[:, at])

    def other_step(i, carry):
        segs = [TRUNK + 2 * i, TRUNK + 2 * i + 1]
        parents = [parent_ref[b] for b in segs]
        leaf = [(parent >= TRUNK).astype(jnp.int32) for parent in parents]
        q3 = [queries(b) for b in segs]
        q6 = jnp.concatenate(q3, axis=0)
        scores = dot(k_ref[0:trunk_len, :], q6, NT)
        near = scores[last:] + pair_bias(bias_ref, 1 - leaf[0], 1 - leaf[1])
        far = scores[:last]
        extra = []
        for s in range(2):
            keys = jnp.concatenate([k_ref[seg_at(parents[s]), :], k_ref[seg_at(segs[s]), :]], axis=0)
            bias = jnp.concatenate([bias_ref[3 - 2 * leaf[s]], bias_ref[2]], axis=0)
            extra.append(dot(keys, q3[s], NT) + bias)
        top = jnp.maximum(jnp.max(far, axis=0, keepdims=True), jnp.max(near, axis=0, keepdims=True))
        top = jnp.maximum(top, jnp.concatenate([jnp.max(e, axis=0, keepdims=True) for e in extra], axis=1))
        far, near = jnp.exp(far - top), jnp.exp(near - top)
        extra = [jnp.exp(extra[s] - top[:, s * cols:(s + 1) * cols]) for s in range(2)]
        total = jnp.sum(far, axis=0, keepdims=True) + jnp.sum(near, axis=0, keepdims=True)
        total = total + jnp.concatenate([jnp.sum(e, axis=0, keepdims=True) for e in extra], axis=1)
        acc = dot(vt_ref[:, 0:trunk_len], jnp.concatenate([far.astype(BF16), near.astype(BF16)], axis=0), NN)
        for s in range(2):
            at = slice(s * cols, (s + 1) * cols)
            values = jnp.concatenate([vt_ref[:, seg_at(parents[s])], vt_ref[:, seg_at(segs[s])]], axis=1)
            finish(segs[s], acc[:, at] + dot(values, extra[s].astype(BF16), NN), total[:, at], top[:, at])
        return carry

    lax.fori_loop(0, (SEGS - TRUNK) // 2, other_step, 0)
    for rel, o_ref in enumerate((o0, o1, o2, o3)):
        count, width = o_ref.shape
        at = pl.ds(pl.multiple_of(jnp.bitwise_xor(me_ref[0], rel) * count, SEG), count)
        o_ref[...] = out_all[at, :][:, :width]


def attn_backward_kernel(
    heads, me_ref, parent_ref, q_ref, k_ref, v_ref, kt_ref, raw_ref, lse_ref, g0, g1, g2, g3_ref, bias_ref,
    d0, d1, d2, d3, bins_ref, grad_all, dq_all, dk_acc, dv_acc, bins_acc,
):
    cols = heads * SEG
    trunk_len = TRUNK * SEG
    dk_acc[...] = jnp.zeros_like(dk_acc)
    dv_acc[...] = jnp.zeros_like(dv_acc)
    bins_acc[...] = jnp.zeros_like(bins_acc)
    for rel, g_ref in enumerate((g0, g1, g2, g3_ref)):
        count, width = g_ref.shape
        at = pl.ds(pl.multiple_of(jnp.bitwise_xor(me_ref[0], rel) * count, SEG), count)
        grad_all[at, :] = jnp.concatenate([g_ref[...], jnp.zeros((count, HW - width), BF16)], axis=1)

    def common(b):
        q3 = by_head(q_ref[seg_at(b), :], heads)
        grad = grad_all[seg_at(b), :]
        product = by_head(grad.astype(F32) * raw_ref[seg_at(b), :], heads)
        high = product.astype(BF16)
        low = (product - high.astype(F32)).astype(BF16)
        ones = jnp.ones((8, HW), BF16)
        row_dot = (dot(ones, high, NT) + dot(ones, low, NT))[0:1]
        return q3, by_head(grad, heads), row_dot, lse_ref[pl.ds(b * 8, 8), :][0:1]

    def block(keys, values, q, g, row_dot, lse, bias):
        scores = dot(keys, q, NT)
        if bias is not None:
            scores = scores + bias
        prob = jnp.exp(scores - lse)
        grad_score = prob * (dot(values, g, NT) - row_dot)
        return prob.astype(BF16), grad_score

    def write_dq(b, acc):
        dq_all[seg_at(b), :] = (head_rows(acc, heads) * DH ** -0.5).astype(BF16)

    def both(pair):
        return [jnp.concatenate([a, b], axis=0 if a.shape[0] > 1 else 1) for a, b in zip(*pair)]

    zero = 0
    for j in range(TRUNK // 2):
        q6, g6, row_dot, lse = both([common(2 * j), common(2 * j + 1)])
        kept = []
        for i in range(j + 1):
            at = slice(2 * i * SEG, 2 * (i + 1) * SEG)
            bias = None
            if i == j:
                bias = jnp.concatenate([pair_bias(bias_ref, 2, 1), pair_bias(bias_ref, 3, 2)], axis=0)
            if i == j - 1:
                bias = jnp.concatenate([pair_bias(bias_ref, zero, zero), pair_bias(bias_ref, 1, zero)], axis=0)
            prob, score = block(k_ref[at, :], v_ref[at, :], q6, g6, row_dot, lse, bias)
            if i == j:
                bins_acc[0] += score[:SEG, cols:]
                bins_acc[1] += score[:SEG, :cols] + score[SEG:, cols:]
            if i == j - 1:
                bins_acc[0] += score[SEG:, :cols]
            score = score.astype(BF16)
            dv_acc[at, :] += dot(prob, g6, NN)
            dk_acc[at, :] += dot(score, q6, NN)
            kept.append(score)
        acc = dot(kt_ref[:, 0:(j + 1) * 2 * SEG], jnp.concatenate(kept, axis=0), NN)
        for s in range(2):
            write_dq(2 * j + s, acc[:, s * cols:(s + 1) * cols])

    def other_step(step, carry):
        segs = [TRUNK + 2 * step, TRUNK + 2 * step + 1]
        parents = [parent_ref[b] for b in segs]
        leaf = [(parent >= TRUNK).astype(jnp.int32) for parent in parents]
        each = [common(b) for b in segs]
        q6, g6, row_dot, lse = both(each)
        kept = []
        for i in range(TRUNK // 2):
            at = slice(2 * i * SEG, 2 * (i + 1) * SEG)
            bias = None
            if i == TRUNK // 2 - 1:
                near = pair_bias(bias_ref, 1 - leaf[0], 1 - leaf[1])
                bias = jnp.concatenate([jnp.zeros_like(near), near], axis=0)
            prob, score = block(k_ref[at, :], v_ref[at, :], q6, g6, row_dot, lse, bias)
            if i == TRUNK // 2 - 1:
                for s in range(2):
                    bins_acc[0] += jnp.where(leaf[s] == 0, score[SEG:, s * cols:(s + 1) * cols], 0.0)
            score = score.astype(BF16)
            dv_acc[at, :] += dot(prob, g6, NN)
            dk_acc[at, :] += dot(score, q6, NN)
            kept.append(score)
        acc = dot(kt_ref[:, 0:trunk_len], jnp.concatenate(kept, axis=0), NN)
        for s in range(2):
            q3, g3, row, own_lse = each[s]
            first, second = seg_at(parents[s]), seg_at(segs[s])
            keys = jnp.concatenate([k_ref[first, :], k_ref[second, :]], axis=0)
            values = jnp.concatenate([v_ref[first, :], v_ref[second, :]], axis=0)
            keys_t = jnp.concatenate([kt_ref[:, first], kt_ref[:, second]], axis=1)
            bias = jnp.concatenate([bias_ref[3 - 2 * leaf[s]], bias_ref[2]], axis=0)
            prob, score = block(keys, values, q3, g3, row, own_lse, bias)
            bins_acc[0] += score[:SEG]
            bins_acc[1] += score[SEG:]
            score = score.astype(BF16)
            grad_v, grad_k = dot(prob, g3, NN), dot(score, q3, NN)
            dv_acc[first, :] += grad_v[:SEG]
            dv_acc[second, :] += grad_v[SEG:]
            dk_acc[first, :] += grad_k[:SEG]
            dk_acc[second, :] += grad_k[SEG:]
            write_dq(segs[s], acc[:, s * cols:(s + 1) * cols] + dot(keys_t, score, NN))
        return carry

    lax.fori_loop(0, (SEGS - TRUNK) // 2, other_step, 0)
    for rel, d_ref in enumerate((d0, d1, d2, d3)):
        count = d_ref.shape[0]
        width = heads * DH
        at = pl.ds(pl.multiple_of(jnp.bitwise_xor(me_ref[0], rel) * count, SEG), count)
        parts = [dq_all[at, :][:, :width], dk_acc[at, :][:, :width].astype(BF16), dv_acc[at, :][:, :width].astype(BF16)]
        parts.append(jnp.zeros((count, d_ref.shape[1] - 3 * width), BF16))
        d_ref[...] = jnp.concatenate(parts, axis=1)
    key = lax.broadcasted_iota(jnp.int32, (SEG, cols), 0)
    query = lax.broadcasted_iota(jnp.int32, (SEG, cols), 1) % SEG
    gap = query - key
    parent_sum, own_sum = bins_acc[0], bins_acc[1]
    lines = [jnp.sum(parent_sum + own_sum, axis=0, keepdims=True)]
    for threshold in THRESHOLDS:
        hit = jnp.where(gap + SEG >= threshold, parent_sum, 0.0) + jnp.where(gap >= threshold, own_sum, 0.0)
        lines.append(jnp.sum(hit, axis=0, keepdims=True))
    bins_ref[...] = jnp.concatenate(lines, axis=0)


class Slots:
    def __init__(self, n_expert, capacity):
        self.n_expert = n_expert
        self.cut = n_expert == 8
        self.near = n_expert // 2 if self.cut else n_expert
        self.block = -(-(capacity + SPARE) // 16) * 16
        self.chunks = [[list(range(self.near))]]
        if self.cut:
            self.chunks += [[[4], [5]], [[6], [7]]]
        self.arrays = [array for chunk in self.chunks for array in chunk]

    def block_of(self, expert, me):
        if not self.cut:
            return expert
        inside = jnp.bitwise_xor(expert, me) & (self.near - 1)
        return jnp.where((expert & self.near) == (me & self.near), expert & (self.near - 1), self.near + inside)

    def expert_of(self, block, me):
        if not self.cut:
            return block
        if block < self.near:
            return (me & self.near) + block
        return jnp.bitwise_xor(me, block)

    def split(self, flat):
        flat = list(flat)
        return [[flat.pop(0) for _ in chunk] for chunk in self.chunks]

    def exchange(self, c, blocks):
        if c == 0:
            groups = [[g * self.near + i for i in range(self.near)] for g in range(self.n_expert // self.near)]
            return [
                lax.all_to_all(
                    blocks[0], "expert", split_axis=0, concat_axis=0, tiled=True,
                    axis_index_groups=groups if self.cut else None,
                )
            ]
        return [swap(block, "expert", array[0]) for array, block in zip(self.chunks[c], blocks)]


def over_experts(block):
    return lax.all_to_all(block, "expert", split_axis=0, concat_axis=0, tiled=True)


def swap(block, axis, rel):
    if rel == 0:
        return block
    return lax.ppermute(block, axis, [(i, i ^ rel) for i in range(lax.axis_size(axis))])


def swap_all(blocks, axis):
    return [swap(block, axis, rel) for rel, block in enumerate(blocks)]


def from_all(block):
    near, far = swap(block, "shard", 1), swap(block, "shard", 2)
    return [block, near, far, swap(far, "shard", 1)]


def reorder(parts, me):
    bit = 1
    while bit < len(parts):
        parts = [jnp.where(me & bit, parts[i ^ bit], parts[i]) for i in range(len(parts))]
        bit *= 2
    return parts


def send_rows(slots, rows, places_ref, out_refs):
    tokens = places_ref.shape[1]
    for array, out_ref in zip(slots.arrays, out_refs):
        for i, block in enumerate(array):
            slot = block * slots.block + lax.broadcasted_iota(jnp.int32, (slots.block, tokens), 0)
            hit = (slot == places_ref[0:1, :]) | (slot == places_ref[1:2, :])
            picked = dot(jnp.where(hit, 1.0, 0.0).astype(BF16), rows, NN).astype(BF16)
            out_ref[i * slots.block:(i + 1) * slots.block, :] = picked


def diagonal(count):
    return lax.broadcasted_iota(jnp.int32, (count, count), 0) == lax.broadcasted_iota(jnp.int32, (count, count), 1)


def padded_row(row, width):
    count = row.shape[1]
    return row if count == width else jnp.concatenate([row, jnp.zeros((1, width - count), row.dtype)], axis=1)


def dispatch_kernel(slots, me_ref, places_ref, others_ref, rows_ref, *refs):
    out_ref = refs[-1]
    tokens = places_ref.shape[1]
    width = rows_ref.shape[1]
    rows = rows_ref[...]
    count = slots.block

    def one(expert, carry):
        slot = slots.block_of(expert, me_ref[0]) * count + lax.broadcasted_iota(jnp.int32, (count, tokens), 0)
        hot = [jnp.where(slot == places_ref[j:j + 1, :], 1.0, 0.0).astype(BF16) for j in range(2)]
        picked = dot(hot[0] + hot[1], rows, NN)
        ids = sum(dot(others_ref[8 * j:8 * j + 8, :], hot[j], NT) for j in range(2))
        line = lax.broadcasted_iota(jnp.int32, picked.shape, 0)
        picked = jnp.where(line == count - 1, padded_row(ids[0:1], width), picked)
        out_ref[pl.ds(pl.multiple_of(expert * count, 16), count), :] = picked.astype(BF16)
        return carry

    lax.fori_loop(0, slots.n_expert, one, 0)


def post_kernel(
    slots, me_ref, x_ref, gain_ref, router_ref, routes_ref, places_ref, m0, m1, m2, m3, w_ref, before_ref,
    after_ref, normed_ref, gates_ref, *out_refs,
):
    after = x_ref[...].astype(F32)
    for rel, m_ref in enumerate((m0, m1, m2, m3)):
        after = after + dot(m_ref[...], w_ref[jnp.bitwise_xor(me_ref[0], rel)], NN)
    after_ref[...] = after
    unit, _ = rms_parts(after)
    normed = (unit * gain_ref[...]).astype(BF16)
    normed_ref[...] = normed
    send_rows(slots, normed_ref[...], places_ref, out_refs)
    logits = dot(normed, router_ref[...], NN)
    expert = lax.broadcasted_iota(jnp.int32, logits.shape, 1)
    first = jnp.sum(jnp.where(expert == routes_ref[:, 0:1], logits, 0.0), axis=-1, keepdims=True)
    second = jnp.sum(jnp.where(expert == routes_ref[:, 1:2], logits, 0.0), axis=-1, keepdims=True)
    top = jnp.maximum(first, second)
    first, second = jnp.exp(first - top), jnp.exp(second - top)
    gates_ref[...] = jnp.concatenate([first / (first + second), second / (first + second)], axis=1)


def expert_kernel(slots, chunk, fresh, me_ref, *refs):
    refs = list(refs)
    take = lambda n: [refs.pop(0) for _ in range(n)]
    x_refs = take(len(chunk))
    g_all, router_ref, first_ref, second_ref = take(4)
    if not fresh:
        take(2)
    (out_all,) = take(1)
    dx_refs = take(len(chunk))
    if not fresh:
        take(1)
    rows_ref, grad_ref, act_ref, inner_ref, g_buf, out_buf, out_acc, dx_acc, sem = refs
    step = pl.program_id(0)
    total, width = rows_ref.shape
    rows = slots.block
    pieces = []
    for x_ref, dx_ref, array in zip(x_refs, dx_refs, chunk):
        for i, block in enumerate(array):
            pieces.append((block, x_ref, dx_ref, i * rows, len(pieces) * rows))

    def home(block):
        return pl.ds(pl.multiple_of(slots.expert_of(block, me_ref[0]) * rows, 16), rows)

    @pl.when(step == 0)
    def _():
        copies = [
            pltpu.make_async_copy(g_all.at[home(block), :], g_buf.at[pl.ds(first, rows), :], sem.at[i])
            for i, (block, _, _, _, first) in enumerate(pieces)
        ]
        for copy in copies:
            copy.start()
        out_acc[...] = jnp.zeros_like(out_acc)
        dx_acc[...] = jnp.zeros_like(dx_acc)
        for _, x_ref, _, inside, first in pieces:
            rows_ref[first:first + rows, :] = x_ref[inside:inside + rows, :]
        for copy in copies:
            copy.wait()
        for *_, first in pieces:
            at = slice(first, first + rows)
            grads = g_buf[at, :].astype(F32)
            other = jnp.sum(jnp.where(diagonal(rows), grads[rows - 1:, :rows], 0.0), axis=1, keepdims=True).astype(jnp.int32)
            logits = dot(rows_ref[at, :], router_ref[...], NN)
            expert = lax.broadcasted_iota(jnp.int32, logits.shape, 1)
            mine = jnp.sum(jnp.where(expert == me_ref[0], logits, 0.0), axis=-1, keepdims=True)
            its = jnp.sum(jnp.where(expert == other, logits, 0.0), axis=-1, keepdims=True)
            top = jnp.maximum(mine, its)
            mine, its = jnp.exp(mine - top), jnp.exp(its - top)
            line = lax.broadcasted_iota(jnp.int32, grads.shape, 0)
            grad_ref[at, :] = jnp.where(line < rows - SPARE, mine / (mine + its) * grads, 0.0).astype(BF16)

    parts = 1
    while total // parts > 512 or total % parts or (total // parts) % 16:
        parts += 1
    part = total // parts
    for i in range(parts):
        at = slice(i * part, (i + 1) * part)
        first_w, second_w = first_ref[...], second_ref[...]
        value = dot(rows_ref[at, :], first_w, NN)
        grad_act = dot(grad_ref[at, :], second_w, NT)
        square = value * value
        half = 0.5 * value
        scale = 0.7978845608028654
        th = jnp.tanh(value * (scale + (scale * 0.044715) * square))
        act = (half + half * th).astype(BF16)
        slope = 0.5 + 0.5 * th + (half * (1.0 - th * th)) * (scale + (3 * scale * 0.044715) * square)
        inner = (grad_act * slope).astype(BF16)
        act_ref[at, :] = act
        inner_ref[at, :] = inner
        out_acc[at, :] += dot(act, second_w, NN)
        dx_acc[at, :] += dot(inner, first_w, NT)

    @pl.when(step == pl.num_programs(0) - 1)
    def _():
        out_buf[...] = out_acc[...].astype(BF16)
        copies = [
            pltpu.make_async_copy(out_buf.at[pl.ds(first, rows), :], out_all.at[home(block), :], sem.at[i])
            for i, (block, _, _, _, first) in enumerate(pieces)
        ]
        for copy in copies:
            copy.start()
        for _, _, dx_ref, inside, first in pieces:
            at = slice(first, first + rows)
            gates = jnp.sum(out_buf[at, :].astype(F32) * g_buf[at, :].astype(F32), axis=1, keepdims=True)
            gates = jnp.sum(jnp.where(diagonal(rows), gates, 0.0), axis=0, keepdims=True)
            dx_ref[inside:inside + rows, :] = dx_acc[at, :].astype(BF16)
            tail = dx_acc[first + rows - 16:first + rows, :]
            line = lax.broadcasted_iota(jnp.int32, tail.shape, 0)
            for place in range(SPARE):
                piece = gates.astype(BF16).astype(F32)
                gates = gates - piece
                tail = jnp.where(line == 16 - SPARE + place, padded_row(piece, width), tail)
            dx_ref[inside + rows - 16:inside + rows, :] = tail.astype(BF16)
        for copy in copies:
            copy.wait()


def run_expert(slots, chunk, me, blocks, g_all, router, first_w, second_w, out_all, near):
    width, hidden = first_w.shape
    total = sum(block.shape[0] for block in blocks)
    block = hidden // 4
    whole = lambda a: pl.BlockSpec(a.shape, lambda i: (0, 0))
    column = pl.BlockSpec((total, block), lambda i: (0, i))
    rows = pl.BlockSpec((total, width), lambda i: (0, 0))
    fresh = out_all is None
    inputs = [me, *blocks, g_all, router, first_w, second_w] + ([] if fresh else [out_all, near])
    return pl.pallas_call(
        functools.partial(expert_kernel, slots, chunk, fresh),
        grid=(4,),
        in_specs=[SMEM]
        + [whole(b) for b in blocks]
        + [ANY, whole(router), pl.BlockSpec((width, block), lambda i: (0, i)), pl.BlockSpec((block, width), lambda i: (i, 0))]
        + ([] if fresh else [ANY, ANY]),
        out_specs=[ANY] + [whole(b) for b in blocks] + ([] if fresh else [ANY]) + [rows, rows, column, column],
        out_shape=arrays(
            (g_all.shape, BF16), *[(b.shape, BF16) for b in blocks], *([] if fresh else [(near.shape, BF16)]), *[((total, width), BF16)] * 2, *[((total, hidden), BF16)] * 2
        ),
        scratch_shapes=[
            pltpu.VMEM((total, width), BF16),
            pltpu.VMEM((total, width), BF16),
            pltpu.VMEM((total, width), F32),
            pltpu.VMEM((total, width), F32),
            pltpu.SemaphoreType.DMA((sum(len(array) for array in chunk),)),
        ],
        input_output_aliases={} if fresh else {len(inputs) - 2: 0, len(inputs) - 1: 1 + len(blocks)},
        compiler_params=params(dimension_semantics=("arbitrary",)),
        cost_estimate=SHORT,
    )(*inputs)


def first_grad_kernel(parts, *refs):
    out_ref = refs[-1]
    out_ref[...] = sum(dot(x[...], inner[...], TN) for x, inner in zip(refs[:parts], refs[parts:2 * parts])).astype(BF16)


def run_first_grad(rows, inners, more):
    width, hidden = rows[0].shape[1], inners[0].shape[1]
    block = hidden // 4
    total = sum(a.shape[0] for a in rows)
    return pl.pallas_call(
        functools.partial(first_grad_kernel, len(rows)),
        grid=(4,),
        in_specs=[pl.BlockSpec(a.shape, lambda i: (0, 0)) for a in rows]
        + [pl.BlockSpec((a.shape[0], block), lambda i: (0, i)) for a in inners],
        out_specs=pl.BlockSpec((width, block), lambda i: (0, i)),
        out_shape=jax.ShapeDtypeStruct((width, hidden + more), BF16),
        compiler_params=params(dimension_semantics=("arbitrary",)),
        cost_estimate=SHORT,
    )(*rows, *inners)


def run_second_grad(acts, grads):
    width, hidden = grads[0].shape[1], acts[0].shape[1]
    block = hidden // 4
    total = sum(a.shape[0] for a in acts)
    return pl.pallas_call(
        functools.partial(first_grad_kernel, len(acts)),
        grid=(4,),
        in_specs=[pl.BlockSpec((a.shape[0], block), lambda i: (0, i)) for a in acts]
        + [pl.BlockSpec(a.shape, lambda i: (0, 0)) for a in grads],
        out_specs=pl.BlockSpec((block, width), lambda i: (i, 0)),
        out_shape=jax.ShapeDtypeStruct((hidden, width), BF16),
        compiler_params=params(dimension_semantics=("arbitrary",)),
        cost_estimate=SHORT,
    )(*acts, *grads)


def gather_blocks(slots, refs, scratch):
    for array, ref in zip(slots.arrays, refs):
        scratch[array[0] * slots.block:(array[-1] + 1) * slots.block, :] = ref[...]


def back_kernel(slots, me_ref, *refs):
    refs_left = list(refs)
    take = lambda n: [refs_left.pop(0) for _ in range(n)]
    ret_refs = take(len(slots.arrays))
    places_ref, routes_ref, gates_ref, after_ref, gain_ref, router_ref, g_ref = take(7)
    (w_ref,) = take(1)
    grad_after_ref, branch_ref = take(2)
    mixed_refs = take(4)
    glogits_ref, ggain_ref, scratch = refs_left
    tokens = after_ref.shape[0]
    part = 128
    gather_blocks(slots, ret_refs, scratch)
    pieces = []
    for end in range(slots.block, scratch.shape[0] + 1, slots.block):
        tail = scratch[end - 16:end, :].astype(F32)[16 - SPARE:, :slots.block]
        pieces.append(jnp.sum(tail, axis=0, keepdims=True))
    gg = jnp.concatenate(pieces, axis=1)
    ggain_ref[...] = jnp.zeros_like(ggain_ref)

    def one(i, carry):
        at = pl.ds(pl.multiple_of(i * part, part), part)
        slot = lax.broadcasted_iota(jnp.int32, (part, gg.shape[1]), 1)
        hit0, hit1 = slot == places_ref[at, 0:1], slot == places_ref[at, 1:2]
        gg0 = jnp.sum(jnp.where(hit0, gg, 0.0), axis=-1, keepdims=True)
        gg1 = jnp.sum(jnp.where(hit1, gg, 0.0), axis=-1, keepdims=True)
        total = dot(jnp.where(hit0 | hit1, 1.0, 0.0).astype(BF16), scratch[...], NN)
        gate0, gate1 = gates_ref[at, 0:1], gates_ref[at, 1:2]
        mean = gate0 * gg0 + gate1 * gg1
        expert = lax.broadcasted_iota(jnp.int32, (part, router_ref.shape[1]), 1)
        glogits = jnp.where(expert == routes_ref[at, 0:1], gate0 * (gg0 - mean), 0.0) + jnp.where(
            expert == routes_ref[at, 1:2], gate1 * (gg1 - mean), 0.0
        )
        glogits = glogits.astype(BF16)
        glogits_ref[at, :] = glogits
        incoming = dot(glogits, router_ref[...], NT) + total
        unit, factor = rms_parts(after_ref[at, :])
        grad_after = g_ref[at, :].astype(F32) + rms_grad(incoming, gain_ref[...], unit, factor)
        ggain_ref[0:1, :] += jnp.sum(incoming * unit, axis=0, keepdims=True)
        grad_after_ref[at, :] = grad_after
        branch = grad_after.astype(BF16)
        branch_ref[at, :] = branch
        for rel, mixed_ref in enumerate(mixed_refs):
            mixed_ref[at, :] = dot(branch, w_ref[jnp.bitwise_xor(me_ref[0], rel)], NT).astype(BF16)
        return carry

    lax.fori_loop(0, tokens // part, one, 0)


def combine_kernel(slots, me_ref, ret_ref, places_ref, gates_ref, after_ref, out_ref, scratch):
    part = 128
    for block in range(slots.n_expert):
        first = pl.multiple_of(slots.expert_of(block, me_ref[0]) * slots.block, 16)
        scratch[block * slots.block:(block + 1) * slots.block, :] = ret_ref[pl.ds(first, slots.block), :]

    def one(i, carry):
        at = pl.ds(pl.multiple_of(i * part, part), part)
        total = after_ref[at, :]
        slot = lax.broadcasted_iota(jnp.int32, (part, scratch.shape[0]), 1)
        for j in range(2):
            hot = jnp.where(slot == places_ref[at, j:j + 1], 1.0, 0.0).astype(BF16)
            total = total + gates_ref[at, j:j + 1] * dot(hot, scratch[...], NN)
        out_ref[at, :] = total.astype(BF16)
        return carry

    lax.fori_loop(0, after_ref.shape[0] // part, one, 0)


def output_grad_kernel(me_ref, branch_ref, normed_ref, glogits_ref, ggain_ref, m0, m1, m2, m3, room_ref, out_ref, buf, sem):
    width = branch_ref.shape[1]
    for rel, m_ref in enumerate((m0, m1, m2, m3)):
        count = m_ref.shape[1]
        at = pl.ds(pl.multiple_of(jnp.bitwise_xor(me_ref[0], rel) * count, 16), count)
        buf[at, 0:width] = dot(m_ref[...], branch_ref[...], TN).astype(BF16)
    grad_router = dot(normed_ref[...], glogits_ref[...], TN)
    gain = jnp.transpose(jnp.concatenate([ggain_ref[...]] * 16, axis=0))[:, 0:1]
    blank = jnp.zeros((width, buf.shape[1] - width - grad_router.shape[1] - 1), F32)
    buf[:, width:] = jnp.concatenate([grad_router, gain, blank], axis=1).astype(BF16)
    hidden = out_ref.shape[1] - buf.shape[1]
    copy = pltpu.make_async_copy(buf, out_ref.at[:, hidden:], sem)
    copy.start()
    copy.wait()


def final_kernel(me_ref, x_ref, gain_ref, after_ref, d0, d1, d2, d3, w_ref, out_ref):
    grad = sum(
        dot(d_ref[...], w_ref[jnp.bitwise_xor(me_ref[0], rel)], NT) for rel, d_ref in enumerate((d0, d1, d2, d3))
    )
    unit, factor = rms_parts(x_ref[...].astype(F32))
    out_ref[...] = (after_ref[...] + rms_grad(grad, gain_ref[...], unit, factor)).astype(BF16)


def column_grad_kernel(order, heads, me_ref, bins_ref, n0, n1, n2, n3, d0, d1, d2, d3, out_ref, acc):
    acc[...] = sum(dot(n[...], d[...], TN) for n, d in ((n0, d0), (n1, d1), (n2, d2), (n3, d3)))
    cols = 3 * heads * DH
    lane = lax.broadcasted_iota(jnp.int32, (NB, acc.shape[1]), 1)
    table = jnp.zeros((NB, acc.shape[1]), F32)
    for h in range(heads):
        above = jnp.sum(bins_ref[:, h * SEG:(h + 1) * SEG], axis=1, keepdims=True)
        column = above - jnp.concatenate([above[1:], jnp.zeros((1, 1), F32)], axis=0)
        column = jnp.concatenate([column[:-1], -jnp.sum(column[:-1], axis=0, keepdims=True)], axis=0)
        table = jnp.where(lane == cols + h, column, table)
    group = acc.shape[0] // 4
    share = group // len(order)
    for i, rel in enumerate(order):
        first = jnp.bitwise_xor(me_ref[0], rel) * share
        block = [acc[pl.ds(pl.multiple_of(p * group + first, 8), share), :] for p in range(4)]
        block[0] = jnp.concatenate([block[0][:NB] + table, block[0][NB:]], axis=0)
        out_ref[i * 4 * share:(i + 1) * 4 * share, :] = jnp.concatenate(block, axis=0).astype(BF16)


def place_kernel(me_ref, wq_ref, wk_ref, wv_ref, *refs):
    *piece_refs, q_ref, k_ref, v_ref, more_ref, gain_ref = refs
    width = q_ref.shape[1]
    for rel, piece_ref in enumerate(piece_refs):
        count = piece_ref.shape[0]
        at = pl.ds(pl.multiple_of(jnp.bitwise_xor(me_ref[0], rel) * count, 8), count)
        piece = piece_ref[...].astype(F32)
        for c, out_ref in enumerate((q_ref, k_ref, v_ref)):
            out_ref[at, :] = piece[:, c * width:(c + 1) * width]
        more_ref[at, :] = piece[:, 3 * width:]
    total = sum(
        w_ref[...].astype(F32) * out_ref[...] for w_ref, out_ref in ((wq_ref, q_ref), (wk_ref, k_ref), (wv_ref, v_ref))
    )
    gain_ref[...] = jnp.sum(total, axis=1, keepdims=True)


def per_device(
    tokens, gain_attn, w_query, w_key, w_value, w_output, rel_table, gain_moe, router,
    w_in, w_out, routes, parents, cotangent,
):
    n_shard = lax.axis_size("shard")
    n_expert = lax.axis_size("expert")
    tok, width = tokens.shape
    tree_len = tok * n_shard
    n_experts = router.shape[1]
    heads = rel_table.shape[0]
    hw = heads * DH
    wide = -(-3 * hw // 128) * 128
    rows = width // n_shard
    slots = Slots(n_expert, max(2, tok * 20 // (7 * n_experts)))
    me_s, me_e = lax.axis_index("shard").astype(jnp.int32), lax.axis_index("expert").astype(jnp.int32)
    me_shard, me_expert = me_s.reshape(1), me_e.reshape(1)

    more = jnp.concatenate([gain_attn[:, None], gain_moe[:, None], router], axis=1)
    w_rel = pl.pallas_call(
        columns_kernel,
        in_specs=[SMEM] + [VMEM] * 4,
        out_specs=VMEM,
        out_shape=jax.ShapeDtypeStruct((n_shard, rows, -(-(3 * hw + 2 + n_experts) // 128) * 128), BF16),
        compiler_params=params(),
        cost_estimate=SHORT,
    )(me_shard, w_query, w_key, w_value, more)
    near_tokens, far_tokens = swap(tokens, "shard", 1), swap(tokens, "shard", 2)
    w_pieces = swap_all([w_rel[rel] for rel in range(n_shard)], "shard")

    expert_range = jnp.arange(n_experts, dtype=jnp.int32)
    flat_routes = routes.reshape(-1)
    expert_hot = (flat_routes[:, None] == expert_range[None, :]).astype(jnp.int32)
    earlier = jnp.cumsum(expert_hot, axis=0) - expert_hot
    rank = jnp.sum(earlier * expert_hot, axis=-1)
    places = (slots.block_of(flat_routes, me_e) * slots.block + rank).reshape(tok, 2)
    places_row = places.T
    others = jnp.repeat(routes.T[::-1], 8, axis=0).astype(BF16)
    block_shapes = [((len(array) * slots.block, width), BF16) for array in slots.arrays]

    sent_grads = pl.pallas_call(
        functools.partial(dispatch_kernel, slots),
        in_specs=[SMEM] + [VMEM] * 3 + [ANY],
        out_specs=VMEM,
        out_shape=jax.ShapeDtypeStruct((n_expert * slots.block, width), BF16),
        compiler_params=params(),
        cost_estimate=SHORT,
    )(me_expert, places_row, others, cotangent, w_rel)
    got_grads = over_experts(sent_grads)
    far_tokens, _ = lax.optimization_barrier((far_tokens, sent_grads))
    tree = [tokens, near_tokens, far_tokens, swap(far_tokens, "shard", 1)]

    *normed_one, queries, keys, values, keys_t, values_t, w_cols, bias, gain_one, gain_two, router_w = pl.pallas_call(
        functools.partial(project_kernel, heads),
        in_specs=[SMEM] * 2 + [VMEM] * 8 + [ANY],
        out_specs=[VMEM] * 14,
        out_shape=arrays(
            *[((tok, width), BF16)] * 4, *[((tree_len, HW), BF16)] * 3, *[((HW, tree_len), BF16)] * 2,
            ((width, wide), BF16), ((4, SEG, heads * SEG), F32), *[((1, width), F32)] * 2, ((width, n_experts), BF16),
        ),
        scratch_shapes=[pltpu.VMEM((width, 3 * HW + 128), BF16)],
        compiler_params=params(),
        cost_estimate=LONG,
    )(me_shard, rel_table.astype(F32), *w_pieces, *tree, sent_grads)
    parent_row = parents[0]
    *mixed, raw, lse = pl.pallas_call(
        functools.partial(attn_forward_kernel, heads),
        in_specs=[SMEM] * 2 + [VMEM] * 5,
        out_specs=[VMEM] * 6,
        out_shape=arrays(*[((tok, hw), BF16)] * 4, ((tree_len, HW), F32), ((SEGS * 8, heads * SEG), F32)),
        scratch_shapes=[pltpu.VMEM((tree_len, HW), BF16)],
        compiler_params=params(),
        cost_estimate=LONG,
    )(me_shard, parent_row, queries, keys, values, values_t, bias)
    mixed = swap_all(mixed, "shard")

    w_o = lax.all_gather(w_output, "shard", axis=0)
    after, normed_two, gates, *sent_rows = pl.pallas_call(
        functools.partial(post_kernel, slots),
        in_specs=[SMEM] + [VMEM] * 10 + [ANY],
        out_specs=[VMEM] * (3 + len(block_shapes)),
        out_shape=arrays(((tok, width), F32), ((tok, width), BF16), ((tok, 2), F32), *block_shapes),
        compiler_params=params(),
        cost_estimate=LONG,
    )(me_shard, tokens, gain_two, router_w, routes, places_row, *mixed, w_o, got_grads)
    sent_rows = slots.split(sent_rows)
    got_rows = [slots.exchange(c, blocks) for c, blocks in enumerate(sent_rows)]

    w_in, w_out, _ = lax.optimization_barrier((w_in, w_out, w_cols))
    first_w = lax.all_gather(w_in[0], "shard", axis=0, tiled=True)
    second_w = lax.all_gather(w_out[0], "shard", axis=0, tiled=True)
    out_all = near = None
    sent_dx, kept = [], []
    for c, chunk in enumerate(slots.chunks):
        n = len(chunk)
        out_all, *done = run_expert(
            slots, chunk, me_expert, got_rows[c], got_grads, router_w, first_w, second_w, out_all, near
        )
        sent_dx.append(done[:n])
        near = done[0] if c == 0 else done[n]
        kept.append(done[-4:])
    sent_dx[0] = [near]
    dx = [slots.exchange(c, blocks) for c, blocks in enumerate(sent_dx)]
    grad_first = run_first_grad([k[0] for k in kept], [k[3] for k in kept], width + 128)
    grad_second = run_second_grad([k[2] for k in kept], [k[1] for k in kept])

    dx = [block for blocks in dx for block in blocks]
    out_all, _ = lax.optimization_barrier((out_all, dx))
    returned = over_experts(out_all)
    dx, grad_first, grad_second = lax.optimization_barrier((dx, grad_first, grad_second))

    slot_rows = slots.n_expert * slots.block
    grad_after, branch, gm0, gm1, gm2, gm3, glogits, ggain_two = pl.pallas_call(
        functools.partial(back_kernel, slots),
        in_specs=[SMEM] + [VMEM] * (len(block_shapes) + 8),
        out_specs=[VMEM] * 8,
        out_shape=arrays(
            ((tok, width), F32), ((tok, width), BF16), *[((tok, hw), BF16)] * 4, ((tok, n_experts), BF16), ((8, width), F32)
        ),
        scratch_shapes=[pltpu.VMEM((slot_rows, width), BF16)],
        compiler_params=params(),
        cost_estimate=SHORT,
    )(me_shard, *dx, places, routes, gates, after, gain_two, router_w, cotangent, w_o)
    grad_mixed = swap_all([gm0, gm1, gm2, gm3], "shard")
    grad_first = pl.pallas_call(
        output_grad_kernel,
        in_specs=[SMEM] + [VMEM] * 8 + [ANY],
        out_specs=ANY,
        out_shape=jax.ShapeDtypeStruct(grad_first.shape, BF16),
        scratch_shapes=[pltpu.VMEM((width, width + 128), BF16), pltpu.SemaphoreType.DMA],
        input_output_aliases={9: 0},
        compiler_params=params(),
        cost_estimate=SHORT,
    )(me_shard, branch, normed_two, glogits, ggain_two, *mixed, grad_first)

    grad_w_out = lax.psum_scatter(grad_second, "shard", scatter_dimension=0, tiled=True)
    grad_mixed, grad_w_out = lax.optimization_barrier((grad_mixed, grad_w_out))
    *dqkv, bins = pl.pallas_call(
        functools.partial(attn_backward_kernel, heads),
        in_specs=[SMEM] * 2 + [VMEM] * 11,
        out_specs=[VMEM] * 5,
        out_shape=arrays(*[((tok, wide), BF16)] * 4, ((NB, heads * SEG), F32)),
        scratch_shapes=[
            pltpu.VMEM((tree_len, HW), BF16),
            pltpu.VMEM((tree_len, HW), BF16),
            pltpu.VMEM((tree_len, HW), F32),
            pltpu.VMEM((tree_len, HW), F32),
            pltpu.VMEM((2, SEG, heads * SEG), F32),
        ],
        compiler_params=params(),
        cost_estimate=SHORT,
    )(me_shard, parent_row, queries, keys, values, keys_t, raw, lse, *grad_mixed, bias)
    dqkv_own = swap_all(dqkv, "shard")

    hidden = w_in.shape[2]
    grad_w_out = grad_w_out.astype(F32)[None]
    grad_first = lax.psum_scatter(grad_first, "shard", scatter_dimension=0, tiled=True)
    grad_w_in = grad_first[:, :hidden].astype(F32)[None]
    grad_wo = grad_first[:, hidden:]
    output = pl.pallas_call(
        functools.partial(combine_kernel, slots),
        in_specs=[SMEM] + [VMEM] * 4,
        out_specs=VMEM,
        out_shape=jax.ShapeDtypeStruct((tok, width), BF16),
        scratch_shapes=[pltpu.VMEM((slot_rows, width), BF16)],
        compiler_params=params(),
        cost_estimate=SHORT,
    )(me_expert, returned, places, gates, after)

    w_cols, _ = lax.optimization_barrier((w_cols, after))
    w_all = lax.all_gather(w_cols, "shard", axis=0)
    grad_tokens = pl.pallas_call(
        final_kernel,
        in_specs=[SMEM] + [VMEM] * 8,
        out_specs=VMEM,
        out_shape=jax.ShapeDtypeStruct((tok, width), BF16),
        compiler_params=params(),
        cost_estimate=SHORT,
    )(me_shard, tokens, gain_one, grad_after, *dqkv_own, w_all)

    halving = [bit for bit in (1, 2, 4) if bit < n_expert] if n_expert <= 8 else []
    rels = [0]
    for bit in reversed(halving):
        rels = rels + [rel | bit for rel in rels]
    cols = pl.pallas_call(
        functools.partial(column_grad_kernel, rels, heads),
        in_specs=[SMEM] + [VMEM] * 9,
        out_specs=VMEM,
        out_shape=jax.ShapeDtypeStruct((width, wide), BF16),
        scratch_shapes=[pltpu.VMEM((width, wide), F32)],
        compiler_params=params(),
        cost_estimate=SHORT,
    )(me_expert if halving else jnp.zeros((1,), jnp.int32), bins, *normed_one, *dqkv)
    for bit in halving:
        kept_half, sent_half = jnp.split(cols, 2, axis=0)
        cols = (kept_half.astype(F32) + swap(sent_half, "expert", bit).astype(F32)).astype(BF16)
    if halving:
        grad_wo = grad_wo.reshape(n_expert, rows // n_expert, -1)
        grad_wo = reorder([grad_wo[e] for e in range(n_expert)], me_e)
        grad_wo = jnp.concatenate([grad_wo[rel] for rel in rels], axis=0)
        for bit in halving:
            kept_half, sent_half = jnp.split(grad_wo, 2, axis=0)
            grad_wo = (kept_half.astype(F32) + swap(sent_half, "expert", bit).astype(F32)).astype(BF16)
    else:
        cols, grad_wo = lax.psum((cols.astype(F32), grad_wo.astype(F32)), "expert")
        grad_wo = grad_wo.astype(BF16)
    table = cols[:NB, 3 * hw:3 * hw + heads].astype(F32).T
    share = cols.shape[0] // n_shard
    cols = cols.astype(BF16)[:, :3 * hw].reshape(n_shard, share, 3 * hw)
    cols = reorder([cols[p] for p in range(n_shard)], me_s)
    cols = reorder(swap_all(cols, "shard"), me_s)
    cols = jnp.concatenate([c[:, i * hw:(i + 1) * hw] for i in range(3) for c in cols], axis=1)
    cols = jnp.concatenate([cols, grad_wo], axis=1)
    pieces = swap_all([cols] * n_expert, "expert") if halving else [cols]
    pieces, output, grad_w_in, grad_w_out = lax.optimization_barrier((pieces, output, grad_w_in, grad_w_out))
    grad_q, grad_k, grad_v, grad_wo, grad_gain_one = pl.pallas_call(
        place_kernel,
        in_specs=[SMEM] + [VMEM] * (3 + len(pieces)),
        out_specs=[VMEM] * 5,
        out_shape=arrays(*[((rows, width), F32)] * 3, ((rows, width + 128), F32), ((rows, 1), F32)),
        compiler_params=params(),
        cost_estimate=SHORT,
    )(me_expert if halving else jnp.zeros((1,), jnp.int32), w_query, w_key, w_value, *pieces)
    grad_gain_one = grad_gain_one[:, 0] / gain_attn.astype(F32)

    return (
        output, grad_tokens, grad_gain_one, grad_q, grad_k, grad_v, grad_wo[:, :width],
        table, grad_wo[:, width + n_experts], grad_wo[:, width:width + n_experts], grad_w_in, grad_w_out,
    )


def solution(mesh):
    both, shard = P(("expert", "shard"), None), P("shard", None)
    three = P("expert", "shard", None)
    return jax.shard_map(
        per_device,
        mesh=mesh,
        in_specs=(
            both, P("shard"), shard, shard, shard, shard, shard, P("shard"), shard, three, three, both,
            P("expert", None), both,
        ),
        out_specs=(both, both, P("shard"), shard, shard, shard, shard, shard, P("shard"), shard, three, three),
        check_vma=False,
    )
```

time: 931 us -> 567 us (0.61)
  blocking collectives: 230 us -> 0 us
  local copies, waits for them, and re-layouts: 152 us -> 20.9 us
  waiting for transfers between devices: 98.5 us -> 216 us
  matrix products: 67.3 us -> 0 us
  other arithmetic: 48.4 us -> 12 us
    ppermute x0 -> x39, waiting for transfers between devices: none -> 184 us  [swap(): lax.ppermute(block, axis, [(i, i ^ rel) for i in range(lax.axis_size(axis...]
    all_to_all x4 -> x0, blocking collectives: 106 us -> none  [the longest x3 84.1 us: over_experts(): lax.all_to_all(array, 'expert', split_axis=0, concat_axis=0, tiled=True)]
    broadcast_in_dim x66 -> x2, local copies, waits for them, and re-layouts: 92.1 us -> 0.01 us  [the longest x1 0.01 us: per_device(): gain_moe[:, None]]
    psum x2 -> x0, blocking collectives: 84 us -> none  [the longest x1 46.9 us: per_device(): grad_w_o = lax.psum(grad_w_o, 'expert')]
    all_to_all x14 -> x4, waiting for transfers between devices: 95.8 us -> 27.3 us  [the longest x2 27.3 us: exchange(): lax.all_to_all(blocks[0], 'expert', split_axis=0, concat_axis=0, tiled=Tr...]
    dot_general x14 -> x0, matrix products: 67.3 us -> none  [the longest x4 36.6 us: weight_grad(): lax.dot_general(a, b, (((0,), (0,)), ((), ())), preferred_element_type=F32)]
    ppermute x0 -> x39, starting transfers between devices: none -> 51.6 us  [swap(): lax.ppermute(block, axis, [(i, i ^ rel) for i in range(lax.axis_size(axis...]
    all_to_all x14 -> x4, starting transfers between devices: 68.2 us -> 17.9 us  [the longest x2 9.86 us: over_experts(): lax.all_to_all(block, 'expert', split_axis=0, concat_axis=0, tiled=True)]
  transfers between devices with their start and end apart: 22 -> 49, of which waited for: 5 -> 20; matrix products, arithmetic and copies ran while one was open for 28% -> 3% of each run, Pallas kernels for 24% -> 37%
where the time goes in v2:
time: 567 us; the launch traced here: 560 us
  Pallas kernels  226 us (40%)
  waiting for transfers between devices  216 us (38%)
  starting transfers between devices  69.9 us (12%)
  local copies, waits for them, and re-layouts  20.9 us (4%)
  between operations  15.2 us (3%)
  other arithmetic  12 us (2%)
    ppermute x39, waiting for transfers between devices, swap(): lax.ppermute(block, axis, [(i, i ^ rel) for i in range(lax.axis_size(axis...  184 us
    pallas_call x3, Pallas kernels, run_expert(): pl.pallas_call(functools.partial(expert_kernel, slots, chunk, fresh), gri...  65.5 us
    ppermute x39, starting transfers between devices, swap(): lax.ppermute(block, axis, [(i, i ^ rel) for i in range(lax.axis_size(axis...  51.6 us
    pallas_call x1, Pallas kernels, per_device(): pl.pallas_call(functools.partial(attn_backward_kernel, heads), in_specs=[...  32.9 us
    all_to_all x2, waiting for transfers between devices, exchange(): lax.all_to_all(blocks[0], 'expert', split_axis=0, concat_axis=0, tiled=Tr...  27.3 us
    pallas_call x1, Pallas kernels, per_device(): pl.pallas_call(functools.partial(attn_forward_kernel, heads), in_specs=[S...  20.7 us
    pallas_call x1, Pallas kernels, per_device(): pl.pallas_call(functools.partial(back_kernel, slots), in_specs=[SMEM] + [...  15 us
    pallas_call x1, Pallas kernels, run_first_grad(): pl.pallas_call(functools.partial(first_grad_kernel, len(rows)), grid=(4,)...  14.8 us
  transfers between devices with their start and end apart: 49, of which 20 were waited for; matrix products, arithmetic and copies ran while one was open for 3% of the time, Pallas kernels for 37%

profile of v2, /device:TPU:0, one launch (start us, length us, event | category | flops | bytes accessed | tf_op | source)
XLA Modules:
  0.0 559.5 jit_solution(16876156310519440470)
XLA Ops:
  19.4 8.3 %shard_map.230.before_ref = bf16[1920,768]{1,0:T(8,128)(2,1)} custom-call(s32[1]{0:T(128)} %bitcast.me_ref, s32[2,640]{1,0:T(2,128)} %copy.75.places_ref, bf16[16,640]{1,0:T(8,128)(2,1)} %broadcast_bitcast_fusion.others_ref, bf16[640,768]{1,0:T(8,128)(2,1)} %refs_11_.1, bf16[4,192,640]{2,1,0:T(8,128)(2,1)} %shard_map.229.refs_0_), custom_call_target="tpu_custom_call" | custom-call | bytes 1024 | tf_op jit(solution)/shard_map/pallas_call | solution.py:793
  47.0 10.5 %shard_map.231 = (bf16[640,768]{1,0:T(8,128)(2,1)}, bf16[640,768]{1,0:T(8,128)(2,1)}, bf16[640,768]{1,0:T(8,128)(2,1)}, bf16[640,768]{1,0:T(8,128)(2,1)}, bf16[2...) custom-call(s32[1]{0:T(128)} %bitcast.1.me_ref, ...), custom_call_target="tpu_custom_call" | custom-call | flops 1099511627776 | bytes 4294967296 | tf_op jit(solution)/shard_map/pallas_call | solution.py:805
  57.9 20.7 %shard_map.232 = (bf16[640,192]{1,0:T(8,128)(2,1)}, bf16[640,192]{1,0:T(8,128)(2,1)}, bf16[640,192]{1,0:T(8,128)(2,1)}, bf16[640,192]{1,0:T(8,128)(2,1)}, f32[2560,256]{1,0:T(8,128)}, /*index=5*/f32[160,384]{1,0:T(8,128)}) custom-call(s32[1]{0:T(128)} %bitcast.1.me_ref, s32[20]{0:T(128)} %bitcast.74, bf16[2560,256]{1,0:T(8,128)(2,1)} %get-tuple-element.109.q_ref, ...), custom_call_target="tpu_custom_call" | custom-call | flops 1099511627776 | bytes 4294967296 | tf_op jit(solution)/shard_map/pallas_call | solution.py:818
  81.3 16.0 %collective-permute-done.7.m2 = bf16[640,192]{1,0:T(8,128)(2,1)S(1)} collective-permute-done((bf16[640,192]{1,0:T(8,128)(2,1)}, bf16[640,192]{1,0:T(8,128)(2,1)S(1)}, u32[]{:S(2)}, u32[]{:S(2)}) %collective-permute-start.7) | collective-permute-done | bytes 245792 | tf_op jit(solution)/shard_map/ppermute | solution.py:377
  97.2 13.1 %collective-permute-done.8.m3 = bf16[640,192]{1,0:T(8,128)(2,1)S(1)} collective-permute-done((bf16[640,192]{1,0:T(8,128)(2,1)}, bf16[640,192]{1,0:T(8,128)(2,1)S(1)}, u32[]{:S(2)}, u32[]{:S(2)}) %collective-permute-start.8) | collective-permute-done | bytes 245792 | tf_op jit(solution)/shard_map/ppermute | solution.py:377
  130.5 27.3 %all-to-all-done.1 = bf16[4,240,768]{2,1,0:T(8,128)(2,1)S(1)} async-done(((bf16[4,240,768]{2,1,0:T(8,128)(2,1)}), bf16[4,240,768]{2,1,0:T(8,128)(2,1)S(1)}, u32[]{:S(2)}, u32[]{:S(2)}) %all-to-all-start.1) | async-done | bytes 1474592 | tf_op jit(solution)/shard_map/all_to_all | solution.py:362
  158.9 30.4 %shard_map.234 = (bf16[1920,768]{1,0:T(8,128)(2,1)}, bf16[960,768]{1,0:T(8,128)(2,1)}, bf16[960,768]{1,0:T(8,128)(2,1)}, bf16[960,768]{1,0:T(8,128)(2,1)}, bf16[...) custom-call(s32[1]{0:T(128)} %bitcast.me_ref, bf16[960,768]{1,0:T(8,128)(2,1)} %bitcast.66, ...), custom_call_target="tpu_custom_call" | custom-call | bytes 1024 | tf_op jit(solution)/shard_map/pallas_call | solution.py:562
  190.2 17.5 %shard_map.235 = (bf16[1920,768]{1,0:T(8,128)(2,1)}, bf16[240,768]{1,0:T(8,128)(2,1)}, bf16[240,768]{1,0:T(8,128)(2,1)}, bf16[960,768]{1,0:T(8,128)(2,1)}, bf16[...) custom-call(s32[1]{0:T(128)} %bitcast.me_ref, ...), custom_call_target="tpu_custom_call", output_to_operand_aliasing={{0}: (7, {}), {3}: (8, {})} | custom-call | bytes 1024 | tf_op jit(solution)/shard_map/pallas_call | solution.py:562
  208.5 17.7 %shard_map.236 = (bf16[1920,768]{1,0:T(8,128)(2,1)}, bf16[240,768]{1,0:T(8,128)(2,1)}, bf16[240,768]{1,0:T(8,128)(2,1)}, bf16[960,768]{1,0:T(8,128)(2,1)}, bf16[...) custom-call(s32[1]{0:T(128)} %bitcast.me_ref, ...), custom_call_target="tpu_custom_call", output_to_operand_aliasing={{0}: (7, {}), {3}: (8, {})} | custom-call | bytes 1024 | tf_op jit(solution)/shard_map/pallas_call | solution.py:562
  237.7 14.8 %shard_map.238 = bf16[3072,768]{1,0:T(8,128)(2,1)} custom-call(bf16[960,3072]{1,0:T(8,128)(2,1)} %get-tuple-element.146.refs_0_, bf16[480,3072]{1,0:T(8,128)(2,1)} %get-tuple-element.147.refs_1_, bf16[480,3072]{1,0:T(8,128)(2,1)} %get-tuple-element.148.refs_2_, bf16[960,768]{1,0:T(8,128)(2,1)} %get-tuple-element.149.refs_3_, ...), custom_call_target="tpu_custom_call" | custom-call | bytes 1024 | tf_op jit(solution)/shard_map/pallas_call | solution.py:611
  252.5 14.8 %shard_map.237.room_ref = bf16[768,3968]{1,0:T(8,128)(2,1)} custom-call(bf16[960,768]{1,0:T(8,128)(2,1)} %get-tuple-element.140.refs_0_, bf16[480,768]{1,0:T(8,128)(2,1)} %get-tuple-element.141.refs_1_, bf16[480,768]{1,0:T(8,128)(2,1)} %get-tuple-element.142.refs_2_, bf16[960,3072]{1,0:T(8,128)(2,1)} %get-tuple-element.143.refs_3_, ...), custom_call_target="tpu_custom_call" | custom-call | bytes 1024 | tf_op jit(solution)/shard_map/pallas_call | solution.py:595
  267.3 23.2 %collective-permute-done.13.refs_1_ = bf16[240,768]{1,0:T(8,128)(2,1)S(1)} collective-permute-done((bf16[240,768]{1,0:T(8,128)(2,1)}, bf16[240,768]{1,0:T(8,128)(2,1)S(1)}, u32[]{:S(2)}, u32[]{:S(2)}) %collective-permute-start.13) | collective-permute-done | bytes 368672 | tf_op jit(solution)/shard_map/ppermute | solution.py:377
  290.5 7.4 %collective-permute-done.14.refs_2_ = bf16[240,768]{1,0:T(8,128)(2,1)S(1)} collective-permute-done((bf16[240,768]{1,0:T(8,128)(2,1)S(1)}, bf16[240,768]{1,0:T(8,128)(2,1)S(1)}, u32[]{:S(2)}, u32[]{:S(2)}) %collective-permute-start.14) | collective-permute-done | bytes 368672 | tf_op jit(solution)/shard_map/ppermute | solution.py:377
  299.8 15.0 %shard_map.239 = (f32[640,768]{1,0:T(8,128)}, bf16[640,768]{1,0:T(8,128)(2,1)}, bf16[640,192]{1,0:T(8,128)(2,1)}, bf16[640,192]{1,0:T(8,128)(2,1)}, bf16[640,192...) custom-call(s32[1]{0:T(128)} %bitcast.1.me_ref, ...), custom_call_target="tpu_custom_call" | custom-call | bytes 1024 | tf_op jit(solution)/shard_map/pallas_call | solution.py:865
  325.7 16.0 %collective-permute-done.18.g2 = bf16[640,192]{1,0:T(8,128)(2,1)} collective-permute-done((bf16[640,192]{1,0:T(8,128)(2,1)}, bf16[640,192]{1,0:T(8,128)(2,1)}, u32[]{:S(2)}, u32[]{:S(2)}) %collective-permute-start.18) | collective-permute-done | bytes 245792 | tf_op jit(solution)/shard_map/ppermute | solution.py:377
  341.7 13.4 %collective-permute-done.19.g3_ref = bf16[640,192]{1,0:T(8,128)(2,1)} collective-permute-done((bf16[640,192]{1,0:T(8,128)(2,1)}, bf16[640,192]{1,0:T(8,128)(2,1)}, u32[]{:S(2)}, u32[]{:S(2)}) %collective-permute-start.19) | collective-permute-done | bytes 245792 | tf_op jit(solution)/shard_map/ppermute | solution.py:377
  358.1 32.9 %shard_map.240 = (bf16[640,640]{1,0:T(8,128)(2,1)}, bf16[640,640]{1,0:T(8,128)(2,1)}, bf16[640,640]{1,0:T(8,128)(2,1)}, bf16[640,640]{1,0:T(8,128)(2,1)}, f32[16,384]{1,0:T(8,128)}) custom-call(s32[1]{0:T(128)} %bitcast.1.me_ref, s32[20]{0:T(128)} %bitcast.75, bf16[2560,256]{1,0:T(8,128)(2,1)} %get-tuple-element.109.q_ref, ...), custom_call_target="tpu_custom_call" | custom-call | bytes 1024 | tf_op jit(solution)/shard_map/pallas_call | solution.py:890
  391.0 7.8 %shard_map.241 = bf16[768,640]{1,0:T(8,128)(2,1)} custom-call(s32[1]{0:T(128)} %bitcast.me_ref, f32[16,384]{1,0:T(8,128)} %get-tuple-element.168.bins_ref, bf16[640,768]{1,0:T(8,128)(2,1)} %get-tuple-element.169.n0, bf16[640,768]{1,0:T(8,128)(2,1)} %get-tuple-element.170.n1, bf16[640,768]{1,0:T(8,128)(2,1)} %get-tuple-element.171.n2, ...), custom_call_target="tpu_custom_call" | custom-call | bytes 1024 | tf_op jit(solution)/shard_map/pallas_call | solution.py:937
  401.5 11.5 %collective-permute-done.20 = bf16[384,640]{1,0:T(8,128)(2,1)S(1)} collective-permute-done((bf16[384,640]{1,0:T(8,128)(2,1)S(1)}, bf16[384,640]{1,0:T(8,128)(2,1)S(1)}, u32[]{:S(2)}, u32[]{:S(2)}) %collective-permute-start.20) | collective-permute-done | bytes 491552 | tf_op jit(solution)/shard_map/ppermute | solution.py:377
  425.3 9.0 %shard_map.243 = bf16[640,768]{1,0:T(8,128)(2,1)} custom-call(s32[1]{0:T(128)} %bitcast.me_ref, bf16[1920,768]{1,0:T(8,128)(2,1)} %bitcast.64, s32[640,2]{1,0:T(8,128)} %copy-done.5, f32[640,2]{1,0:T(8,128)} %get-tuple-element.157.refs_7_.gates_ref, f32[640,768]{1,0:T(8,128)} %get-tuple-element.158.refs_8_.after_ref), custom_call_target="tpu_custom_call" | custom-call | bytes 1024 | tf_op jit(solution)/shard_map/pallas_call | solution.py:912
  441.1 21.4 %collective-permute-done.37.d2 = bf16[640,640]{1,0:T(8,128)(2,1)} collective-permute-done((bf16[640,640]{1,0:T(8,128)(2,1)}, bf16[640,640]{1,0:T(8,128)(2,1)}, u32[]{:S(2)}, u32[]{:S(2)}) %collective-permute-start.37) | collective-permute-done | bytes 819232 | tf_op jit(solution)/shard_map/ppermute | solution.py:377
  462.6 22.3 %collective-permute-done.38.d3 = bf16[640,640]{1,0:T(8,128)(2,1)} collective-permute-done((bf16[640,640]{1,0:T(8,128)(2,1)}, bf16[640,640]{1,0:T(8,128)(2,1)}, u32[]{:S(2)}, u32[]{:S(2)}) %collective-permute-start.38) | collective-permute-done | bytes 819232 | tf_op jit(solution)/shard_map/ppermute | solution.py:377
  484.8 8.6 %shard_map.244 = bf16[640,768]{1,0:T(8,128)(2,1)} custom-call(s32[1]{0:T(128)} %bitcast.1.me_ref, bf16[640,768]{1,0:T(8,128)(2,1)} %x_ref.3, f32[1,768]{1,0:T(1,128)} %get-tuple-element.186.gain_ref, f32[640,768]{1,0:T(8,128)} %get-tuple-element.187.after_ref, bf16[640,640]{1,0:T(8,128)(2,1)} %get-tuple-element.173.d0, ...), custom_call_target="tpu_custom_call" | custom-call | bytes 1024 | tf_op jit(solution)/shard_map/pallas_call | solution.py:924
  526.0 10.8 %collective-permute-done.32.refs_4_ = bf16[24,3200]{1,0:T(8,128)(2,1)S(1)} collective-permute-done((bf16[24,3200]{1,0:T(8,128)(2,1)S(1)}, bf16[24,3200]{1,0:T(8,128)(2,1)S(1)}, u32[]{:S(2)}, u32[]{:S(2)}) %collective-permute-start.32) | collective-permute-done | bytes 153632 | tf_op jit(solution)/shard_map/ppermute | solution.py:377
  (226 shorter events, 154.0 us)
Async XLA Ops:
  10.2 35.9 %collective-permute-start.3 = (bf16[640,768]{1,0:T(8,128)(2,1)}, bf16[640,768]{1,0:T(8,128)(2,1)S(1)}, u32[]{:S(2)}, u32[]{:S(2)}) collective-permute-start(bf16[640,768]{1,0:T(8,128)(2,1)} %x_ref.3), channel_id=1, source_target_pairs={{0,1},{1,0},{2,3},{3,2},{4,5},{5,4},{6,7},{7,6},{8,9},{9,8},{10,11... | collective-permute-start | bytes 2949128 | tf_op jit(solution)/shard_map/ppermute | solution.py:377
  35.2 75.1 %all-to-all-start = ((bf16[8,240,768]{2,1,0:T(8,128)(2,1)}), bf16[8,240,768]{2,1,0:T(8,128)(2,1)}, u32[]{:S(2)}, u32[]{:S(2)}) async-start(bf16[8,240,768]{2,1,0:T(8,128)(2,1)} %bitcast.63), calls=%async_computation | async-start | bytes 5898240 | tf_op jit(solution)/shard_map/all_to_all | solution.py:371
  41.2 40.0 %all-gather.9.cloned.1.call-start = ((), (), s32[]{:S(2)}) async-start(), calls=%async_computation.8 | async-start | bytes 1474560 | tf_op jit(solution)/shard_map/all_gather | solution.py:829
  42.0 115.9 %all-gather.11.cloned.1.call-start = ((), (), s32[]{:S(2)}) async-start(), calls=%async_computation.9 | async-start | bytes 5898240 | tf_op jit(solution)/shard_map/all_gather | solution.py:842
  57.6 100.2 %all-gather.13.cloned.1.call-start = ((), (), s32[]{:S(2)}) async-start(), calls=%async_computation.10 | async-start | bytes 5898240 | tf_op jit(solution)/shard_map/all_gather | solution.py:843
  118.3 39.5 %all-to-all-start.1 = ((bf16[4,240,768]{2,1,0:T(8,128)(2,1)}), bf16[4,240,768]{2,1,0:T(8,128)(2,1)S(1)}, u32[]{:S(2)}, u32[]{:S(2)}) async-start(bf16[4,240,768]{2,1,0:T(8,128)(2,1)} %bitcast.69), calls=%async_computation.1 | async-start | bytes 2949120 | tf_op jit(solution)/shard_map/all_to_all | solution.py:362
  122.6 66.7 %collective-permute-start.11 = (bf16[240,768]{1,0:T(8,128)(2,1)}, bf16[240,768]{1,0:T(8,128)(2,1)S(1)}, u32[]{:S(2)}, u32[]{:S(2)}) collective-permute-start(bf16[240,768]{1,0:T(8,128)(2,1)} %get-tuple-element.128), channel_id=1, source_target_pairs={{0,16},{4,20},{8,24},{12,28},{16,0},{20,4},{24,8},{28,12},{1,17},{... | collective-permute-start | bytes 1105928 | tf_op jit(solution)/shard_map/ppermute | solution.py:377
  125.3 64.1 %collective-permute-start.12 = (bf16[240,768]{1,0:T(8,128)(2,1)}, bf16[240,768]{1,0:T(8,128)(2,1)S(1)}, u32[]{:S(2)}, u32[]{:S(2)}) collective-permute-start(bf16[240,768]{1,0:T(8,128)(2,1)} %get-tuple-element.129), channel_id=1, source_target_pairs={{0,20},{4,16},{8,28},{12,24},{16,4},{20,0},{24,12},{28,8},{1,21},{... | collective-permute-start | bytes 1105928 | tf_op jit(solution)/shard_map/ppermute | solution.py:377
  127.1 80.6 %collective-permute-start.10 = (bf16[240,768]{1,0:T(8,128)(2,1)}, bf16[240,768]{1,0:T(8,128)(2,1)S(1)}, u32[]{:S(2)}, u32[]{:S(2)}) collective-permute-start(bf16[240,768]{1,0:T(8,128)(2,1)} %get-tuple-element.124), channel_id=1, source_target_pairs={{0,28},{4,24},{8,20},{12,16},{16,12},{20,8},{24,4},{28,0},{1,29},{... | collective-permute-start | bytes 1105928 | tf_op jit(solution)/shard_map/ppermute | solution.py:377
  130.5 77.1 %collective-permute-start.9 = (bf16[240,768]{1,0:T(8,128)(2,1)S(1)}, bf16[240,768]{1,0:T(8,128)(2,1)S(1)}, u32[]{:S(2)}, u32[]{:S(2)}) collective-permute-start(bf16[240,768]{1,0:T(8,128)(2,1)S(1)} %copy-done.35), channel_id=1, source_target_pairs={{0,24},{4,28},{8,16},{12,20},{16,8},{20,12},{24,0},{28,4},{1,25},{... | collective-permute-start | bytes 1105928 | tf_op jit(solution)/shard_map/ppermute | solution.py:377
  226.2 71.7 %all-to-all-start.2 = ((bf16[4,240,768]{2,1,0:T(8,128)(2,1)}), bf16[4,240,768]{2,1,0:T(8,128)(2,1)S(1)}, u32[]{:S(2)}, u32[]{:S(2)}) async-start(bf16[4,240,768]{2,1,0:T(8,128)(2,1)} %bitcast.62), calls=%async_computation.2 | async-start | bytes 2949120 | tf_op jit(solution)/shard_map/all_to_all | solution.py:362
  229.9 128.2 %reduce-scatter.3.cloned.1.call-start = ((), (), s32[]{:S(2)}) async-start(), calls=%async_computation.6 | async-start | bytes 5898240 | tf_op jit(solution)/shard_map/reduce_scatter | solution.py:888
  230.0 37.3 %collective-permute-start.15 = (bf16[240,768]{1,0:T(8,128)(2,1)}, bf16[240,768]{1,0:T(8,128)(2,1)S(1)}, u32[]{:S(2)}, u32[]{:S(2)}) collective-permute-start(bf16[240,768]{1,0:T(8,128)(2,1)} %get-tuple-element.138), channel_id=1, source_target_pairs={{0,24},{4,28},{8,16},{12,20},{16,8},{20,12},{24,0},{28,4},{1,25},{... | collective-permute-start | bytes 1105928 | tf_op jit(solution)/shard_map/ppermute | solution.py:377
  230.9 36.3 %collective-permute-start.16 = (bf16[240,768]{1,0:T(8,128)(2,1)}, bf16[240,768]{1,0:T(8,128)(2,1)S(1)}, u32[]{:S(2)}, u32[]{:S(2)}) collective-permute-start(bf16[240,768]{1,0:T(8,128)(2,1)} %get-tuple-element.139), channel_id=1, source_target_pairs={{0,28},{4,24},{8,20},{12,16},{16,12},{20,8},{24,4},{28,0},{1,29},{... | collective-permute-start | bytes 1105928 | tf_op jit(solution)/shard_map/ppermute | solution.py:377
  235.2 55.3 %collective-permute-start.13 = (bf16[240,768]{1,0:T(8,128)(2,1)}, bf16[240,768]{1,0:T(8,128)(2,1)S(1)}, u32[]{:S(2)}, u32[]{:S(2)}) collective-permute-start(bf16[240,768]{1,0:T(8,128)(2,1)} %get-tuple-element.136), channel_id=1, source_target_pairs={{0,16},{4,20},{8,24},{12,28},{16,0},{20,4},{24,8},{28,12},{1,17},{... | collective-permute-start | bytes 1105928 | tf_op jit(solution)/shard_map/ppermute | solution.py:377
  235.2 62.7 %collective-permute-start.14 = (bf16[240,768]{1,0:T(8,128)(2,1)S(1)}, bf16[240,768]{1,0:T(8,128)(2,1)S(1)}, u32[]{:S(2)}, u32[]{:S(2)}) collective-permute-start(bf16[240,768]{1,0:T(8,128)(2,1)S(1)} %copy-done.34), channel_id=1, source_target_pairs={{0,20},{4,16},{8,28},{12,24},{16,4},{20,0},{24,12},{28,8},{1,21},{... | collective-permute-start | bytes 1105928 | tf_op jit(solution)/shard_map/ppermute | solution.py:377
  299.2 141.9 %all-gather.15.cloned.1.call-start = ((), (), s32[]{:S(2)}) async-start(), calls=%async_computation.11 | async-start | bytes 4915200 | tf_op jit(solution)/shard_map/all_gather | solution.py:923
  299.8 193.8 %reduce-scatter.5.cloned.1.call-start = ((), (), s32[]{:S(2)}) async-start(), calls=%async_computation.7 | async-start | bytes 7618560 | tf_op jit(solution)/shard_map/reduce_scatter | solution.py:909
  319.8 103.8 %all-to-all-start.3 = ((bf16[8,240,768]{2,1,0:T(8,128)(2,1)}), bf16[8,240,768]{2,1,0:T(8,128)(2,1)S(1)}, u32[]{:S(2)}, u32[]{:S(2)}) async-start(bf16[8,240,768]{2,1,0:T(8,128)(2,1)} %bitcast.20), calls=%async_computation.5 | async-start | bytes 5898240 | tf_op jit(solution)/shard_map/all_to_all | solution.py:371
  423.6 38.9 %collective-permute-start.37 = (bf16[640,640]{1,0:T(8,128)(2,1)}, bf16[640,640]{1,0:T(8,128)(2,1)}, u32[]{:S(2)}, u32[]{:S(2)}) collective-permute-start(bf16[640,640]{1,0:T(8,128)(2,1)} %get-tuple-element.175.d2), channel_id=1, source_target_pairs={{0,2},{1,3},{2,0},{3,1},{4,6},{5,7},{6,4},{7,5},{8,10},{9,11},{10,... | collective-permute-start | bytes 2457608 | tf_op jit(solution)/shard_map/ppermute | solution.py:377
  423.6 61.2 %collective-permute-start.38 = (bf16[640,640]{1,0:T(8,128)(2,1)}, bf16[640,640]{1,0:T(8,128)(2,1)}, u32[]{:S(2)}, u32[]{:S(2)}) collective-permute-start(bf16[640,640]{1,0:T(8,128)(2,1)} %get-tuple-element.176.d3), channel_id=1, source_target_pairs={{0,3},{1,2},{2,1},{3,0},{4,7},{5,6},{6,5},{7,4},{8,11},{9,10},{10,... | collective-permute-start | bytes 2457608 | tf_op jit(solution)/shard_map/ppermute | solution.py:377
  434.3 59.1 %collective-permute-start.23 = (bf16[24,576]{1,0:T(8,128)(2,1)S(1)}, bf16[24,576]{1,0:T(8,128)(2,1)S(1)}, u32[]{:S(2)}, u32[]{:S(2)}) collective-permute-start(bf16[24,576]{1,0:T(8,128)(2,1)S(1)} %get-tuple-element.285), channel_id=1, source_target_pairs={{0,3},{1,2},{2,1},{3,0},{4,7},{5,6},{6,5},{7,4},{8,11},{9,10},{10,... | collective-permute-start | bytes 82952 | tf_op jit(solution)/shard_map/ppermute | solution.py:377
  436.3 57.1 %collective-permute-start.24 = (bf16[24,576]{1,0:T(8,128)(2,1)S(1)}, bf16[24,576]{1,0:T(8,128)(2,1)S(1)}, u32[]{:S(2)}, u32[]{:S(2)}) collective-permute-start(bf16[24,576]{1,0:T(8,128)(2,1)S(1)} %get-tuple-element.262), channel_id=1, source_target_pairs={{0,2},{1,3},{2,0},{3,1},{4,6},{5,7},{6,4},{7,5},{8,10},{9,11},{10,... | collective-permute-start | bytes 82952 | tf_op jit(solution)/shard_map/ppermute | solution.py:377
  438.3 55.2 %collective-permute-start.25 = (bf16[24,576]{1,0:T(8,128)(2,1)S(1)}, bf16[24,576]{1,0:T(8,128)(2,1)S(1)}, u32[]{:S(2)}, u32[]{:S(2)}) collective-permute-start(bf16[24,576]{1,0:T(8,128)(2,1)S(1)} %get-tuple-element.284), channel_id=1, source_target_pairs={{0,1},{1,0},{2,3},{3,2},{4,5},{5,4},{6,7},{7,6},{8,9},{9,8},{10,11... | collective-permute-start | bytes 82952 | tf_op jit(solution)/shard_map/ppermute | solution.py:377
  (64 other events, 747.8 us)
Sparse Core Ops, SparseCore 0:
  43.6 18.8 all-gather.8
  64.1 51.5 all-gather.10
  117.2 37.4 all-gather.12
  298.1 59.9 reduce-scatter.2
  359.6 32.9 all-gather.14
  395.2 82.5 reduce-scatter.4

commit v3 on v2

--- a/solution.py
+++ b/solution.py
@@ -331,25 +331,29 @@
     def __init__(self, n_expert, capacity):
         self.n_expert = n_expert
         self.cut = n_expert == 8
-        self.near = n_expert // 2 if self.cut else n_expert
         self.block = -(-(capacity + SPARE) // 16) * 16
-        self.chunks = [[list(range(self.near))]]
         if self.cut:
-            self.chunks += [[[4], [5]], [[6], [7]]]
+            self.groups = [[0, 1, 4, 5], [2, 3, 6, 7]]
+            self.rels = [2, 3, 6, 7]
+            self.chunks = [[[0, 1, 2, 3]], [[4], [5], [6], [7]]]
+        else:
+            self.groups = None
+            self.chunks = [[list(range(n_expert))]]
         self.arrays = [array for chunk in self.chunks for array in chunk]
 
     def block_of(self, expert, me):
         if not self.cut:
             return expert
-        inside = jnp.bitwise_xor(expert, me) & (self.near - 1)
-        return jnp.where((expert & self.near) == (me & self.near), expert & (self.near - 1), self.near + inside)
+        rel = jnp.bitwise_xor(expert, me)
+        inside = lambda index: (index & 1) | ((index >> 1) & 2)
+        return jnp.where((rel & 2) == 0, inside(expert), 4 + inside(rel))
 
     def expert_of(self, block, me):
         if not self.cut:
             return block
-        if block < self.near:
-            return (me & self.near) + block
-        return jnp.bitwise_xor(me, block)
+        if block < 4:
+            return (me & 2) | (block & 1) | ((block & 2) << 1)
+        return jnp.bitwise_xor(me, self.rels[block - 4])
 
     def split(self, flat):
         flat = list(flat)
@@ -357,14 +361,12 @@
 
     def exchange(self, c, blocks):
         if c == 0:
-            groups = [[g * self.near + i for i in range(self.near)] for g in range(self.n_expert // self.near)]
             return [
                 lax.all_to_all(
-                    blocks[0], "expert", split_axis=0, concat_axis=0, tiled=True,
-                    axis_index_groups=groups if self.cut else None,
+                    blocks[0], "expert", split_axis=0, concat_axis=0, tiled=True, axis_index_groups=self.groups
                 )
             ]
-        return [swap(block, "expert", array[0]) for array, block in zip(self.chunks[c], blocks)]
+        return [swap(block, "expert", rel) for rel, block in zip(self.rels, blocks)]
 
 
 def over_experts(block):
@@ -458,16 +460,42 @@
     refs = list(refs)
     take = lambda n: [refs.pop(0) for _ in range(n)]
     x_refs = take(len(chunk))
-    g_all, router_ref, first_ref, second_ref = take(4)
+    g_all, router_ref = take(2)
+    first_refs = take(4)
+    (second_ref,) = take(1)
     if not fresh:
-        take(2)
+        take(1)
     (out_all,) = take(1)
     dx_refs = take(len(chunk))
-    if not fresh:
-        take(1)
-    rows_ref, grad_ref, act_ref, inner_ref, g_buf, out_buf, out_acc, dx_acc, sem = refs
+    rows_ref, grad_ref, act_ref, inner_ref, first_buf, second_buf, g_buf, out_buf, out_acc, dx_acc, gate_acc, gates_acc, sem, in_sem = refs
     step = pl.program_id(0)
+    slot = lax.rem(step, 2)
     total, width = rows_ref.shape
+    depth, units = first_refs[0].shape[0], second_buf.shape[1]
+
+    def fetch(rel, slot):
+        column = pl.multiple_of(jnp.bitwise_xor(me_ref[1], rel) * units, 128)
+        copies = [pltpu.make_async_copy(second_ref.at[pl.ds(column, units), :], second_buf.at[slot], in_sem.at[slot, 4])]
+        for piece, ref in enumerate(first_refs):
+            row = pl.multiple_of(jnp.bitwise_xor(me_ref[1], piece) * depth, 16)
+            copies.append(
+                pltpu.make_async_copy(
+                    ref.at[:, pl.ds(column, units)], first_buf.at[slot, pl.ds(row, depth), :], in_sem.at[slot, piece]
+                )
+            )
+        return copies
+
+    @pl.when(step == 0)
+    def _():
+        for copy in fetch(0, 0):
+            copy.start()
+
+    for rel in range(4):
+        @pl.when(step == rel)
+        def _(rel=rel):
+            if rel < 3:
+                for copy in fetch(rel + 1, (rel + 1) % 2):
+                    copy.start()
     rows = slots.block
     pieces = []
     for x_ref, dx_ref, array in zip(x_refs, dx_refs, chunk):
@@ -502,7 +530,15 @@
             top = jnp.maximum(mine, its)
             mine, its = jnp.exp(mine - top), jnp.exp(its - top)
             line = lax.broadcasted_iota(jnp.int32, grads.shape, 0)
-            grad_ref[at, :] = jnp.where(line < rows - SPARE, mine / (mine + its) * grads, 0.0).astype(BF16)
+            gate = mine / (mine + its)
+            gate_acc[at, :] = jnp.broadcast_to(gate, (rows, 128))
+            grad_ref[at, :] = jnp.where(line < rows - SPARE, gate * grads, 0.0).astype(BF16)
+
+    for rel in range(4):
+        @pl.when(step == rel)
+        def _(rel=rel):
+            for copy in fetch(rel, rel % 2):
+                copy.wait()
 
     parts = 1
     while total // parts > 512 or total % parts or (total // parts) % 16:
@@ -510,7 +546,7 @@
     part = total // parts
     for i in range(parts):
         at = slice(i * part, (i + 1) * part)
-        first_w, second_w = first_ref[...], second_ref[...]
+        first_w, second_w = first_buf[slot], second_buf[slot]
         value = dot(rows_ref[at, :], first_w, NN)
         grad_act = dot(grad_ref[at, :], second_w, NT)
         square = value * value
@@ -527,7 +563,12 @@
 
     @pl.when(step == pl.num_programs(0) - 1)
     def _():
-        out_buf[...] = out_acc[...].astype(BF16)
+        for *_, first in pieces:
+            at = slice(first, first + rows)
+            out = out_acc[at, :].astype(BF16).astype(F32)
+            gates = jnp.sum(out * g_buf[at, :].astype(F32), axis=1, keepdims=True)
+            gates_acc[at, :] = jnp.broadcast_to(gates, (rows, 128))
+            out_buf[at, :] = (gate_acc[at, 0:1] * out).astype(BF16)
         copies = [
             pltpu.make_async_copy(out_buf.at[pl.ds(first, rows), :], out_all.at[home(block), :], sem.at[i])
             for i, (block, _, _, _, first) in enumerate(pieces)
@@ -536,7 +577,7 @@
             copy.start()
         for _, _, dx_ref, inside, first in pieces:
             at = slice(first, first + rows)
-            gates = jnp.sum(out_buf[at, :].astype(F32) * g_buf[at, :].astype(F32), axis=1, keepdims=True)
+            gates = gates_acc[at, 0:1]
             gates = jnp.sum(jnp.where(diagonal(rows), gates, 0.0), axis=0, keepdims=True)
             dx_ref[inside:inside + rows, :] = dx_acc[at, :].astype(BF16)
             tail = dx_acc[first + rows - 16:first + rows, :]
@@ -550,74 +591,121 @@
             copy.wait()
 
 
-def run_expert(slots, chunk, me, blocks, g_all, router, first_w, second_w, out_all, near):
-    width, hidden = first_w.shape
+def run_expert(slots, chunk, me, blocks, g_all, router, first_w, second_w, out_all, estimate):
+    hidden, width = first_w[0].shape[1], router.shape[0]
     total = sum(block.shape[0] for block in blocks)
     block = hidden // 4
     whole = lambda a: pl.BlockSpec(a.shape, lambda i: (0, 0))
     column = pl.BlockSpec((total, block), lambda i: (0, i))
     rows = pl.BlockSpec((total, width), lambda i: (0, 0))
     fresh = out_all is None
-    inputs = [me, *blocks, g_all, router, first_w, second_w] + ([] if fresh else [out_all, near])
+    inputs = [me, *blocks, g_all, router, *first_w, second_w] + ([] if fresh else [out_all])
     return pl.pallas_call(
         functools.partial(expert_kernel, slots, chunk, fresh),
         grid=(4,),
-        in_specs=[SMEM]
-        + [whole(b) for b in blocks]
-        + [ANY, whole(router), pl.BlockSpec((width, block), lambda i: (0, i)), pl.BlockSpec((block, width), lambda i: (i, 0))]
-        + ([] if fresh else [ANY, ANY]),
-        out_specs=[ANY] + [whole(b) for b in blocks] + ([] if fresh else [ANY]) + [rows, rows, column, column],
+        in_specs=[SMEM] + [whole(b) for b in blocks] + [ANY, whole(router)] + [ANY] * 5 + ([] if fresh else [ANY]),
+        out_specs=[ANY] + [whole(b) for b in blocks] + [rows, rows, column, column],
         out_shape=arrays(
-            (g_all.shape, BF16), *[(b.shape, BF16) for b in blocks], *([] if fresh else [(near.shape, BF16)]), *[((total, width), BF16)] * 2, *[((total, hidden), BF16)] * 2
+            (g_all.shape, BF16), *[(b.shape, BF16) for b in blocks], *[((total, width), BF16)] * 2, *[((total, hidden), BF16)] * 2
         ),
         scratch_shapes=[
+            pltpu.VMEM((2, width, block), BF16),
+            pltpu.VMEM((2, block, width), BF16),
             pltpu.VMEM((total, width), BF16),
             pltpu.VMEM((total, width), BF16),
             pltpu.VMEM((total, width), F32),
             pltpu.VMEM((total, width), F32),
+            pltpu.VMEM((total, 128), F32),
+            pltpu.VMEM((total, 128), F32),
             pltpu.SemaphoreType.DMA((sum(len(array) for array in chunk),)),
+            pltpu.SemaphoreType.DMA((2, 5)),
         ],
-        input_output_aliases={} if fresh else {len(inputs) - 2: 0, len(inputs) - 1: 1 + len(blocks)},
+        input_output_aliases={} if fresh else {len(inputs) - 1: 0},
+        compiler_params=params(dimension_semantics=("arbitrary",)),
+        cost_estimate=estimate,
+    )(*inputs)
+
+
+def first_grad_kernel(parts, me_ref, *refs):
+    send_ref, keep_ref, total = refs[-3:]
+    total[...] = sum(dot(x[...], inner[...], TN) for x, inner in zip(refs[:parts], refs[parts:2 * parts]))
+    depth = send_ref.shape[0] // 2
+    for rel in range(4):
+        ref = (keep_ref, send_ref)[rel % 2]
+        row = pl.multiple_of(jnp.bitwise_xor(me_ref[1], rel) * depth, 16)
+        at = rel // 2 * depth
+        ref[at:at + depth, :] = total[pl.ds(row, depth), :].astype(BF16)
+
+
+def run_first_grad(me, rows, inners, depth, *after):
+    width, hidden = rows[0].shape[1], inners[0].shape[1]
+    block = hidden // 4
+    column = pl.BlockSpec((2 * depth, block), lambda i, me_ref: (0, jnp.bitwise_xor(me_ref[1], i)))
+    return pl.pallas_call(
+        functools.partial(first_grad_kernel, len(rows)),
+        grid_spec=pltpu.PrefetchScalarGridSpec(
+            num_scalar_prefetch=1,
+            grid=(4,),
+            in_specs=[pl.BlockSpec(a.shape, lambda i, me_ref: (0, 0)) for a in rows]
+            + [pl.BlockSpec((a.shape[0], block), lambda i, me_ref: (0, i)) for a in inners]
+            + [ANY] * len(after),
+            out_specs=[column, column],
+            scratch_shapes=[pltpu.VMEM((width, block), F32)],
+        ),
+        out_shape=arrays(*[((2 * depth, hidden), BF16)] * 2),
         compiler_params=params(dimension_semantics=("arbitrary",)),
         cost_estimate=SHORT,
-    )(*inputs)
-
-
-def first_grad_kernel(parts, *refs):
-    out_ref = refs[-1]
-    out_ref[...] = sum(dot(x[...], inner[...], TN) for x, inner in zip(refs[:parts], refs[parts:2 * parts])).astype(BF16)
-
-
-def run_first_grad(rows, inners, more):
-    width, hidden = rows[0].shape[1], inners[0].shape[1]
-    block = hidden // 4
-    total = sum(a.shape[0] for a in rows)
-    return pl.pallas_call(
-        functools.partial(first_grad_kernel, len(rows)),
-        grid=(4,),
-        in_specs=[pl.BlockSpec(a.shape, lambda i: (0, 0)) for a in rows]
-        + [pl.BlockSpec((a.shape[0], block), lambda i: (0, i)) for a in inners],
-        out_specs=pl.BlockSpec((width, block), lambda i: (0, i)),
-        out_shape=jax.ShapeDtypeStruct((width, hidden + more), BF16),
-        compiler_params=params(dimension_semantics=("arbitrary",)),
-        cost_estimate=SHORT,
-    )(*rows, *inners)
+    )(me, *rows, *inners, *after)
+
+
+def second_grad_kernel(parts, *refs):
+    send_ref, keep_ref = refs[2 * parts:]
+    step = pl.program_id(0)
+    block = sum(dot(act[...], g[...], TN) for act, g in zip(refs[:parts], refs[parts:2 * parts])).astype(BF16)
+
+    @pl.when(step < 2)
+    def _():
+        send_ref[...] = block
+
+    @pl.when(step >= 2)
+    def _():
+        keep_ref[...] = block
 
 
 def run_second_grad(acts, grads):
     width, hidden = grads[0].shape[1], acts[0].shape[1]
     block = hidden // 4
-    total = sum(a.shape[0] for a in acts)
     return pl.pallas_call(
-        functools.partial(first_grad_kernel, len(acts)),
+        functools.partial(second_grad_kernel, len(acts)),
         grid=(4,),
-        in_specs=[pl.BlockSpec((a.shape[0], block), lambda i: (0, i)) for a in acts]
+        in_specs=[pl.BlockSpec((a.shape[0], block), lambda i: (0, 2 * (i % 2) + 1 - i // 2)) for a in acts]
         + [pl.BlockSpec(a.shape, lambda i: (0, 0)) for a in grads],
-        out_specs=pl.BlockSpec((block, width), lambda i: (i, 0)),
-        out_shape=jax.ShapeDtypeStruct((hidden, width), BF16),
+        out_specs=[
+            pl.BlockSpec((block, width), lambda i: (jnp.minimum(i, 1), 0)),
+            pl.BlockSpec((block, width), lambda i: (jnp.maximum(i - 2, 0), 0)),
+        ],
+        out_shape=arrays(*[((2 * block, width), BF16)] * 2),
         compiler_params=params(dimension_semantics=("arbitrary",)),
         cost_estimate=SHORT,
     )(*acts, *grads)
+
+
+def core_sum(send, keep):
+    near = swap(send, "shard", 1)
+    half = keep.shape[0] // 2
+    other = (keep[half:].astype(F32) + near[half:].astype(F32)).astype(BF16)
+    return keep, near, other
+
+
+def across_sum(parts):
+    keep, near, other = parts
+    return keep, near, swap(other, "shard", 2)
+
+
+def total_sum(parts):
+    keep, near, far = parts
+    half = keep.shape[0] // 2
+    return keep[:half].astype(F32) + near[:half].astype(F32) + far.astype(F32)
 
 
 def gather_blocks(slots, refs, scratch):
@@ -630,10 +718,11 @@
     take = lambda n: [refs_left.pop(0) for _ in range(n)]
     ret_refs = take(len(slots.arrays))
     places_ref, routes_ref, gates_ref, after_ref, gain_ref, router_ref, g_ref = take(7)
-    (w_ref,) = take(1)
-    grad_after_ref, branch_ref = take(2)
+    w_ref, normed_ref = take(2)
+    m_refs = take(4)
+    (grad_after_ref,) = take(1)
     mixed_refs = take(4)
-    glogits_ref, ggain_ref, scratch = refs_left
+    send_ref, keep_ref, branch_ref, glogits_ref, ggain_ref, more, scratch = refs_left
     tokens = after_ref.shape[0]
     part = 128
     gather_blocks(slots, ret_refs, scratch)
@@ -671,9 +760,21 @@
         return carry
 
     lax.fori_loop(0, tokens // part, one, 0)
-
-
-def combine_kernel(slots, me_ref, ret_ref, places_ref, gates_ref, after_ref, out_ref, scratch):
+    width = branch_ref.shape[1]
+    grad_router = dot(normed_ref[...], glogits_ref[...], TN)
+    gain = jnp.transpose(jnp.concatenate([ggain_ref[...]] * 16, axis=0))[:, 0:1]
+    blank = jnp.zeros((width, more.shape[1] - grad_router.shape[1] - 1), F32)
+    more[...] = jnp.concatenate([grad_router, gain, blank], axis=1)
+    for rel, m_ref in enumerate(m_refs):
+        ref = (keep_ref, send_ref)[rel % 2]
+        count = m_ref.shape[1]
+        at = slice(rel // 2 * count, (rel // 2 + 1) * count)
+        ref[at, 0:width] = dot(m_ref[...], branch_ref[...], TN).astype(BF16)
+        row = pl.multiple_of(jnp.bitwise_xor(me_ref[0], rel) * count, 16)
+        ref[at, width:] = more[pl.ds(row, count), :].astype(BF16)
+
+
+def combine_kernel(slots, me_ref, ret_ref, places_ref, after_ref, out_ref, scratch):
     part = 128
     for block in range(slots.n_expert):
         first = pl.multiple_of(slots.expert_of(block, me_ref[0]) * slots.block, 16)
@@ -681,31 +782,13 @@
 
     def one(i, carry):
         at = pl.ds(pl.multiple_of(i * part, part), part)
-        total = after_ref[at, :]
         slot = lax.broadcasted_iota(jnp.int32, (part, scratch.shape[0]), 1)
-        for j in range(2):
-            hot = jnp.where(slot == places_ref[at, j:j + 1], 1.0, 0.0).astype(BF16)
-            total = total + gates_ref[at, j:j + 1] * dot(hot, scratch[...], NN)
+        hit = (slot == places_ref[at, 0:1]) | (slot == places_ref[at, 1:2])
+        total = after_ref[at, :] + dot(jnp.where(hit, 1.0, 0.0).astype(BF16), scratch[...], NN)
         out_ref[at, :] = total.astype(BF16)
         return carry
 
     lax.fori_loop(0, after_ref.shape[0] // part, one, 0)
-
-
-def output_grad_kernel(me_ref, branch_ref, normed_ref, glogits_ref, ggain_ref, m0, m1, m2, m3, room_ref, out_ref, buf, sem):
-    width = branch_ref.shape[1]
-    for rel, m_ref in enumerate((m0, m1, m2, m3)):
-        count = m_ref.shape[1]
-        at = pl.ds(pl.multiple_of(jnp.bitwise_xor(me_ref[0], rel) * count, 16), count)
-        buf[at, 0:width] = dot(m_ref[...], branch_ref[...], TN).astype(BF16)
-    grad_router = dot(normed_ref[...], glogits_ref[...], TN)
-    gain = jnp.transpose(jnp.concatenate([ggain_ref[...]] * 16, axis=0))[:, 0:1]
-    blank = jnp.zeros((width, buf.shape[1] - width - grad_router.shape[1] - 1), F32)
-    buf[:, width:] = jnp.concatenate([grad_router, gain, blank], axis=1).astype(BF16)
-    hidden = out_ref.shape[1] - buf.shape[1]
-    copy = pltpu.make_async_copy(buf, out_ref.at[:, hidden:], sem)
-    copy.start()
-    copy.wait()
 
 
 def final_kernel(me_ref, x_ref, gain_ref, after_ref, d0, d1, d2, d3, w_ref, out_ref):
@@ -766,7 +849,7 @@
     rows = width // n_shard
     slots = Slots(n_expert, max(2, tok * 20 // (7 * n_experts)))
     me_s, me_e = lax.axis_index("shard").astype(jnp.int32), lax.axis_index("expert").astype(jnp.int32)
-    me_shard, me_expert = me_s.reshape(1), me_e.reshape(1)
+    me_shard, me_expert, me = me_s.reshape(1), me_e.reshape(1), jnp.stack([me_e, me_s])
 
     more = jnp.concatenate([gain_attn[:, None], gain_moe[:, None], router], axis=1)
     w_rel = pl.pallas_call(
@@ -824,7 +907,13 @@
         compiler_params=params(),
         cost_estimate=LONG,
     )(me_shard, parent_row, queries, keys, values, values_t, bias)
+    first_far = swap(w_in[0], "shard", 2)
+    mixed, first_far = lax.optimization_barrier((mixed, first_far))
     mixed = swap_all(mixed, "shard")
+    first_w = [w_in[0], swap(w_in[0], "shard", 1), first_far, swap(first_far, "shard", 1)]
+    w_out, w_cols, _ = lax.optimization_barrier((w_out, w_cols, mixed))
+    second_w = lax.all_gather(w_out[0], "shard", axis=0, tiled=True)
+    mixed, first_w = lax.optimization_barrier((mixed, first_w))
 
     w_o = lax.all_gather(w_output, "shard", axis=0)
     after, normed_two, gates, *sent_rows = pl.pallas_call(
@@ -838,55 +927,49 @@
     sent_rows = slots.split(sent_rows)
     got_rows = [slots.exchange(c, blocks) for c, blocks in enumerate(sent_rows)]
 
-    w_in, w_out, _ = lax.optimization_barrier((w_in, w_out, w_cols))
-    first_w = lax.all_gather(w_in[0], "shard", axis=0, tiled=True)
-    second_w = lax.all_gather(w_out[0], "shard", axis=0, tiled=True)
-    out_all = near = None
-    sent_dx, kept = [], []
+    out_all = None
+    dx, kept = [], []
     for c, chunk in enumerate(slots.chunks):
         n = len(chunk)
         out_all, *done = run_expert(
-            slots, chunk, me_expert, got_rows[c], got_grads, router_w, first_w, second_w, out_all, near
+            slots, chunk, me, got_rows[c], got_grads, router_w, first_w, second_w, out_all, LONG if c else SHORT
         )
-        sent_dx.append(done[:n])
-        near = done[0] if c == 0 else done[n]
-        kept.append(done[-4:])
-    sent_dx[0] = [near]
-    dx = [slots.exchange(c, blocks) for c, blocks in enumerate(sent_dx)]
-    grad_first = run_first_grad([k[0] for k in kept], [k[3] for k in kept], width + 128)
-    grad_second = run_second_grad([k[2] for k in kept], [k[1] for k in kept])
-
+        dx.append(slots.exchange(c, done[:n]))
+        kept.append(done[n:])
+    send_second, keep_second = run_second_grad([k[2] for k in kept], [k[1] for k in kept])
     dx = [block for blocks in dx for block in blocks]
+    w_cols, _ = lax.optimization_barrier((w_cols, kept[0][0]))
+    w_all = lax.all_gather(w_cols, "shard", axis=0)
+    send_first, keep_first = run_first_grad(me, [k[0] for k in kept], [k[3] for k in kept], rows, dx[0], w_all)
     out_all, _ = lax.optimization_barrier((out_all, dx))
     returned = over_experts(out_all)
-    dx, grad_first, grad_second = lax.optimization_barrier((dx, grad_first, grad_second))
+    dx, send_first, send_second = lax.optimization_barrier((dx, send_first, send_second))
 
     slot_rows = slots.n_expert * slots.block
-    grad_after, branch, gm0, gm1, gm2, gm3, glogits, ggain_two = pl.pallas_call(
+    grad_after, gm0, gm1, gm2, gm3, send_wo, keep_wo = pl.pallas_call(
         functools.partial(back_kernel, slots),
-        in_specs=[SMEM] + [VMEM] * (len(block_shapes) + 8),
-        out_specs=[VMEM] * 8,
-        out_shape=arrays(
-            ((tok, width), F32), ((tok, width), BF16), *[((tok, hw), BF16)] * 4, ((tok, n_experts), BF16), ((8, width), F32)
-        ),
-        scratch_shapes=[pltpu.VMEM((slot_rows, width), BF16)],
+        in_specs=[SMEM] + [VMEM] * (len(block_shapes) + 13),
+        out_specs=[VMEM] * 7,
+        out_shape=arrays(((tok, width), F32), *[((tok, hw), BF16)] * 4, *[((2 * rows, width + 128), BF16)] * 2),
+        scratch_shapes=[
+            pltpu.VMEM((tok, width), BF16),
+            pltpu.VMEM((tok, n_experts), BF16),
+            pltpu.VMEM((8, width), F32),
+            pltpu.VMEM((width, 128), F32),
+            pltpu.VMEM((slot_rows, width), BF16),
+        ],
         compiler_params=params(),
         cost_estimate=SHORT,
-    )(me_shard, *dx, places, routes, gates, after, gain_two, router_w, cotangent, w_o)
+    )(me_shard, *dx, places, routes, gates, after, gain_two, router_w, cotangent, w_o, normed_two, *mixed)
     grad_mixed = swap_all([gm0, gm1, gm2, gm3], "shard")
-    grad_first = pl.pallas_call(
-        output_grad_kernel,
-        in_specs=[SMEM] + [VMEM] * 8 + [ANY],
-        out_specs=ANY,
-        out_shape=jax.ShapeDtypeStruct(grad_first.shape, BF16),
-        scratch_shapes=[pltpu.VMEM((width, width + 128), BF16), pltpu.SemaphoreType.DMA],
-        input_output_aliases={9: 0},
-        compiler_params=params(),
-        cost_estimate=SHORT,
-    )(me_shard, branch, normed_two, glogits, ggain_two, *mixed, grad_first)
-
-    grad_w_out = lax.psum_scatter(grad_second, "shard", scatter_dimension=0, tiled=True)
-    grad_mixed, grad_w_out = lax.optimization_barrier((grad_mixed, grad_w_out))
+    sums = [
+        core_sum(send, keep)
+        for send, keep in ((send_second, keep_second), (send_first, keep_first), (send_wo, keep_wo))
+    ]
+    grad_mixed, sums = lax.optimization_barrier((grad_mixed, sums))
+    second_sum, first_sum, wo_sum = sums
+    second_sum, wo_sum = across_sum(second_sum), across_sum(wo_sum)
+
     *dqkv, bins = pl.pallas_call(
         functools.partial(attn_backward_kernel, heads),
         in_specs=[SMEM] * 2 + [VMEM] * 11,
@@ -900,36 +983,12 @@
             pltpu.VMEM((2, SEG, heads * SEG), F32),
         ],
         compiler_params=params(),
-        cost_estimate=SHORT,
+        cost_estimate=LONG,
     )(me_shard, parent_row, queries, keys, values, keys_t, raw, lse, *grad_mixed, bias)
+    dqkv, second_sum, wo_sum = lax.optimization_barrier((dqkv, second_sum, wo_sum))
     dqkv_own = swap_all(dqkv, "shard")
 
-    hidden = w_in.shape[2]
-    grad_w_out = grad_w_out.astype(F32)[None]
-    grad_first = lax.psum_scatter(grad_first, "shard", scatter_dimension=0, tiled=True)
-    grad_w_in = grad_first[:, :hidden].astype(F32)[None]
-    grad_wo = grad_first[:, hidden:]
-    output = pl.pallas_call(
-        functools.partial(combine_kernel, slots),
-        in_specs=[SMEM] + [VMEM] * 4,
-        out_specs=VMEM,
-        out_shape=jax.ShapeDtypeStruct((tok, width), BF16),
-        scratch_shapes=[pltpu.VMEM((slot_rows, width), BF16)],
-        compiler_params=params(),
-        cost_estimate=SHORT,
-    )(me_expert, returned, places, gates, after)
-
-    w_cols, _ = lax.optimization_barrier((w_cols, after))
-    w_all = lax.all_gather(w_cols, "shard", axis=0)
-    grad_tokens = pl.pallas_call(
-        final_kernel,
-        in_specs=[SMEM] + [VMEM] * 8,
-        out_specs=VMEM,
-        out_shape=jax.ShapeDtypeStruct((tok, width), BF16),
-        compiler_params=params(),
-        cost_estimate=SHORT,
-    )(me_shard, tokens, gain_one, grad_after, *dqkv_own, w_all)
-
+    grad_w_out, grad_wo = total_sum(second_sum)[None], total_sum(wo_sum).astype(BF16)
     halving = [bit for bit in (1, 2, 4) if bit < n_expert] if n_expert <= 8 else []
     rels = [0]
     for bit in reversed(halving):
@@ -945,6 +1004,8 @@
     )(me_expert if halving else jnp.zeros((1,), jnp.int32), bins, *normed_one, *dqkv)
     for bit in halving:
         kept_half, sent_half = jnp.split(cols, 2, axis=0)
+        if bit == halving[-1]:
+            sent_half, dqkv_own = lax.optimization_barrier((sent_half, dqkv_own))
         cols = (kept_half.astype(F32) + swap(sent_half, "expert", bit).astype(F32)).astype(BF16)
     if halving:
         grad_wo = grad_wo.reshape(n_expert, rows // n_expert, -1)
@@ -959,10 +1020,31 @@
     table = cols[:NB, 3 * hw:3 * hw + heads].astype(F32).T
     share = cols.shape[0] // n_shard
     cols = cols.astype(BF16)[:, :3 * hw].reshape(n_shard, share, 3 * hw)
+    cols, dqkv_own = lax.optimization_barrier((cols, dqkv_own))
+    grad_tokens = pl.pallas_call(
+        final_kernel,
+        in_specs=[SMEM] + [VMEM] * 8,
+        out_specs=VMEM,
+        out_shape=jax.ShapeDtypeStruct((tok, width), BF16),
+        compiler_params=params(),
+        cost_estimate=SHORT,
+    )(me_shard, tokens, gain_one, grad_after, *dqkv_own, w_all)
     cols = reorder([cols[p] for p in range(n_shard)], me_s)
-    cols = reorder(swap_all(cols, "shard"), me_s)
+    cols, first_sum = lax.optimization_barrier((swap_all(cols, "shard"), first_sum))
+    cols = reorder(cols, me_s)
+    grad_w_in = total_sum(across_sum(first_sum))[None]
     cols = jnp.concatenate([c[:, i * hw:(i + 1) * hw] for i in range(3) for c in cols], axis=1)
     cols = jnp.concatenate([cols, grad_wo], axis=1)
+    returned, _ = lax.optimization_barrier((returned, cols))
+    output = pl.pallas_call(
+        functools.partial(combine_kernel, slots),
+        in_specs=[SMEM] + [VMEM] * 3,
+        out_specs=VMEM,
+        out_shape=jax.ShapeDtypeStruct((tok, width), BF16),
+        scratch_shapes=[pltpu.VMEM((slot_rows, width), BF16)],
+        compiler_params=params(),
+        cost_estimate=SHORT,
+    )(me_expert, returned, places, after)
     pieces = swap_all([cols] * n_expert, "expert") if halving else [cols]
     pieces, output, grad_w_in, grad_w_out = lax.optimization_barrier((pieces, output, grad_w_in, grad_w_out))
     grad_q, grad_k, grad_v, grad_wo, grad_gain_one = pl.pallas_call(

time: 567 us -> 471 us (0.83)
  waiting for transfers between devices: 216 us -> 107 us
  starting transfers between devices: 69.9 us -> 82.5 us
  other arithmetic: 12 us -> 22.1 us
  Pallas kernels: 226 us -> 219 us
    ppermute x39 -> x48, waiting for transfers between devices: 184 us -> 65.6 us  [swap(): lax.ppermute(block, axis, [(i, i ^ rel) for i in range(lax.axis_size(axis...]
    all_to_all x2, waiting for transfers between devices: 0.01 us -> 11.3 us  [over_experts(): lax.all_to_all(block, 'expert', split_axis=0, concat_axis=0, tiled=True)]
    all_to_all x2, starting transfers between devices: 8.02 us -> 16.8 us  [exchange(): lax.all_to_all(blocks[0], 'expert', split_axis=0, concat_axis=0, tiled=Tr...]
    convert_element_type x0 -> x4, other arithmetic: none -> 8.3 us  [the longest x3 7.09 us: core_sum(): other = (keep[half:].astype(F32) + near[half:].astype(F32)).astype(BF16)]
    ppermute x39 -> x48, starting transfers between devices: 51.6 us -> 54.9 us  [swap(): lax.ppermute(block, axis, [(i, i ^ rel) for i in range(lax.axis_size(axis...]
    pallas_call x3 -> x2, Pallas kernels: 34.5 us -> 31.4 us  [the longest x1 16 us: run_first_grad(): pl.pallas_call(functools.partial(first_grad_kernel, len(rows)), grid_spec...]
    pallas_call x3 -> x2, Pallas kernels: 65.5 us -> 62.5 us  [run_expert(): pl.pallas_call(functools.partial(expert_kernel, slots, chunk, fresh), gri...]
  transfers between devices with their start and end apart: 49 -> 55, of which waited for: 20 -> 17; matrix products, arithmetic and copies ran while one was open for 3% -> 6% of each run, Pallas kernels for 37% -> 47%
where the time goes in v3:
time: 471 us; the launch traced here: 464 us
  Pallas kernels  219 us (46%)
  waiting for transfers between devices  107 us (23%)
  starting transfers between devices  82.5 us (18%)
  other arithmetic  22.1 us (5%)
  local copies, waits for them, and re-layouts  18.6 us (4%)
  between operations  14.7 us (3%)
    ppermute x48, waiting for transfers between devices, swap(): lax.ppermute(block, axis, [(i, i ^ rel) for i in range(lax.axis_size(axis...  65.6 us
    pallas_call x2, Pallas kernels, run_expert(): pl.pallas_call(functools.partial(expert_kernel, slots, chunk, fresh), gri...  62.5 us
    ppermute x48, starting transfers between devices, swap(): lax.ppermute(block, axis, [(i, i ^ rel) for i in range(lax.axis_size(axis...  54.9 us
    pallas_call x1, Pallas kernels, per_device(): pl.pallas_call(functools.partial(attn_backward_kernel, heads), in_specs=[...  32.9 us
    all_to_all x2, waiting for transfers between devices, exchange(): lax.all_to_all(blocks[0], 'expert', split_axis=0, concat_axis=0, tiled=Tr...  29.5 us
    pallas_call x1, Pallas kernels, per_device(): pl.pallas_call(functools.partial(attn_forward_kernel, heads), in_specs=[S...  20.9 us
    all_to_all x2, starting transfers between devices, exchange(): lax.all_to_all(blocks[0], 'expert', split_axis=0, concat_axis=0, tiled=Tr...  16.8 us
    pallas_call x1, Pallas kernels, per_device(): pl.pallas_call(functools.partial(back_kernel, slots), in_specs=[SMEM] + [...  16.3 us
  transfers between devices with their start and end apart: 55, of which 17 were waited for; matrix products, arithmetic and copies ran while one was open for 6% of the time, Pallas kernels for 47%

profile of v3, /device:TPU:0, one launch (start us, length us, event | category | flops | bytes accessed | tf_op | source)
XLA Modules:
  0.0 464.4 jit_solution(1328122210822125266)
XLA Ops:
  20.4 8.3 %shard_map.230.before_ref = bf16[1920,768]{1,0:T(8,128)(2,1)} custom-call(s32[1]{0:T(128)} %bitcast.me_ref, s32[2,640]{1,0:T(2,128)} %copy.74.places_ref, bf16[16,640]{1,0:T(8,128)(2,1)} %broadcast_bitcast_fusion.others_ref, bf16[640,768]{1,0:T(8,128)(2,1)} %refs_11_.1, bf16[4,192,640]{2,1,0:T(8,128)(2,1)} %shard_map.229.refs_0_), custom_call_target="tpu_custom_call" | custom-call | bytes 1024 | tf_op jit(solution)/shard_map/pallas_call | solution.py:876
  35.2 6.0 %all-to-all-start = ((bf16[8,240,768]{2,1,0:T(8,128)(2,1)}), bf16[8,240,768]{2,1,0:T(8,128)(2,1)}, u32[]{:S(2)}, u32[]{:S(2)}) async-start(bf16[8,240,768]{2,1,0:T(8,128)(2,1)} %bitcast.64), calls=%async_computation | async-start | bytes 5898240 | tf_op jit(solution)/shard_map/all_to_all | solution.py:373
  47.8 10.5 %shard_map.231 = (bf16[640,768]{1,0:T(8,128)(2,1)}, bf16[640,768]{1,0:T(8,128)(2,1)}, bf16[640,768]{1,0:T(8,128)(2,1)}, bf16[640,768]{1,0:T(8,128)(2,1)}, bf16[2...) custom-call(s32[1]{0:T(128)} %bitcast.1.me_ref, ...), custom_call_target="tpu_custom_call" | custom-call | flops 1099511627776 | bytes 4294967296 | tf_op jit(solution)/shard_map/pallas_call | solution.py:888
  58.3 20.9 %shard_map.232 = (bf16[640,192]{1,0:T(8,128)(2,1)}, bf16[640,192]{1,0:T(8,128)(2,1)}, bf16[640,192]{1,0:T(8,128)(2,1)}, bf16[640,192]{1,0:T(8,128)(2,1)}, f32[2560,256]{1,0:T(8,128)}, /*index=5*/f32[160,384]{1,0:T(8,128)}) custom-call(s32[1]{0:T(128)} %bitcast.1.me_ref, s32[20]{0:T(128)} %bitcast.76, bf16[2560,256]{1,0:T(8,128)(2,1)} %get-tuple-element.154.q_ref, ...), custom_call_target="tpu_custom_call" | custom-call | flops 1099511627776 | bytes 4294967296 | tf_op jit(solution)/shard_map/pallas_call | solution.py:901
  83.4 7.6 %collective-permute-done.8.m2.refs_16_ = bf16[640,192]{1,0:T(8,128)(2,1)S(1)} collective-permute-done((bf16[640,192]{1,0:T(8,128)(2,1)}, bf16[640,192]{1,0:T(8,128)(2,1)S(1)}, u32[]{:S(2)}, u32[]{:S(2)}) %collective-permute-start.8) | collective-permute-done | bytes 245792 | tf_op jit(solution)/shard_map/ppermute | solution.py:379
  91.1 6.1 %collective-permute-done.9.m3.refs_17_ = bf16[640,192]{1,0:T(8,128)(2,1)S(1)} collective-permute-done((bf16[640,192]{1,0:T(8,128)(2,1)}, bf16[640,192]{1,0:T(8,128)(2,1)S(1)}, u32[]{:S(2)}, u32[]{:S(2)}) %collective-permute-start.9) | collective-permute-done | bytes 245792 | tf_op jit(solution)/shard_map/ppermute | solution.py:379
  97.3 11.3 %all-to-all-done = bf16[8,240,768]{2,1,0:T(8,128)(2,1)} async-done(((bf16[8,240,768]{2,1,0:T(8,128)(2,1)}), bf16[8,240,768]{2,1,0:T(8,128)(2,1)}, u32[]{:S(2)}, u32[]{:S(2)}) %all-to-all-start) | async-done | bytes 2949152 | tf_op jit(solution)/shard_map/all_to_all | solution.py:373
  108.6 7.3 %shard_map.233 = (f32[640,768]{1,0:T(8,128)}, bf16[640,768]{1,0:T(8,128)(2,1)}, f32[640,2]{1,0:T(8,128)}, bf16[960,768]{1,0:T(8,128)(2,1)}, bf16[240,768]{1,0:T(...) custom-call(s32[1]{0:T(128)} %bitcast.1.me_ref, ...), custom_call_target="tpu_custom_call" | custom-call | flops 1099511627776 | bytes 4294967296 | tf_op jit(solution)/shard_map/pallas_call | solution.py:919
  127.1 29.5 %all-to-all-done.1 = bf16[4,240,768]{2,1,0:T(8,128)(2,1)S(1)} async-done(((bf16[4,240,768]{2,1,0:T(8,128)(2,1)}), bf16[4,240,768]{2,1,0:T(8,128)(2,1)S(1)}, u32[]{:S(2)}, u32[]{:S(2)}) %all-to-all-start.1) | async-done | bytes 1474592 | tf_op jit(solution)/shard_map/all_to_all | solution.py:365
  157.8 31.3 %shard_map.234 = (bf16[1920,768]{1,0:T(8,128)(2,1)}, bf16[960,768]{1,0:T(8,128)(2,1)}, bf16[960,768]{1,0:T(8,128)(2,1)}, bf16[960,768]{1,0:T(8,128)(2,1)}, bf16[...) custom-call(s32[2]{0:T(128)} %pad_add_fusion.me_ref, bf16[960,768]{1,0:T(8,128)(2,1)} %bitcast.65, ...), custom_call_target="tpu_custom_call" | custom-call | bytes 1024 | tf_op jit(solution)/shard_map/pallas_call | solution.py:603
  189.1 13.1 %all-to-all-start.2 = ((bf16[4,240,768]{2,1,0:T(8,128)(2,1)}), bf16[4,240,768]{2,1,0:T(8,128)(2,1)}, u32[]{:S(2)}, u32[]{:S(2)}) async-start(bf16[4,240,768]{2,1,0:T(8,128)(2,1)} %bitcast.69), calls=%async_computation.2 | async-start | bytes 2949120 | tf_op jit(solution)/shard_map/all_to_all | solution.py:365
  203.2 31.2 %shard_map.235 = (bf16[1920,768]{1,0:T(8,128)(2,1)}, bf16[240,768]{1,0:T(8,128)(2,1)}, bf16[240,768]{1,0:T(8,128)(2,1)}, bf16[240,768]{1,0:T(8,128)(2,1)}, bf16[...) custom-call(s32[2]{0:T(128)} %pad_add_fusion.me_ref, ...), custom_call_target="tpu_custom_call", output_to_operand_aliasing={{0}: (12, {})} | custom-call | flops 1099511627776 | bytes 4294967296 | tf_op jit(solution)/shard_map/pallas_call | solution.py:603
  241.2 15.4 %shard_map.237 = (bf16[1536,768]{1,0:T(8,128)(2,1)}, bf16[1536,768]{1,0:T(8,128)(2,1)}) custom-call(bf16[960,3072]{1,0:T(8,128)(2,1)} %get-tuple-element.201.refs_0_, bf16[960,3072]{1,0:T(8,128)(2,1)} %get-tuple-element.202.refs_1_, bf16[960,768]{1,0:T(8,128)(2,1)} %get-tuple-element.203.refs_2_, bf16[960,768]{1,0:T(8,128)(2,1)} %get-tuple-element.204.refs_3_), custom_call_target="tpu_custom_call" | custom-call | bytes 1024 | tf_op jit(solution)/shard_map/pallas_call | solution.py:678
  256.7 16.0 %shard_map.236 = (bf16[384,3072]{1,0:T(8,128)(2,1)}, bf16[384,3072]{1,0:T(8,128)(2,1)}) custom-call(s32[2]{0:T(128)} %pad_add_fusion.me_ref, bf16[960,768]{1,0:T(8,128)(2,1)} %get-tuple-element.194.refs_0_, bf16[960,768]{1,0:T(8,128)(2,1)} %get-tuple-element.195.refs_1_, bf16[960,3072]{1,0:T(8,128)(2,1)} %get-tuple-element.196.refs_2_, ...), custom_call_target="tpu_custom_call" | custom-call | bytes 1024 | tf_op jit(solution)/shard_map/pallas_call | solution.py:644
  273.7 16.3 %shard_map.238 = (f32[640,768]{1,0:T(8,128)}, bf16[640,192]{1,0:T(8,128)(2,1)}, bf16[640,192]{1,0:T(8,128)(2,1)}, bf16[640,192]{1,0:T(8,128)(2,1)}, bf16[640,192...) custom-call(s32[1]{0:T(128)} %bitcast.1.me_ref, bf16[960,768]{1,0:T(8,128)(2,1)} %bitcast.19.refs_4_.refs_0_, ...), custom_call_target="tpu_custom_call" | custom-call | bytes 1024 | tf_op jit(solution)/shard_map/pallas_call | solution.py:949
  306.1 5.3 %collective-permute-done.22.g3_ref = bf16[640,192]{1,0:T(8,128)(2,1)S(1)} collective-permute-done((bf16[640,192]{1,0:T(8,128)(2,1)S(1)}, bf16[640,192]{1,0:T(8,128)(2,1)S(1)}, u32[]{:S(2)}, u32[]{:S(2)}) %collective-permute-start.22) | collective-permute-done | bytes 245792 | tf_op jit(solution)/shard_map/ppermute | solution.py:379
  314.1 32.9 %shard_map.239 = (bf16[640,640]{1,0:T(8,128)(2,1)}, bf16[640,640]{1,0:T(8,128)(2,1)}, bf16[640,640]{1,0:T(8,128)(2,1)}, bf16[640,640]{1,0:T(8,128)(2,1)}, f32[16,384]{1,0:T(8,128)}) custom-call(s32[1]{0:T(128)} %bitcast.1.me_ref, s32[20]{0:T(128)} %bitcast.77, bf16[2560,256]{1,0:T(8,128)(2,1)} %get-tuple-element.154.q_ref, ...), custom_call_target="tpu_custom_call" | custom-call | flops 1099511627776 | bytes 4294967296 | tf_op jit(solution)/shard_map/pallas_call | solution.py:973
  350.4 7.8 %shard_map.240 = bf16[768,640]{1,0:T(8,128)(2,1)} custom-call(s32[1]{0:T(128)} %bitcast.me_ref, f32[16,384]{1,0:T(8,128)} %get-tuple-element.228.bins_ref, bf16[640,768]{1,0:T(8,128)(2,1)} %get-tuple-element.229.n0, bf16[640,768]{1,0:T(8,128)(2,1)} %get-tuple-element.230.n1, bf16[640,768]{1,0:T(8,128)(2,1)} %get-tuple-element.231.n2, ...), custom_call_target="tpu_custom_call" | custom-call | bytes 1024 | tf_op jit(solution)/shard_map/pallas_call | solution.py:996
  362.9 10.4 %collective-permute-done.28 = bf16[384,640]{1,0:T(8,128)(2,1)S(1)} collective-permute-done((bf16[384,640]{1,0:T(8,128)(2,1)S(1)}, bf16[384,640]{1,0:T(8,128)(2,1)S(1)}, u32[]{:S(2)}, u32[]{:S(2)}) %collective-permute-start.28) | collective-permute-done | bytes 491552 | tf_op jit(solution)/shard_map/ppermute | solution.py:379
  381.4 5.1 %collective-permute-done.32.d3 = bf16[640,640]{1,0:T(8,128)(2,1)} collective-permute-done((bf16[640,640]{1,0:T(8,128)(2,1)}, bf16[640,640]{1,0:T(8,128)(2,1)}, u32[]{:S(2)}, u32[]{:S(2)}) %collective-permute-start.32) | collective-permute-done | bytes 819232 | tf_op jit(solution)/shard_map/ppermute | solution.py:379
  391.3 4.7 %collective-permute-done.33 = bf16[96,640]{1,0:T(8,128)(2,1)S(1)} collective-permute-done((bf16[96,640]{1,0:T(8,128)(2,1)S(1)}, bf16[96,640]{1,0:T(8,128)(2,1)S(1)}, u32[]{:S(2)}, u32[]{:S(2)}) %collective-permute-start.33) | collective-permute-done | bytes 122912 | tf_op jit(solution)/shard_map/ppermute | solution.py:379
  410.0 8.6 %shard_map.242 = bf16[640,768]{1,0:T(8,128)(2,1)} custom-call(s32[1]{0:T(128)} %bitcast.1.me_ref, bf16[640,768]{1,0:T(8,128)(2,1)} %x_ref.3, f32[1,768]{1,0:T(1,128)} %get-tuple-element.273.gain_ref, f32[640,768]{1,0:T(8,128)} %get-tuple-element.274.after_ref, bf16[640,640]{1,0:T(8,128)(2,1)} %get-tuple-element.275.d0, bf16[640,640]{1,0:T(8,128)(2,1)} %copy-done.11, ...), custom_call_target="tpu_custom_call" | custom-call | bytes 1024 | tf_op jit(solution)/shard_map/pallas_call | solution.py:1024
  420.8 7.1 %shard_map.241 = bf16[640,768]{1,0:T(8,128)(2,1)} custom-call(s32[1]{0:T(128)} %bitcast.me_ref, bf16[1920,768]{1,0:T(8,128)(2,1)} %bitcast.27.ret_ref, s32[640,2]{1,0:T(8,128)} %copy-done.3, f32[640,768]{1,0:T(8,128)} %get-tuple-element.212.refs_8_.after_ref), custom_call_target="tpu_custom_call" | custom-call | bytes 1024 | tf_op jit(solution)/shard_map/pallas_call | solution.py:1039
  437.3 8.6 %collective-permute-done.44.refs_5_ = bf16[24,3200]{1,0:T(8,128)(2,1)S(1)} collective-permute-done((bf16[24,3200]{1,0:T(8,128)(2,1)S(1)}, bf16[24,3200]{1,0:T(8,128)(2,1)S(1)}, u32[]{:S(2)}, u32[]{:S(2)}) %collective-permute-start.44) | collective-permute-done | bytes 153632 | tf_op jit(solution)/shard_map/ppermute | solution.py:379
  (256 shorter events, 128.2 us)
Async XLA Ops:
  10.2 36.6 %collective-permute-start.3 = (bf16[640,768]{1,0:T(8,128)(2,1)}, bf16[640,768]{1,0:T(8,128)(2,1)S(1)}, u32[]{:S(2)}, u32[]{:S(2)}) collective-permute-start(bf16[640,768]{1,0:T(8,128)(2,1)} %x_ref.3), channel_id=1, source_target_pairs={{0,1},{1,0},{2,3},{3,2},{4,5},{5,4},{6,7},{7,6},{8,9},{9,8},{10,11... | collective-permute-start | bytes 2949128 | tf_op jit(solution)/shard_map/ppermute | solution.py:379
  35.2 73.4 %all-to-all-start = ((bf16[8,240,768]{2,1,0:T(8,128)(2,1)}), bf16[8,240,768]{2,1,0:T(8,128)(2,1)}, u32[]{:S(2)}, u32[]{:S(2)}) async-start(bf16[8,240,768]{2,1,0:T(8,128)(2,1)} %bitcast.64), calls=%async_computation | async-start | bytes 5898240 | tf_op jit(solution)/shard_map/all_to_all | solution.py:373
  41.2 56.0 %all-gather.7.cloned.1.call-start = ((), (), s32[]{:S(2)}) async-start(), calls=%async_computation.4 | async-start | bytes 1474560 | tf_op jit(solution)/shard_map/all_gather | solution.py:918
  42.0 114.7 %all-gather.9.cloned.1.call-start = ((), (), s32[]{:S(2)}) async-start(), calls=%async_computation.5 | async-start | bytes 5898240 | tf_op jit(solution)/shard_map/all_gather | solution.py:915
  42.6 36.6 %collective-permute-start.6 = (bf16[192,3072]{1,0:T(8,128)(2,1)}, bf16[192,3072]{1,0:T(8,128)(2,1)}, u32[]{:S(2)}, u32[]{:S(2)}) collective-permute-start(bf16[192,3072]{1,0:T(8,128)(2,1)} %bitcast.11.refs_3_.refs_6_), channel_id=1, source_target_pairs={{0,2},{1,3},{2,0},{3,1},{4,6},{5,7},{6,4},{7,5},{8,10},{9,11},{10,... | collective-permute-start | bytes 3538952 | tf_op jit(solution)/shard_map/ppermute | solution.py:379
  44.0 53.2 %collective-permute-start.10 = (bf16[192,3072]{1,0:T(8,128)(2,1)}, bf16[192,3072]{1,0:T(8,128)(2,1)}, u32[]{:S(2)}, u32[]{:S(2)}) collective-permute-start(bf16[192,3072]{1,0:T(8,128)(2,1)} %bitcast.11.refs_3_.refs_6_), channel_id=1, source_target_pairs={{0,1},{1,0},{2,3},{3,2},{4,5},{5,4},{6,7},{7,6},{8,9},{9,8},{10,11... | collective-permute-start | bytes 3538952 | tf_op jit(solution)/shard_map/ppermute | solution.py:379
  116.0 40.7 %all-to-all-start.1 = ((bf16[4,240,768]{2,1,0:T(8,128)(2,1)}), bf16[4,240,768]{2,1,0:T(8,128)(2,1)S(1)}, u32[]{:S(2)}, u32[]{:S(2)}) async-start(bf16[4,240,768]{2,1,0:T(8,128)(2,1)} %bitcast.70), calls=%async_computation.1 | async-start | bytes 2949120 | tf_op jit(solution)/shard_map/all_to_all | solution.py:365
  119.7 137.0 %all-gather.11.cloned.1.call-start = ((), (), s32[]{:S(2)}) async-start(), calls=%async_computation.6 | async-start | bytes 4915200 | tf_op jit(solution)/shard_map/all_gather | solution.py:942
  119.7 82.4 %collective-permute-start.12 = (bf16[240,768]{1,0:T(8,128)(2,1)}, bf16[240,768]{1,0:T(8,128)(2,1)S(1)}, u32[]{:S(2)}, u32[]{:S(2)}) collective-permute-start(bf16[240,768]{1,0:T(8,128)(2,1)} %get-tuple-element.185), channel_id=1, source_target_pairs={{0,8},{4,12},{8,0},{12,4},{16,24},{20,28},{24,16},{28,20},{1,9},{5... | collective-permute-start | bytes 1105928 | tf_op jit(solution)/shard_map/ppermute | solution.py:379
  120.9 81.3 %collective-permute-start.13 = (bf16[240,768]{1,0:T(8,128)(2,1)}, bf16[240,768]{1,0:T(8,128)(2,1)S(1)}, u32[]{:S(2)}, u32[]{:S(2)}) collective-permute-start(bf16[240,768]{1,0:T(8,128)(2,1)} %get-tuple-element.186), channel_id=1, source_target_pairs={{0,12},{4,8},{8,4},{12,0},{16,28},{20,24},{24,20},{28,16},{1,13},{... | collective-permute-start | bytes 1105928 | tf_op jit(solution)/shard_map/ppermute | solution.py:379
  123.1 79.1 %collective-permute-start.14 = (bf16[240,768]{1,0:T(8,128)(2,1)S(1)}, bf16[240,768]{1,0:T(8,128)(2,1)S(1)}, u32[]{:S(2)}, u32[]{:S(2)}) collective-permute-start(bf16[240,768]{1,0:T(8,128)(2,1)S(1)} %copy-done.38), channel_id=1, source_target_pairs={{0,24},{4,28},{8,16},{12,20},{16,8},{20,12},{24,0},{28,4},{1,25},{... | collective-permute-start | bytes 1105928 | tf_op jit(solution)/shard_map/ppermute | solution.py:379
  126.1 76.1 %collective-permute-start.15 = (bf16[240,768]{1,0:T(8,128)(2,1)S(1)}, bf16[240,768]{1,0:T(8,128)(2,1)}, u32[]{:S(2)}, u32[]{:S(2)}) collective-permute-start(bf16[240,768]{1,0:T(8,128)(2,1)S(1)} %copy-done.36), channel_id=1, source_target_pairs={{0,28},{4,24},{8,20},{12,16},{16,12},{20,8},{24,4},{28,0},{1,29},{... | collective-permute-start | bytes 1105928 | tf_op jit(solution)/shard_map/ppermute | solution.py:379
  189.1 67.5 %all-to-all-start.2 = ((bf16[4,240,768]{2,1,0:T(8,128)(2,1)}), bf16[4,240,768]{2,1,0:T(8,128)(2,1)}, u32[]{:S(2)}, u32[]{:S(2)}) async-start(bf16[4,240,768]{2,1,0:T(8,128)(2,1)} %bitcast.69), calls=%async_computation.2 | async-start | bytes 2949120 | tf_op jit(solution)/shard_map/all_to_all | solution.py:365
  234.4 38.3 %collective-permute-start.16 = (bf16[240,768]{1,0:T(8,128)(2,1)}, bf16[240,768]{1,0:T(8,128)(2,1)S(1)}, u32[]{:S(2)}, u32[]{:S(2)}) collective-permute-start(bf16[240,768]{1,0:T(8,128)(2,1)} %get-tuple-element.190), channel_id=1, source_target_pairs={{0,8},{4,12},{8,0},{12,4},{16,24},{20,28},{24,16},{28,20},{1,9},{5... | collective-permute-start | bytes 1105928 | tf_op jit(solution)/shard_map/ppermute | solution.py:379
  234.4 38.2 %collective-permute-start.17 = (bf16[240,768]{1,0:T(8,128)(2,1)}, bf16[240,768]{1,0:T(8,128)(2,1)S(1)}, u32[]{:S(2)}, u32[]{:S(2)}) collective-permute-start(bf16[240,768]{1,0:T(8,128)(2,1)} %get-tuple-element.191), channel_id=1, source_target_pairs={{0,12},{4,8},{8,4},{12,0},{16,28},{20,24},{24,20},{28,16},{1,13},{... | collective-permute-start | bytes 1105928 | tf_op jit(solution)/shard_map/ppermute | solution.py:379
  237.7 35.0 %collective-permute-start.18 = (bf16[240,768]{1,0:T(8,128)(2,1)}, bf16[240,768]{1,0:T(8,128)(2,1)S(1)}, u32[]{:S(2)}, u32[]{:S(2)}) collective-permute-start(bf16[240,768]{1,0:T(8,128)(2,1)} %get-tuple-element.192), channel_id=1, source_target_pairs={{0,24},{4,28},{8,16},{12,20},{16,8},{20,12},{24,0},{28,4},{1,25},{... | collective-permute-start | bytes 1105928 | tf_op jit(solution)/shard_map/ppermute | solution.py:379
  239.6 33.1 %collective-permute-start.19 = (bf16[240,768]{1,0:T(8,128)(2,1)}, bf16[240,768]{1,0:T(8,128)(2,1)S(1)}, u32[]{:S(2)}, u32[]{:S(2)}) collective-permute-start(bf16[240,768]{1,0:T(8,128)(2,1)} %get-tuple-element.193), channel_id=1, source_target_pairs={{0,28},{4,24},{8,20},{12,16},{16,12},{20,8},{24,4},{28,0},{1,29},{... | collective-permute-start | bytes 1105928 | tf_op jit(solution)/shard_map/ppermute | solution.py:379
  290.1 130.7 %all-to-all-start.3 = ((bf16[8,240,768]{2,1,0:T(8,128)(2,1)}), bf16[8,240,768]{2,1,0:T(8,128)(2,1)}, u32[]{:S(2)}, u32[]{:S(2)}) async-start(bf16[8,240,768]{2,1,0:T(8,128)(2,1)} %bitcast.26), calls=%async_computation.3 | async-start | bytes 5898240 | tf_op jit(solution)/shard_map/all_to_all | solution.py:373
  312.1 36.4 %collective-permute-start.26 = (bf16[768,768]{1,0:T(8,128)(2,1)}, bf16[768,768]{1,0:T(8,128)(2,1)}, u32[]{:S(2)}, u32[]{:S(2)}) collective-permute-start(bf16[768,768]{1,0:T(8,128)(2,1)} %add_convert_fusion.1), channel_id=1, source_target_pairs={{0,2},{1,3},{2,0},{3,1},{4,6},{5,7},{6,4},{7,5},{8,10},{9,11},{10,... | collective-permute-start | bytes 3538952 | tf_op jit(solution)/shard_map/ppermute | solution.py:379
  313.6 34.9 %collective-permute-start.27 = (bf16[192,896]{1,0:T(8,128)(2,1)}, bf16[192,896]{1,0:T(8,128)(2,1)}, u32[]{:S(2)}, u32[]{:S(2)}) collective-permute-start(bf16[192,896]{1,0:T(8,128)(2,1)} %add_convert_fusion.4), channel_id=1, source_target_pairs={{0,2},{1,3},{2,0},{3,1},{4,6},{5,7},{6,4},{7,5},{8,10},{9,11},{10,... | collective-permute-start | bytes 1032200 | tf_op jit(solution)/shard_map/ppermute | solution.py:379
  348.5 32.9 %collective-permute-start.30 = (bf16[640,640]{1,0:T(8,128)(2,1)}, bf16[640,640]{1,0:T(8,128)(2,1)S(1)}, u32[]{:S(2)}, u32[]{:S(2)}) collective-permute-start(bf16[640,640]{1,0:T(8,128)(2,1)} %get-tuple-element.244.d1), channel_id=1, source_target_pairs={{0,1},{1,0},{2,3},{3,2},{4,5},{5,4},{6,7},{7,6},{8,9},{9,8},{10,11... | collective-permute-start | bytes 2457608 | tf_op jit(solution)/shard_map/ppermute | solution.py:379
  348.6 32.8 %collective-permute-start.31 = (bf16[640,640]{1,0:T(8,128)(2,1)}, bf16[640,640]{1,0:T(8,128)(2,1)S(1)}, u32[]{:S(2)}, u32[]{:S(2)}) collective-permute-start(bf16[640,640]{1,0:T(8,128)(2,1)} %get-tuple-element.245.d2), channel_id=1, source_target_pairs={{0,2},{1,3},{2,0},{3,1},{4,6},{5,7},{6,4},{7,5},{8,10},{9,11},{10,... | collective-permute-start | bytes 2457608 | tf_op jit(solution)/shard_map/ppermute | solution.py:379
  350.2 36.3 %collective-permute-start.32 = (bf16[640,640]{1,0:T(8,128)(2,1)}, bf16[640,640]{1,0:T(8,128)(2,1)}, u32[]{:S(2)}, u32[]{:S(2)}) collective-permute-start(bf16[640,640]{1,0:T(8,128)(2,1)} %get-tuple-element.246.d3), channel_id=1, source_target_pairs={{0,3},{1,2},{2,1},{3,0},{4,7},{5,6},{6,5},{7,4},{8,11},{9,10},{10,... | collective-permute-start | bytes 2457608 | tf_op jit(solution)/shard_map/ppermute | solution.py:379
  401.1 32.2 %collective-permute-start.47 = (bf16[192,3072]{1,0:T(8,128)(2,1)S(1)}, bf16[192,3072]{1,0:T(8,128)(2,1)}, u32[]{:S(2)}, u32[]{:S(2)}) collective-permute-start(bf16[192,3072]{1,0:T(8,128)(2,1)S(1)} %copy-done.9), channel_id=1, source_target_pairs={{0,2},{1,3},{2,0},{3,1},{4,6},{5,7},{6,4},{7,5},{8,10},{9,11},{10,... | collective-permute-start | bytes 3538952 | tf_op jit(solution)/shard_map/ppermute | solution.py:379
  (78 other events, 868.4 us)
Sparse Core Ops, SparseCore 0:
  43.6 25.2 all-gather.6
  97.3 39.3 all-gather.8
  189.2 31.5 all-gather.10
